TPU v7x, 32 devices: a whole 2x2x4 slice. The times are simulated.
32 devices in a mesh: groups: 2 (over x), modes: 16 (over z, y, core).
Axes of the slice: x: 2, y: 2, z: 4, core: 2. Of those that a mesh axis runs over, the one named last changes fastest.
Arguments:
- mode_fields: bfloat16 [256, 256, 2048], P(('groups', 'modes')), parts along dimension 0, may hold values from -0.59765625 to 0.59765625
- coeff: float32 [256], P('groups'), parts along dimension 0, may hold values from -6 to 6
- eigen: float32 [256], P('groups'), parts along dimension 0, may hold values from 0.1 to 100
- map_friction: float32 [512, 2048], P(('groups', 'modes')), parts along dimension 0, may hold values from 1 to 2.5
- bed: float32 [512, 2048], P(('groups', 'modes')), parts along dimension 0, may hold values from -5 to 5
- smb: float32 [512, 2048], P(('groups', 'modes')), parts along dimension 0, may hold values from -0.6 to 0.4
- thickness: float32 [512, 2048], P(('groups', 'modes')), parts along dimension 0, may hold values from 1.9 to 2.6
Outputs:
- log_friction: float32 [512, 2048], P(('groups', 'modes')), parts along dimension 0
- final_thickness: float32 [512, 2048], P(('groups', 'modes')), parts along dimension 0
There are 2 independent parts, one for each index of `groups`. A program takes and returns all parts, laid end to end along the dimension named above; each array names one. Nothing has to cross between parts.
All inputs are finite; a program needn't handle non-finite values.
Results may differ from a plain program's by a relative error of at most 0.0014.
Values may be sent and summed in bfloat16 or wider, within the bound.
No kernel may reach another device: no remote copies, remote signals or barrier semaphores. Data moves between devices by JAX's collectives and lax.ppermute only.
A program may use at most 64 MiB of HBM per device.

v0:
```python
import jax
import jax.numpy as jnp
from jax import lax
from jax.sharding import PartitionSpec as P

STEPS = 8


flow_rate = 0.02
slide_rate = 0.1
diff_cap = 0.5
time_step = 0.4


def padded(value, sides, width):
    for axis, dim in sides:
        peers, length = (lax.axis_size(axis), value.shape[dim])
        up = [(i, (i + 1) % peers) for i in range(peers - 1)]
        down = [(j, i) for i, j in up]
        last = lax.slice_in_dim(value, length - width, length, axis=dim)
        leading = lax.slice_in_dim(value, 0, width, axis=dim)
        before = lax.ppermute(last, axis, up)
        after = lax.ppermute(leading, axis, down)
        value = jnp.concatenate([before, value, after], axis=dim)
    return value


def advance(height, base, friction, balance):
    hpad = jnp.pad(height, ((0, 0), (2, 2)))
    bpad = jnp.pad(base, ((0, 0), (2, 2)))
    fpad = jnp.pad(friction, ((0, 0), (2, 2)))
    surface = bpad + hpad
    grad_x = (surface[2:, 1:-1] - surface[:-2, 1:-1]) * 0.5
    grad_y = (surface[1:-1, 2:] - surface[1:-1, :-2]) * 0.5
    center = hpad[1:-1, 1:-1]
    fcent = fpad[1:-1, 1:-1]
    squared = center * center
    diff = flow_rate * squared * squared * center * (grad_x * grad_x + grad_y * grad_y)
    diff = jnp.minimum(diff + slide_rate * squared * jnp.exp(-fcent), diff_cap)
    scent = surface[1:-1, 1:-1]
    mid_d = diff[1:-1, 1:-1]
    mid_s = scent[1:-1, 1:-1]
    up_x = 0.5 * (diff[2:, 1:-1] + mid_d) * (scent[2:, 1:-1] - mid_s)
    down_x = 0.5 * (mid_d + diff[:-2, 1:-1]) * (mid_s - scent[:-2, 1:-1])
    up_y = 0.5 * (diff[1:-1, 2:] + mid_d) * (scent[1:-1, 2:] - mid_s)
    down_y = 0.5 * (mid_d + diff[1:-1, :-2]) * (mid_s - scent[1:-1, :-2])
    total = up_x - down_x + up_y - down_y
    return jnp.maximum(height[2:-2] + time_step * (total + balance[2:-2]), 0.0)


def march(extended, count, wide, reach, first, total_rows):
    for inner_step in range(count):
        begin = reach - 2 * count + 2 * inner_step
        length = extended.shape[0]
        statics = wide[:, begin : begin + length]
        extended = advance(extended, statics[0], statics[1], statics[2])
        remain = 2 * count - 2 * inner_step - 2
        if remain > 0:
            global_row = first - remain + jnp.arange(extended.shape[0], dtype=jnp.int32)
            inside = (global_row >= 0) & (global_row < total_rows)
            extended = jnp.where(inside[:, None], extended, 0.0)
    return extended


def per_device(mode_fields, coeff, eigen, map_friction, bed, smb, thickness):
    weights = (coeff / jnp.sqrt(1.0 + eigen)).astype(jnp.bfloat16)
    rows_dev = map_friction.shape[0]
    mode_dev = mode_fields.shape[0]
    local_w = lax.dynamic_slice_in_dim(weights, lax.axis_index("modes") * mode_dev, mode_dev, 0)
    perturb = lax.psum_scatter(
        jnp.einsum("k,kxy->xy", local_w, mode_fields, preferred_element_type=jnp.float32),
        "modes",
        scatter_dimension=0,
        tiled=True,
    )
    log_friction = map_friction + perturb
    per_round = min(STEPS, rows_dev // 2)
    reach = 2 * per_round
    statics = jnp.stack([bed, log_friction, smb])
    wide = padded(statics, (("modes", 1),), reach)
    first = lax.axis_index("modes") * rows_dev
    total_rows = rows_dev * lax.axis_size("modes")
    height = thickness
    extended = padded(height, (("modes", 0),), 2 * per_round)
    height = march(extended, per_round, wide, reach, first, total_rows)
    return (log_friction, height)


def solution(mesh):
    return jax.shard_map(
        per_device,
        mesh=mesh,
        in_specs=(
            P(("groups", "modes"), None, None),
            P("groups"),
            P("groups"),
            P(("groups", "modes"), None),
            P(("groups", "modes"), None),
            P(("groups", "modes"), None),
            P(("groups", "modes"), None),
        ),
        out_specs=(P(("groups", "modes"), None), P(("groups", "modes"), None)),
        check_vma=False,
    )
```

profile of v0, /device:TPU:1, one launch (start us, length us, event | category | flops | bytes accessed | tf_op | source)
XLA Modules:
  0.0 116.6 jit_solution(11758352358127257634)
XLA Ops:
  7.2 0.0 reduce-scatter.2.cloned.1.call-start
  7.2 0.7 multiply_convert_fusion
  7.9 9.4 %fusion = f32[1,256,2048]{2,0,1:T(1,128)S(1)} fusion(bf16[8,256,2048]{2,1,0:T(8,128)(2,1)} %param.7, bf16[128]{0:T(256)(128)(2,1)S(1)} %multiply_convert_fusion, s32[]{:T(128)S(6)} %select_n.31), kind=kOutput, calls=%fused_computation | convolution fusion | flops 8388608 | bytes 10486020 | tf_op jit(solution)/shard_map/k,kxy->xy/dot_general | solution.py:71
  17.3 2.2 %copy.14 = f32[1,256,2048]{2,1,0:T(8,128)} copy(f32[1,256,2048]{2,0,1:T(1,128)S(1)} %fusion) | data formatting | bytes 4194304 | tf_op jit(solution)/shard_map/k,kxy->xy/dot_general | solution.py:71
  19.5 0.0 copy-start.4
  19.5 0.0 copy-start.3
  19.5 0.0 copy-start.1
  19.5 0.0 copy-start.2
  19.5 0.0 reduce-scatter.2.cloned.1.call-update
  19.5 0.9 copy-done.4
  20.4 4.5 %collective-permute-start = (f32[16,2048]{1,0:T(8,128)S(1)}, f32[16,2048]{1,0:T(8,128)S(1)}, u32[]{:S(2)}, u32[]{:S(2)}) collective-permute-start(f32[16,2048]{1,0:T(8,128)S(1)} %copy-done.4), channel_id=1, source_target_pairs={{0,1},{1,2},{2,3},{3,4},{4,5},{5,6},{6,7},{7,8},{8,9},{9,10},{10,1... | collective-permute-start | bytes 393224 | tf_op jit(solution)/shard_map/ppermute | solution.py:22
  24.9 1.9 %collective-permute-start.1 = (f32[16,2048]{1,0:T(8,128)S(1)}, f32[16,2048]{1,0:T(8,128)S(1)}, u32[]{:S(2)}, u32[]{:S(2)}) collective-permute-start(f32[16,2048]{1,0:T(8,128)S(1)} %copy-done.4), channel_id=1, source_target_pairs={{1,0},{2,1},{3,2},{4,3},{5,4},{6,5},{7,6},{8,7},{9,8},{10,9},{11,1... | collective-permute-start | bytes 393224 | tf_op jit(solution)/shard_map/ppermute | solution.py:23
  27.0 0.0 collective-permute-done
  27.0 54.8 %reduce-scatter.2.cloned.1.call-done = f32[16,2048]{1,0:T(8,128)} async-done(((f32[256,2048]{1,0:T(8,128)}), f32[16,2048]{1,0:T(8,128)}) %reduce-scatter.2.cloned.1.call-update) | async-done | bytes 131088 | tf_op jit(solution)/shard_map/reduce_scatter | solution.py:70
  81.8 0.0 copy-done.3
  81.8 0.9 add.382
  82.7 0.0 copy-start
  82.7 0.0 copy-done.1
  82.7 0.0 copy-done.2
  82.8 4.9 %collective-permute-start.2 = (f32[3,16,2048]{2,1,0:T(8,128)S(1)}, f32[3,16,2048]{2,1,0:T(8,128)S(1)}, u32[]{:S(2)}, u32[]{:S(2)}) collective-permute-start(f32[3,16,2048]{2,1,0:T(8,128)S(1)} %pad_maximum_fusion.1), channel_id=1, source_target_pairs={{0,1},{1,2},{2,3},{3,4},{4,5},{5,6},{6,7},{7,8},{8,9},{9,10},{10,1... | collective-permute-start | bytes 1179656 | tf_op jit(solution)/shard_map/ppermute | solution.py:22
  87.7 2.1 %collective-permute-start.3 = (f32[3,16,2048]{2,1,0:T(8,128)S(1)}, f32[3,16,2048]{2,1,0:T(8,128)S(1)}, u32[]{:S(2)}, u32[]{:S(2)}) collective-permute-start(f32[3,16,2048]{2,1,0:T(8,128)S(1)} %pad_maximum_fusion.1), channel_id=1, source_target_pairs={{1,0},{2,1},{3,2},{4,3},{5,4},{6,5},{7,6},{8,7},{9,8},{10,9},{11,1... | collective-permute-start | bytes 1179656 | tf_op jit(solution)/shard_map/ppermute | solution.py:23
  89.8 0.0 collective-permute-done.1
  89.8 2.5 %collective-permute-done.2 = f32[3,16,2048]{2,1,0:T(8,128)S(1)} collective-permute-done((f32[3,16,2048]{2,1,0:T(8,128)S(1)}, f32[3,16,2048]{2,1,0:T(8,128)S(1)}, u32[]{:S(2)}, u32[]{:S(2)}) %collective-permute-start.2) | collective-permute-done | bytes 393248 | tf_op jit(solution)/shard_map/ppermute | solution.py:22
  92.4 4.4 %collective-permute-done.3 = f32[3,16,2048]{2,1,0:T(8,128)S(1)} collective-permute-done((f32[3,16,2048]{2,1,0:T(8,128)S(1)}, f32[3,16,2048]{2,1,0:T(8,128)S(1)}, u32[]{:S(2)}, u32[]{:S(2)}) %collective-permute-start.3) | collective-permute-done | bytes 393248 | tf_op jit(solution)/shard_map/ppermute | solution.py:23
  96.7 0.1 pad_maximum_fusion
  96.8 0.0 copy-done
  96.9 0.1 slice_bitcast_fusion.3
  96.9 0.1 slice_bitcast_fusion
  97.0 0.1 slice_bitcast_fusion.8
  97.1 0.1 slice_bitcast_fusion.5
  97.3 0.9 fusion.5
  98.2 1.2 %fusion.24 = f32[44,2048]{1,0:T(8,128)S(1)} fusion(f32[3,48,2048]{2,1,0:T(8,128)S(1)} %pad_maximum_fusion, f32[48,2048]{1,0:T(8,128)S(1)} %constant_dynamic-update-slice_fusion, f32[48,2048]{1,0:T(8,128)S(1)} %get-tuple-element.17, f32[46,2050]{1,0:T(8,128)S(1)} %fusion.5, pred[44]{0:T(512)(128)(4,1)S(1)} %compare_and_fusion), kind=kLoop, calls=%fused_computation.39 | loop fusion | flops 2613248 | bytes 3899904 | tf_op jit(solution)/shard_map/jit(_where)/select_n | solution.py:61
  99.4 0.9 fusion.9
  100.4 1.0 fusion.67
  101.4 0.8 fusion.43
  102.2 0.9 fusion.80
  103.1 0.8 fusion.47
  103.9 0.7 fusion.129
  104.6 0.7 fusion.105
  105.3 0.7 fusion.142
  106.0 0.6 fusion.109
  106.7 0.5 fusion.191
  107.2 0.5 fusion.167
  107.7 0.5 fusion.204
  108.2 0.5 fusion.171
  108.7 1.0 fusion.234
  (15 shorter events, 0.3 us)
Async XLA Ops:
  7.2 74.6 %reduce-scatter.2.cloned.1.call-start = ((), (), s32[]{:S(2)}) async-start(), calls=%async_computation.1 | async-start | bytes 2228224 | tf_op jit(solution)/shard_map/reduce_scatter | solution.py:70
  19.5 0.9 copy-start.4
  19.5 62.3 %copy-start.3 = (f32[16,2048]{1,0:T(8,128)S(1)}, f32[16,2048]{1,0:T(8,128)}, u32[]{:S(2)}) copy-start(f32[16,2048]{1,0:T(8,128)} %param.10) | copy-start | bytes 393220
  19.5 63.2 %copy-start.1 = (f32[16,2048]{1,0:T(8,128)S(1)}, f32[16,2048]{1,0:T(8,128)}, u32[]{:S(2)}) copy-start(f32[16,2048]{1,0:T(8,128)} %param.12) | copy-start | bytes 393220
  19.5 63.2 %copy-start.2 = (f32[16,2048]{1,0:T(8,128)S(1)}, f32[16,2048]{1,0:T(8,128)}, u32[]{:S(2)}) copy-start(f32[16,2048]{1,0:T(8,128)} %param.11) | copy-start | bytes 393220
  20.4 6.6 %collective-permute-start = (f32[16,2048]{1,0:T(8,128)S(1)}, f32[16,2048]{1,0:T(8,128)S(1)}, u32[]{:S(2)}, u32[]{:S(2)}) collective-permute-start(f32[16,2048]{1,0:T(8,128)S(1)} %copy-done.4), channel_id=1, source_target_pairs={{0,1},{1,2},{2,3},{3,4},{4,5},{5,6},{6,7},{7,8},{8,9},{9,10},{10,1... | collective-permute-start | bytes 393224 | tf_op jit(solution)/shard_map/ppermute | solution.py:22
  24.9 64.9 %collective-permute-start.1 = (f32[16,2048]{1,0:T(8,128)S(1)}, f32[16,2048]{1,0:T(8,128)S(1)}, u32[]{:S(2)}, u32[]{:S(2)}) collective-permute-start(f32[16,2048]{1,0:T(8,128)S(1)} %copy-done.4), channel_id=1, source_target_pairs={{1,0},{2,1},{3,2},{4,3},{5,4},{6,5},{7,6},{8,7},{9,8},{10,9},{11,1... | collective-permute-start | bytes 393224 | tf_op jit(solution)/shard_map/ppermute | solution.py:23
  82.7 14.1 %copy-start = (f32[16,2048]{1,0:T(8,128)}, f32[16,2048]{1,0:T(8,128)S(1)}, u32[]{:S(2)}) copy-start(f32[16,2048]{1,0:T(8,128)S(1)} %add.382) | copy-start | bytes 393220
  82.8 9.6 %collective-permute-start.2 = (f32[3,16,2048]{2,1,0:T(8,128)S(1)}, f32[3,16,2048]{2,1,0:T(8,128)S(1)}, u32[]{:S(2)}, u32[]{:S(2)}) collective-permute-start(f32[3,16,2048]{2,1,0:T(8,128)S(1)} %pad_maximum_fusion.1), channel_id=1, source_target_pairs={{0,1},{1,2},{2,3},{3,4},{4,5},{5,6},{6,7},{7,8},{8,9},{9,10},{10,1... | collective-permute-start | bytes 1179656 | tf_op jit(solution)/shard_map/ppermute | solution.py:22
  87.7 9.1 %collective-permute-start.3 = (f32[3,16,2048]{2,1,0:T(8,128)S(1)}, f32[3,16,2048]{2,1,0:T(8,128)S(1)}, u32[]{:S(2)}, u32[]{:S(2)}) collective-permute-start(f32[3,16,2048]{2,1,0:T(8,128)S(1)} %pad_maximum_fusion.1), channel_id=1, source_target_pairs={{1,0},{2,1},{3,2},{4,3},{5,4},{6,5},{7,6},{8,7},{9,8},{10,9},{11,1... | collective-permute-start | bytes 1179656 | tf_op jit(solution)/shard_map/ppermute | solution.py:23
Sparse Core Ops, SparseCore 0:
  19.6 62.0 reduce-scatter.1
where the time goes:
time: 118 us; the launch traced here: 117 us
  waiting for transfers between devices  61.7 us (52%)
  between operations  14.4 us (12%)
  other arithmetic  14.1 us (12%)
  starting transfers between devices  13.5 us (11%)
  matrix products  9.37 us (8%)
  local copies, waits for them, and re-layouts  3.52 us (3%)
    reduce_scatter x1, waiting for transfers between devices, per_device(): lax.psum_scatter(jnp.einsum('k,kxy->xy', local_w, mode_fields, preferred_...  54.8 us
    ppermute x2, starting transfers between devices, padded(): before = lax.ppermute(last, axis, up)  9.41 us
    dot_general x1, matrix products, per_device(): jnp.einsum('k,kxy->xy', local_w, mode_fields, preferred_element_type=jnp....  9.37 us
    min x8, other arithmetic, advance(): diff = jnp.minimum(diff + slide_rate * squared * jnp.exp(-fcent), diff_cap)  5.76 us
    select_n x7, other arithmetic, march(): extended = jnp.where(inside[:, None], extended, 0.0)  5.59 us
    ppermute x2, waiting for transfers between devices, padded(): after = lax.ppermute(leading, axis, down)  4.4 us
    ppermute x2, starting transfers between devices, padded(): after = lax.ppermute(leading, axis, down)  4.02 us
    ppermute x2, waiting for transfers between devices, padded(): before = lax.ppermute(last, axis, up)  2.54 us
  transfers between devices with their start and end apart: 5, of which 3 were waited for; matrix products, arithmetic and copies ran while one was open for 1% of the time, Pallas kernels for 0%

commit v1 on v0

v1 whole, which is shorter than its diff:
```python
import jax
import jax.numpy as jnp
from jax import lax
from jax.experimental import pallas as pl
from jax.experimental.pallas import tpu as pltpu
from jax.sharding import PartitionSpec as P

STEPS = 8
LANES = 128
GROUP = 8
LIMIT = 48

flow_rate = 0.02
slide_rate = 0.1
diff_cap = 0.5
time_step = 0.4


def lanes():
    return lax.broadcasted_iota(jnp.int32, (1, LANES), 1)


def fold(parts):
    parts, bit, lane = list(parts), 1, lanes()
    while bit < len(parts):
        high = (lane & bit) != 0
        for k in range(len(parts)):
            if k & bit == 0:
                x, y = parts[k], parts[k + bit]
                parts[k] = jnp.where(high, pltpu.roll(y, bit, 1), x)
                parts[k + bit] = jnp.where(high, y, pltpu.roll(x, LANES - bit, 1))
        bit *= 2
    return parts


def cut(ref, rows, blocks):
    return [ref[rows, k * LANES : (k + 1) * LANES] for k in range(blocks)]


def fold_all(*refs):
    out = refs[-1]
    blocks, rows = out.shape[1], out.shape[2]

    def tile(r, carry):
        at = pl.ds(pl.multiple_of(r * 8, 8), 8)
        for a, ref in enumerate(refs[:-1]):
            for p, part in enumerate(fold(cut(ref, at, blocks))):
                out[a, p, at, :] = part
        return carry

    lax.fori_loop(0, rows // 8, tile, 0)


def folded(*arrays):
    rows, columns = arrays[0].shape
    shape = (len(arrays), columns // LANES, rows, LANES)
    return pl.pallas_call(
        fold_all,
        out_shape=jax.ShapeDtypeStruct(shape, jnp.float32),
        compiler_params=pltpu.CompilerParams(vmem_limit_bytes=8 << 20),
        cost_estimate=pl.CostEstimate(flops=4 << 20, bytes_accessed=4 << 20, transcendentals=0),
    )(*arrays)


def slide_fold(friction, wide, narrow):
    blocks, rows = wide.shape[0], wide.shape[1]
    parts = fold([slide_rate * jnp.exp(-part) for part in cut(friction, slice(0, rows), blocks)])
    for p, part in enumerate(parts):
        wide[p] = part
        narrow[p] = part.astype(narrow.dtype)


def slides(friction):
    rows, columns = friction.shape
    shape = (columns // LANES, rows, LANES)
    return pl.pallas_call(
        slide_fold,
        out_shape=(jax.ShapeDtypeStruct(shape, jnp.float32), jax.ShapeDtypeStruct(shape, jnp.bfloat16)),
        compiler_params=pltpu.CompilerParams(vmem_limit_bytes=8 << 20),
    )(friction)


def weigh(own, coeff_ref, eigen_ref, fields, out, held, given, sems):
    strips, modes, rows, columns = held.shape
    me = lax.axis_index("modes")
    parity = me % 2 if own else 1 - me % 2

    def copy(p):
        row = (((me // 2) ^ p) * 2 + parity) * rows
        return pltpu.make_async_copy(
            fields.at[:, pl.ds(pl.multiple_of(row, rows), rows), :], held.at[p], sems.at[p]
        )

    small = [
        pltpu.make_async_copy(ref, given.at[i], sems.at[strips + i])
        for i, ref in enumerate((coeff_ref, eigen_ref))
    ]
    for one in small:
        one.start()

    def begin(p, carry):
        copy(p).start()
        return carry

    lax.fori_loop(0, strips, begin, 0)
    for one in small:
        one.wait()
    weights = given[0] / jnp.sqrt(1.0 + given[1])
    weights = weights.astype(jnp.bfloat16).astype(jnp.float32)
    at = lax.broadcasted_iota(jnp.int32, weights.shape, 1)
    scale = [
        jnp.sum(jnp.where(at == me * modes + k, weights, 0.0), axis=1, keepdims=True)
        for k in range(modes)
    ]

    def strip(p, carry):
        copy(p).wait()
        for b in range(columns // LANES):
            span = slice(b * LANES, (b + 1) * LANES)
            total = scale[0] * held[p, 0, :, span].astype(jnp.float32)
            for k in range(1, modes):
                total = total + scale[k] * held[p, k, :, span].astype(jnp.float32)
            out[p, :, span] = total.astype(out.dtype)
        return carry

    lax.fori_loop(0, strips, strip, 0)


def shares(coeff, eigen, mode_fields, rows, own, dtype):
    modes, total_rows, columns = mode_fields.shape
    strips = total_rows // rows // 2

    def kernel(*refs):
        weigh(own, *refs)

    return pl.pallas_call(
        kernel,
        in_specs=[pl.BlockSpec(memory_space=pl.ANY)] * 3,
        out_specs=pl.BlockSpec(memory_space=pltpu.VMEM),
        out_shape=jax.ShapeDtypeStruct((strips, rows, columns), dtype),
        scratch_shapes=[
            pltpu.VMEM((strips, modes, rows, columns), jnp.bfloat16),
            pltpu.VMEM((2,) + coeff.shape, jnp.float32),
            pltpu.SemaphoreType.DMA((strips + 2,)),
        ],
        compiler_params=pltpu.CompilerParams(vmem_limit_bytes=LIMIT << 20),
        cost_estimate=pl.CostEstimate(
            flops=modes * total_rows * columns,
            bytes_accessed=modes * total_rows * columns,
            transcendentals=0,
        ),
    )(coeff, eigen, mode_fields)


PAD = 8
NEVER = -1e30


def ice(peers, own_s, near_s, far_s, own_f, near_f, far_f, out, h0, s0, h1, s1, bed, bal, slide, diff):
    blocks, rows, _ = own_f.shape
    reach = 2 * STEPS
    extent = rows + 2 * reach
    me = lax.axis_index("modes")
    zero = jnp.minimum(me, 0)
    odd = me % 2 == 1
    above, below = me > 0, me < peers - 1
    mid_at = pl.ds(PAD + reach, rows)
    near_at = pl.ds(pl.multiple_of(PAD + jnp.where(odd, 0, rows + reach), 8), reach)
    far_at = pl.ds(pl.multiple_of(PAD + jnp.where(odd, rows + reach, 0), 8), reach)
    near_in = jnp.where(odd, above, below)
    far_in = jnp.where(odd, below, above)
    lane = lanes()

    def place_in(p, carry):
        slot = p + 2
        for src, at, inside in ((own_s, mid_at, True), (near_s, near_at, near_in), (far_s, far_at, far_in)):
            h, b, m = (src[a, p].astype(jnp.float32) for a in range(3))
            h0[slot, at, :] = h
            s0[slot, at, :] = h + b
            bed[slot, at, :] = b
            m = time_step * m
            bal[slot, at, :] = m if inside is True else jnp.where(inside, m, NEVER)
        for src, at in ((own_f, mid_at), (near_f, near_at), (far_f, far_at)):
            slide[slot, at, :] = src[p].astype(jnp.float32)
        return carry

    lax.fori_loop(0, blocks, place_in, 0, unroll=4)

    def wrap(ref, at, count):
        for q in range(count):
            x = ref[q + 2, at, :]
            x = jnp.where(
                lane >= LANES - blocks,
                jnp.where(lane == LANES - 1, 0.0, pltpu.roll(x, LANES - blocks - 1, 1)),
                pltpu.roll(x, LANES - blocks, 1),
            )
            ref[blocks + 2 + q, at, :] = x
            x = ref[blocks + 1 - q, at, :]
            x = jnp.where(
                lane < blocks,
                jnp.where(lane == 0, 0.0, pltpu.roll(x, blocks + 1, 1)),
                pltpu.roll(x, blocks, 1),
            )
            ref[1 - q, at, :] = x

    whole = pl.ds(PAD, extent)
    wrap(s0, whole, 2)
    wrap(h0, whole, 1)
    wrap(slide, whole, 1)

    for step in range(STEPS):
        h, s, hn, sn = (h0, s0, h1, s1) if step % 2 == 0 else (h1, s1, h0, s0)
        final = step == STEPS - 1
        edge = 2 * step + 2

        def window(first):
            low = first // 8 * 8
            at = pl.ds(PAD + low, extent - 2 * low)
            up = pl.ds(PAD + low - 1 + zero, extent - 2 * low)
            down = pl.ds(PAD + low + 1 + zero, extent - 2 * low)
            return at, up, down

        at, up, down = window(edge - 1)

        def diffuse(i, carry, h=h, s=s, at=at, up=up, down=down):
            for q in range(span):
                j = 1 + i * span + q
                gx = s[j, down, :] - s[j, up, :]
                gy = s[j + 1, at, :] - s[j - 1, at, :]
                thick = h[j, at, :]
                squared = thick * thick
                grad = (gx * gx + gy * gy) * (0.25 * flow_rate)
                diff[j, at, :] = jnp.minimum(squared * (squared * thick * grad + slide[j, at, :]), diff_cap)
            return carry

        span = (blocks + 2) // 2
        lax.fori_loop(0, 2, diffuse, 0)
        at, up, down = window(edge)

        def flow(i, carry, h=h, s=s, hn=hn, sn=sn, at=at, up=up, down=down, final=final):
            first = 2 + i * count
            s_mid, d_mid = s[first, at, :], diff[first, at, :]
            left = (diff[first - 1, at, :] + d_mid) * (s_mid - s[first - 1, at, :])
            for q in range(count):
                j = first + q
                s_next, d_next = s[j + 1, at, :], diff[j + 1, at, :]
                right = (d_mid + d_next) * (s_next - s_mid)
                total = right - left
                total += (diff[j, down, :] + d_mid) * (s[j, down, :] - s_mid)
                total -= (diff[j, up, :] + d_mid) * (s_mid - s[j, up, :])
                value = jnp.maximum(h[j, at, :] + (0.5 * time_step) * total + bal[j, at, :], 0.0)
                hn[j, at, :] = value
                if not final:
                    sn[j, at, :] = value + bed[j, at, :]
                left, s_mid, d_mid = right, s_next, d_next
            return carry

        count = min(GROUP, blocks)
        lax.fori_loop(0, blocks // count, flow, 0)
        if not final:
            wrap(sn, at, 2)
            wrap(hn, at, 1)

    h = h1 if STEPS % 2 else h0

    def tile(r, carry):
        at = pl.ds(pl.multiple_of(r * 8, 8), 8)
        from_at = pl.ds(pl.multiple_of(PAD + reach + r * 8, 8), 8)
        for k, part in enumerate(fold([h[p + 2, from_at, :] for p in range(blocks)])):
            out[at, k * LANES : (k + 1) * LANES] = part
        return carry

    lax.fori_loop(0, rows // 8, tile, 0)


def march(peers, own_s, near_s, far_s, own_f, near_f, far_f):
    blocks, rows, _ = own_f.shape
    vmem = pl.BlockSpec(memory_space=pltpu.VMEM)
    scratch = pltpu.VMEM((blocks + 4, rows + 4 * STEPS + 2 * PAD, LANES), jnp.float32)

    def kernel(*refs):
        ice(peers, *refs)

    return pl.pallas_call(
        kernel,
        in_specs=[vmem] * 6,
        out_specs=vmem,
        out_shape=jax.ShapeDtypeStruct((rows, blocks * LANES), jnp.float32),
        scratch_shapes=[scratch] * 8,
        compiler_params=pltpu.CompilerParams(vmem_limit_bytes=32 << 20),
    )(own_s, near_s, far_s, own_f, near_f, far_f)


def per_device(mode_fields, coeff, eigen, map_friction, bed, smb, thickness):
    peers = lax.axis_size("modes")
    rows, columns = map_friction.shape
    blocks = columns // LANES
    assert rows == 2 * STEPS and peers >= 2 and peers & (peers - 1) == 0
    assert peers >= 4 and columns % LANES == 0 and blocks & (blocks - 1) == 0 and 2 <= blocks <= LANES

    def swap(value, mask):
        return lax.ppermute(value, "modes", [(i, i ^ mask) for i in range(peers)])

    def across(value):
        pairs = [(i, i + 1) for i in range(1, peers - 1, 2)]
        return lax.ppermute(value, "modes", pairs + [(j, i) for i, j in pairs])

    given = shares(coeff[None], eigen[None], mode_fields, rows, False, jnp.bfloat16)
    kept = shares(coeff[None], eigen[None], mode_fields, rows, True, jnp.float32)
    total = kept + swap(given, 1).astype(jnp.float32)
    strips = total.shape[0]
    inner = min(strips, 4)
    taken = total[::inner]
    for part in [swap(total[k::inner].astype(jnp.float16), 2 * k) for k in reversed(range(1, inner))]:
        taken = taken + part.astype(jnp.float32)

    thickness, total = lax.optimization_barrier((thickness, total))
    statics = folded(thickness, bed, smb)
    sent = statics.astype(jnp.float16)
    near_s, far_s = swap(sent, 1).astype(jnp.float32), across(sent).astype(jnp.float32)

    while taken.shape[0] > 1:
        half = taken.shape[0] // 2
        taken = taken[:half] + swap(taken[half:].astype(jnp.float16), 2 * inner * half).astype(jnp.float32)
    log_friction = map_friction + taken[0]
    sliding, sent = slides(log_friction)
    far_f, near_f = across(sent), swap(sent, 1)
    height = march(peers, statics, near_s, far_s, sliding, near_f, far_f)
    return (log_friction, height)


def solution(mesh):
    return jax.shard_map(
        per_device,
        mesh=mesh,
        in_specs=(
            P(("groups", "modes"), None, None),
            P("groups"),
            P("groups"),
            P(("groups", "modes"), None),
            P(("groups", "modes"), None),
            P(("groups", "modes"), None),
            P(("groups", "modes"), None),
        ),
        out_specs=(P(("groups", "modes"), None), P(("groups", "modes"), None)),
        check_vma=False,
    )
```

time: 118 us -> 36.4 us (0.31)
  waiting for transfers between devices: 61.7 us -> 8.23 us
  other arithmetic: 14.1 us -> 0.36 us
  between operations: 14.4 us -> 0.83 us
  Pallas kernels: 0 us -> 11 us
  matrix products: 9.37 us -> 0 us
  local copies, waits for them, and re-layouts: 3.52 us -> 1.4 us
    reduce_scatter x1 -> x0, waiting for transfers between devices: 54.8 us -> none  [per_device(): lax.psum_scatter(jnp.einsum('k,kxy->xy', local_w, mode_fields, preferred_...]
    pallas_call x0 -> x5, Pallas kernels: none -> 11 us  [the longest x1 5.23 us: march(): pl.pallas_call(kernel, in_specs=[vmem] * 6, out_specs=vmem, out_shape=jax...]
    dot_general x1 -> x0, matrix products: 9.37 us -> none  [per_device(): jnp.einsum('k,kxy->xy', local_w, mode_fields, preferred_element_type=jnp....]
    min x8 -> x0, other arithmetic: 5.76 us -> none  [advance(): diff = jnp.minimum(diff + slide_rate * squared * jnp.exp(-fcent), diff_cap)]
    select_n x7 -> x0, other arithmetic: 5.59 us -> none  [march(): extended = jnp.where(inside[:, None], extended, 0.0)]
    dot_general x1 -> x0, local copies, waits for them, and re-layouts: 2.22 us -> none  [per_device(): jnp.einsum('k,kxy->xy', local_w, mode_fields, preferred_element_type=jnp....]
    ppermute x4 -> x9, waiting for transfers between devices: 6.94 us -> 8.23 us  [the longest x7 6.43 us: swap(): return lax.ppermute(value, 'modes', [(i, i ^ mask) for i in range(peers)])]
    ppermute x4 -> x9, starting transfers between devices: 13.4 us -> 14.2 us  [the longest x2 7.41 us: across(): return lax.ppermute(value, 'modes', pairs + [(j, i) for i, j in pairs])]
  transfers between devices with their start and end apart: 5 -> 9, of which waited for: 3 -> 4; matrix products, arithmetic and copies ran while one was open for 1% -> 0% of each run, Pallas kernels for 0% -> 10%
where the time goes in v1:
time: 36.4 us; the launch traced here: 36 us
  starting transfers between devices  14.2 us (39%)
  Pallas kernels  11 us (30%)
  waiting for transfers between devices  8.23 us (23%)
  local copies, waits for them, and re-layouts  1.4 us (4%)
  between operations  0.83 us (2%)
    ppermute x2, starting transfers between devices, across(): return lax.ppermute(value, 'modes', pairs + [(j, i) for i, j in pairs])  7.41 us
    ppermute x7, starting transfers between devices, swap(): return lax.ppermute(value, 'modes', [(i, i ^ mask) for i in range(peers)])  6.79 us
    ppermute x7, waiting for transfers between devices, swap(): return lax.ppermute(value, 'modes', [(i, i ^ mask) for i in range(peers)])  6.43 us
    pallas_call x1, Pallas kernels, march(): pl.pallas_call(kernel, in_specs=[vmem] * 6, out_specs=vmem, out_shape=jax...  5.23 us
    pallas_call x2, Pallas kernels, shares(): pl.pallas_call(kernel, in_specs=[pl.BlockSpec(memory_space=pl.ANY)] * 3,...  4.76 us
    ppermute x2, waiting for transfers between devices, across(): return lax.ppermute(value, 'modes', pairs + [(j, i) for i, j in pairs])  1.8 us
    unnamed x14, local copies, waits for them, and re-layouts  1.33 us
  transfers between devices with their start and end apart: 9, of which 4 were waited for; matrix products, arithmetic and copies ran while one was open for 0% of the time, Pallas kernels for 10%

profile of v1, /device:TPU:1, one launch (start us, length us, event | category | flops | bytes accessed | tf_op | source)
XLA Modules:
  0.0 36.0 jit_solution(8577975682026968296)
XLA Ops:
  0.6 0.0 copy-start.4
  0.6 0.6 %copy-done.4 = f32[128]{0:T(128)S(1)} copy-done((f32[128]{0:T(128)S(1)}, f32[128]{0:T(128)}, u32[]{:S(2)}) %copy-start.4) | copy-done | bytes 536
  1.3 0.0 copy-start.5
  1.3 0.7 %copy-done.5 = f32[128]{0:T(128)S(1)} copy-done((f32[128]{0:T(128)S(1)}, f32[128]{0:T(128)}, u32[]{:S(2)}) %copy-start.5) | copy-done | bytes 536
  1.9 2.3 %shard_map.87 = bf16[8,16,2048]{2,1,0:T(8,128)(2,1)S(1)} custom-call(f32[1,128]{1,0:T(1,128)S(1)} %bitcast.6, f32[1,128]{1,0:T(1,128)S(1)} %bitcast.8, bf16[8,256,2048]{2,1,0:T(8,128)(2,1)} %refs_2_.4), custom_call_target="tpu_custom_call" | custom-call | flops 4194304 | bytes 4194304 | tf_op jit(solution)/shard_map/pallas_call | solution.py:136
  4.3 0.0 copy-start.1
  4.3 0.0 copy-start.2
  4.3 0.0 copy-start.3
  4.3 0.0 copy-start.6
  4.3 0.1 collective-permute-start
  4.5 2.4 %shard_map.86 = f32[8,16,2048]{2,1,0:T(8,128)S(1)} custom-call(f32[1,128]{1,0:T(1,128)S(1)} %bitcast.7, f32[1,128]{1,0:T(1,128)S(1)} %bitcast.9, bf16[8,256,2048]{2,1,0:T(8,128)(2,1)} %refs_2_.4), custom_call_target="tpu_custom_call" | custom-call | flops 4194304 | bytes 4194304 | tf_op jit(solution)/shard_map/pallas_call | solution.py:136
  6.9 0.0 collective-permute-done
  6.9 0.2 fusion.2
  7.1 0.1 fusion.3
  7.2 3.7 %collective-permute-start.1 = (f16[2,16,2048]{2,1,0:T(8,128)(2,1)S(1)}, f16[2,16,2048]{2,1,0:T(8,128)(2,1)S(1)}, u32[]{:S(2)}, u32[]{:S(2)}) collective-permute-start(f16[2,16,2048]{2,1,0:T(8,128)(2,1)S(1)} %get-tuple-element.10), channel_id=1, source_target_pairs={{0,6},{1,7},{2,4},{3,5},{4,2},{5,3},{6,0},{7,1},{8,14},{9,15},{10,... | collective-permute-start | bytes 393224 | tf_op jit(solution)/shard_map/ppermute | solution.py:302
  10.8 0.2 collective-permute-start.3
  11.1 0.1 collective-permute-start.2
  11.2 3.4 %collective-permute-done.1 = f16[2,16,2048]{2,1,0:T(8,128)(2,1)S(1)} collective-permute-done((f16[2,16,2048]{2,1,0:T(8,128)(2,1)S(1)}, f16[2,16,2048]{2,1,0:T(8,128)(2,1)S(1)}, u32[]{:S(2)}, u32[]{:S(2)}) %collective-permute-start.1) | collective-permute-done | bytes 131104 | tf_op jit(solution)/shard_map/ppermute | solution.py:302
  14.6 3.0 %collective-permute-done.3 = f16[2,16,2048]{2,1,0:T(8,128)(2,1)S(1)} collective-permute-done((f16[2,16,2048]{2,1,0:T(8,128)(2,1)S(1)}, f16[2,16,2048]{2,1,0:T(8,128)(2,1)S(1)}, u32[]{:S(2)}, u32[]{:S(2)}) %collective-permute-start.3) | collective-permute-done | bytes 131104 | tf_op jit(solution)/shard_map/ppermute | solution.py:302
  17.6 0.0 collective-permute-done.2
  17.6 0.1 convert_add_fusion.1
  17.7 2.5 %collective-permute-start.4 = (f16[1,16,2048]{2,1,0:T(8,128)(2,1)S(1)}, f16[1,16,2048]{2,1,0:T(8,128)(2,1)S(1)}, u32[]{:S(2)}, u32[]{:S(2)}) collective-permute-start(f16[1,16,2048]{2,1,0:T(8,128)(2,1)S(1)} %slice_convert_fusion), channel_id=1, source_target_pairs={{0,8},{1,9},{2,10},{3,11},{4,12},{5,13},{6,14},{7,15},{8,0},{9,1},... | collective-permute-start | bytes 196616 | tf_op jit(solution)/shard_map/ppermute | solution.py:302
  20.2 0.0 copy-done.1
  20.2 0.0 copy-done.2
  20.2 0.0 copy-done.3
  20.2 0.7 %shard_map.88.refs_0_ = f32[3,16,16,128]{3,2,1,0:T(8,128)S(1)} custom-call(f32[16,2048]{1,0:T(8,128)S(1)} %copy-done.1, f32[16,2048]{1,0:T(8,128)S(1)} %copy-done.2, f32[16,2048]{1,0:T(8,128)S(1)} %copy-done.3), custom_call_target="tpu_custom_call" | custom-call | flops 4194304 | bytes 4194304 | tf_op jit(solution)/shard_map/pallas_call | solution.py:57
  20.9 3.8 %collective-permute-start.6 = (f16[3,16,16,128]{3,2,1,0:T(8,128)(2,1)S(1)}, f16[3,16,16,128]{3,2,1,0:T(8,128)(2,1)S(1)}, u32[]{:S(2)}, u32[]{:S(2)}) collective-permute-start(f16[3,16,16,128]{3,2,1,0:T(8,128)(2,1)S(1)} %convert_element_type.33), channel_id=1, source_target_pairs={{1,2},{3,4},{5,6},{7,8},{9,10},{11,12},{13,14},{2,1},{4,3},{6,5},{... | collective-permute-start | bytes 589832 | tf_op jit(solution)/shard_map/ppermute | solution.py:306
  24.7 0.1 collective-permute-start.5
  24.8 0.0 collective-permute-done.4
  24.8 0.0 copy-done.6
  24.8 0.0 copy-start
  24.9 0.3 shard_map.89
  25.2 3.6 %collective-permute-start.8 = (bf16[16,16,128]{2,1,0:T(8,128)(2,1)S(1)}, bf16[16,16,128]{2,1,0:T(8,128)(2,1)S(1)}, u32[]{:S(2)}, u32[]{:S(2)}) collective-permute-start(bf16[16,16,128]{2,1,0:T(8,128)(2,1)S(1)} %get-tuple-element.7), channel_id=1, source_target_pairs={{1,2},{3,4},{5,6},{7,8},{9,10},{11,12},{13,14},{2,1},{4,3},{6,5},{... | collective-permute-start | bytes 196616 | tf_op jit(solution)/shard_map/ppermute | solution.py:306
  28.8 0.1 collective-permute-start.7
  28.9 0.5 %collective-permute-done.6 = f16[3,16,16,128]{3,2,1,0:T(8,128)(2,1)S(1)} collective-permute-done((f16[3,16,16,128]{3,2,1,0:T(8,128)(2,1)S(1)}, f16[3,16,16,128]{3,2,1,0:T(8,128)(2,1)S(1)}, u32[]{:S(2)}, u32[]{:S(2)}) %collective-permute-start.6) | collective-permute-done | bytes 196640 | tf_op jit(solution)/shard_map/ppermute | solution.py:306
  29.5 0.0 collective-permute-done.5
  29.5 1.3 %collective-permute-done.8.refs_5_ = bf16[16,16,128]{2,1,0:T(8,128)(2,1)S(1)} collective-permute-done((bf16[16,16,128]{2,1,0:T(8,128)(2,1)S(1)}, bf16[16,16,128]{2,1,0:T(8,128)(2,1)S(1)}, u32[]{:S(2)}, u32[]{:S(2)}) %collective-permute-start.8) | collective-permute-done | bytes 65568 | tf_op jit(solution)/shard_map/ppermute | solution.py:306
  30.8 0.0 collective-permute-done.7.refs_4_
  30.8 5.2 %shard_map.90 = f32[16,2048]{1,0:T(8,128)} custom-call(f32[3,16,16,128]{3,2,1,0:T(8,128)S(1)} %shard_map.88.refs_0_, f32[3,16,16,128]{3,2,1,0:T(8,128)S(1)} %convert_element_type.34.refs_1_, f32[3,16,16,128]{3,2,1,0:T(8,128)S(1)} %convert_element_type.35.refs_2_, f32[16,16,128]{2,1,0:T(8,128)S(1)} %get-tuple-element.6.refs_3_, ...), custom_call_target="tpu_custom_call" | custom-call | tf_op jit(solution)/shard_map/pallas_call | solution.py:284
  36.0 0.0 copy-done
  (5 shorter events, 0.1 us)
Async XLA Ops:
  0.6 0.7 %copy-start.4 = (f32[128]{0:T(128)S(1)}, f32[128]{0:T(128)}, u32[]{:S(2)}) copy-start(f32[128]{0:T(128)} %param.8) | copy-start | bytes 1540
  1.3 0.7 %copy-start.5 = (f32[128]{0:T(128)S(1)}, f32[128]{0:T(128)}, u32[]{:S(2)}) copy-start(f32[128]{0:T(128)} %param.9) | copy-start | bytes 1540
  4.3 15.9 %copy-start.1 = (f32[16,2048]{1,0:T(8,128)S(1)}, f32[16,2048]{1,0:T(8,128)}, u32[]{:S(2)}) copy-start(f32[16,2048]{1,0:T(8,128)} %refs_0_) | copy-start | bytes 393220
  4.3 15.9 %copy-start.2 = (f32[16,2048]{1,0:T(8,128)S(1)}, f32[16,2048]{1,0:T(8,128)}, u32[]{:S(2)}) copy-start(f32[16,2048]{1,0:T(8,128)} %refs_1_.1) | copy-start | bytes 393220
  4.3 15.9 %copy-start.3 = (f32[16,2048]{1,0:T(8,128)S(1)}, f32[16,2048]{1,0:T(8,128)}, u32[]{:S(2)}) copy-start(f32[16,2048]{1,0:T(8,128)} %refs_2_.5) | copy-start | bytes 393220
  4.3 20.5 %copy-start.6 = (f32[16,2048]{1,0:T(8,128)S(1)}, f32[16,2048]{1,0:T(8,128)}, u32[]{:S(2)}) copy-start(f32[16,2048]{1,0:T(8,128)} %param.10) | copy-start | bytes 393220
  4.3 2.6 %collective-permute-start = (bf16[8,16,2048]{2,1,0:T(8,128)(2,1)S(1)}, bf16[8,16,2048]{2,1,0:T(8,128)(2,1)S(1)}, u32[]{:S(2)}, u32[]{:S(2)}) collective-permute-start(bf16[8,16,2048]{2,1,0:T(8,128)(2,1)S(1)} %shard_map.87), channel_id=1, source_target_pairs={{0,1},{1,0},{2,3},{3,2},{4,5},{5,4},{6,7},{7,6},{8,9},{9,8},{10,11... | collective-permute-start | bytes 1572872 | tf_op jit(solution)/shard_map/ppermute | solution.py:302
  7.2 7.4 %collective-permute-start.1 = (f16[2,16,2048]{2,1,0:T(8,128)(2,1)S(1)}, f16[2,16,2048]{2,1,0:T(8,128)(2,1)S(1)}, u32[]{:S(2)}, u32[]{:S(2)}) collective-permute-start(f16[2,16,2048]{2,1,0:T(8,128)(2,1)S(1)} %get-tuple-element.10), channel_id=1, source_target_pairs={{0,6},{1,7},{2,4},{3,5},{4,2},{5,3},{6,0},{7,1},{8,14},{9,15},{10,... | collective-permute-start | bytes 393224 | tf_op jit(solution)/shard_map/ppermute | solution.py:302
  10.8 6.8 %collective-permute-start.3 = (f16[2,16,2048]{2,1,0:T(8,128)(2,1)S(1)}, f16[2,16,2048]{2,1,0:T(8,128)(2,1)S(1)}, u32[]{:S(2)}, u32[]{:S(2)}) collective-permute-start(f16[2,16,2048]{2,1,0:T(8,128)(2,1)S(1)} %get-tuple-element.11), channel_id=1, source_target_pairs={{0,2},{1,3},{2,0},{3,1},{4,6},{5,7},{6,4},{7,5},{8,10},{9,11},{10,... | collective-permute-start | bytes 393224 | tf_op jit(solution)/shard_map/ppermute | solution.py:302
  11.1 6.6 %collective-permute-start.2 = (f16[2,16,2048]{2,1,0:T(8,128)(2,1)S(1)}, f16[2,16,2048]{2,1,0:T(8,128)(2,1)S(1)}, u32[]{:S(2)}, u32[]{:S(2)}) collective-permute-start(f16[2,16,2048]{2,1,0:T(8,128)(2,1)S(1)} %get-tuple-element.12), channel_id=1, source_target_pairs={{0,4},{1,5},{2,6},{3,7},{4,0},{5,1},{6,2},{7,3},{8,12},{9,13},{10,... | collective-permute-start | bytes 393224 | tf_op jit(solution)/shard_map/ppermute | solution.py:302
  17.7 7.1 %collective-permute-start.4 = (f16[1,16,2048]{2,1,0:T(8,128)(2,1)S(1)}, f16[1,16,2048]{2,1,0:T(8,128)(2,1)S(1)}, u32[]{:S(2)}, u32[]{:S(2)}) collective-permute-start(f16[1,16,2048]{2,1,0:T(8,128)(2,1)S(1)} %slice_convert_fusion), channel_id=1, source_target_pairs={{0,8},{1,9},{2,10},{3,11},{4,12},{5,13},{6,14},{7,15},{8,0},{9,1},... | collective-permute-start | bytes 196616 | tf_op jit(solution)/shard_map/ppermute | solution.py:302
  20.9 8.5 %collective-permute-start.6 = (f16[3,16,16,128]{3,2,1,0:T(8,128)(2,1)S(1)}, f16[3,16,16,128]{3,2,1,0:T(8,128)(2,1)S(1)}, u32[]{:S(2)}, u32[]{:S(2)}) collective-permute-start(f16[3,16,16,128]{3,2,1,0:T(8,128)(2,1)S(1)} %convert_element_type.33), channel_id=1, source_target_pairs={{1,2},{3,4},{5,6},{7,8},{9,10},{11,12},{13,14},{2,1},{4,3},{6,5},{... | collective-permute-start | bytes 589832 | tf_op jit(solution)/shard_map/ppermute | solution.py:306
  24.7 4.7 %collective-permute-start.5 = (f16[3,16,16,128]{3,2,1,0:T(8,128)(2,1)S(1)}, f16[3,16,16,128]{3,2,1,0:T(8,128)(2,1)S(1)}, u32[]{:S(2)}, u32[]{:S(2)}) collective-permute-start(f16[3,16,16,128]{3,2,1,0:T(8,128)(2,1)S(1)} %convert_element_type.33), channel_id=1, source_target_pairs={{0,1},{1,0},{2,3},{3,2},{4,5},{5,4},{6,7},{7,6},{8,9},{9,8},{10,11... | collective-permute-start | bytes 589832 | tf_op jit(solution)/shard_map/ppermute | solution.py:302
  24.8 11.2 %copy-start = (f32[16,2048]{1,0:T(8,128)}, f32[16,2048]{1,0:T(8,128)S(1)}, u32[]{:S(2)}) copy-start(f32[16,2048]{1,0:T(8,128)S(1)} %fusion.1.friction) | copy-start | bytes 393220
  25.2 5.6 %collective-permute-start.8 = (bf16[16,16,128]{2,1,0:T(8,128)(2,1)S(1)}, bf16[16,16,128]{2,1,0:T(8,128)(2,1)S(1)}, u32[]{:S(2)}, u32[]{:S(2)}) collective-permute-start(bf16[16,16,128]{2,1,0:T(8,128)(2,1)S(1)} %get-tuple-element.7), channel_id=1, source_target_pairs={{1,2},{3,4},{5,6},{7,8},{9,10},{11,12},{13,14},{2,1},{4,3},{6,5},{... | collective-permute-start | bytes 196616 | tf_op jit(solution)/shard_map/ppermute | solution.py:306
  28.8 2.0 %collective-permute-start.7 = (bf16[16,16,128]{2,1,0:T(8,128)(2,1)S(1)}, bf16[16,16,128]{2,1,0:T(8,128)(2,1)S(1)}, u32[]{:S(2)}, u32[]{:S(2)}) collective-permute-start(bf16[16,16,128]{2,1,0:T(8,128)(2,1)S(1)} %get-tuple-element.7), channel_id=1, source_target_pairs={{0,1},{1,0},{2,3},{3,2},{4,5},{5,4},{6,7},{7,6},{8,9},{9,8},{10,11... | collective-permute-start | bytes 196616 | tf_op jit(solution)/shard_map/ppermute | solution.py:302

commit v2 on v1

--- a/solution.py
+++ b/solution.py
@@ -14,6 +14,10 @@
 slide_rate = 0.1
 diff_cap = 0.5
 time_step = 0.4
+
+unit = (0.25 * flow_rate * 0.5 * time_step) ** (1.0 / 7.0)
+slide_unit = 0.5 * time_step * slide_rate / (unit * unit)
+cap_unit = 0.5 * time_step * diff_cap
 
 
 def lanes():
@@ -64,7 +68,7 @@
 
 def slide_fold(friction, wide, narrow):
     blocks, rows = wide.shape[0], wide.shape[1]
-    parts = fold([slide_rate * jnp.exp(-part) for part in cut(friction, slice(0, rows), blocks)])
+    parts = fold([slide_unit * jnp.exp(-part) for part in cut(friction, slice(0, rows), blocks)])
     for p, part in enumerate(parts):
         wide[p] = part
         narrow[p] = part.astype(narrow.dtype)
@@ -135,7 +139,7 @@
 
     return pl.pallas_call(
         kernel,
-        in_specs=[pl.BlockSpec(memory_space=pl.ANY)] * 3,
+        in_specs=[pl.BlockSpec(memory_space=pltpu.HBM)] * 3,
         out_specs=pl.BlockSpec(memory_space=pltpu.VMEM),
         out_shape=jax.ShapeDtypeStruct((strips, rows, columns), dtype),
         scratch_shapes=[
@@ -156,71 +160,96 @@
 NEVER = -1e30
 
 
-def ice(peers, own_s, near_s, far_s, own_f, near_f, far_f, out, h0, s0, h1, s1, bed, bal, slide, diff):
+def wrap(value, to_right, blocks):
+    lane = lanes()
+    if to_right:
+        turned = jnp.where(
+            lane >= LANES - blocks,
+            pltpu.roll(value, LANES - blocks - 1, 1),
+            pltpu.roll(value, LANES - blocks, 1),
+        )
+        return jnp.where(lane == LANES - 1, 0.0, turned)
+    turned = jnp.where(lane < blocks, pltpu.roll(value, blocks + 1, 1), pltpu.roll(value, blocks, 1))
+    return jnp.where(lane == 0, 0.0, turned)
+
+
+def wrap_slots(ref, at, blocks, count):
+    for q in range(count):
+        ref[blocks + 2 + q, at, :] = wrap(ref[q + 2, at, :], True, blocks)
+        ref[1 - q, at, :] = wrap(ref[blocks + 1 - q, at, :], False, blocks)
+
+
+def spots(rows, reach):
+    odd = lax.axis_index("modes") % 2 == 1
+    near = pl.multiple_of(PAD + jnp.where(odd, 0, rows + reach), 8)
+    far = pl.multiple_of(PAD + jnp.where(odd, rows + reach, 0), 8)
+    return pl.ds(PAD + reach, rows), pl.ds(near, reach), pl.ds(far, reach)
+
+
+def settle(peers, own_s, near_s, far_s, h0, s0, bed, bal):
+    _, blocks, rows, _ = own_s.shape
+    reach = 2 * STEPS
+    me = lax.axis_index("modes")
+    odd, above, below = me % 2 == 1, me > 0, me < peers - 1
+    sides = (None, jnp.where(odd, above, below), jnp.where(odd, below, above))
+
+    def block(p, carry):
+        for src, at, inside in zip((own_s, near_s, far_s), spots(rows, reach), sides):
+            h, b, m = (src[a, p] for a in range(3))
+            h, b, m = unit * h, unit * b, (time_step * unit) * m
+            h0[p + 2, at, :] = h
+            s0[p + 2, at, :] = h + b
+            bed[p + 2, at, :] = b
+            bal[p + 2, at, :] = m if inside is None else jnp.where(inside, m, NEVER)
+        return carry
+
+    lax.fori_loop(0, blocks, block, 0, unroll=2)
+    whole = pl.ds(PAD, rows + 2 * reach)
+    wrap_slots(s0, whole, blocks, 2)
+    wrap_slots(bed, whole, blocks, 1)
+    wrap_slots(h0, whole, blocks, 1)
+
+
+def settled(peers, own_s, near_s, far_s):
+    _, blocks, rows, _ = own_s.shape
+    shape = (blocks + 4, rows + 4 * STEPS + 2 * PAD, LANES)
+
+    def kernel(*refs):
+        settle(peers, *refs)
+
+    return pl.pallas_call(
+        kernel,
+        out_shape=[jax.ShapeDtypeStruct(shape, jnp.float32)] * 4,
+        compiler_params=pltpu.CompilerParams(vmem_limit_bytes=8 << 20),
+        cost_estimate=pl.CostEstimate(flops=1, bytes_accessed=1, transcendentals=0),
+    )(own_s, near_s, far_s)
+
+
+def ice(own_f, near_f, far_f, h_in, s_in, bed, bal, out, h0, s0, h1, s1, slide, diff):
     blocks, rows, _ = own_f.shape
     reach = 2 * STEPS
     extent = rows + 2 * reach
-    me = lax.axis_index("modes")
-    zero = jnp.minimum(me, 0)
-    odd = me % 2 == 1
-    above, below = me > 0, me < peers - 1
-    mid_at = pl.ds(PAD + reach, rows)
-    near_at = pl.ds(pl.multiple_of(PAD + jnp.where(odd, 0, rows + reach), 8), reach)
-    far_at = pl.ds(pl.multiple_of(PAD + jnp.where(odd, rows + reach, 0), 8), reach)
-    near_in = jnp.where(odd, above, below)
-    far_in = jnp.where(odd, below, above)
-    lane = lanes()
-
-    def place_in(p, carry):
-        slot = p + 2
-        for src, at, inside in ((own_s, mid_at, True), (near_s, near_at, near_in), (far_s, far_at, far_in)):
-            h, b, m = (src[a, p].astype(jnp.float32) for a in range(3))
-            h0[slot, at, :] = h
-            s0[slot, at, :] = h + b
-            bed[slot, at, :] = b
-            m = time_step * m
-            bal[slot, at, :] = m if inside is True else jnp.where(inside, m, NEVER)
-        for src, at in ((own_f, mid_at), (near_f, near_at), (far_f, far_at)):
-            slide[slot, at, :] = src[p].astype(jnp.float32)
-        return carry
-
-    lax.fori_loop(0, blocks, place_in, 0, unroll=4)
-
-    def wrap(ref, at, count):
-        for q in range(count):
-            x = ref[q + 2, at, :]
-            x = jnp.where(
-                lane >= LANES - blocks,
-                jnp.where(lane == LANES - 1, 0.0, pltpu.roll(x, LANES - blocks - 1, 1)),
-                pltpu.roll(x, LANES - blocks, 1),
-            )
-            ref[blocks + 2 + q, at, :] = x
-            x = ref[blocks + 1 - q, at, :]
-            x = jnp.where(
-                lane < blocks,
-                jnp.where(lane == 0, 0.0, pltpu.roll(x, blocks + 1, 1)),
-                pltpu.roll(x, blocks, 1),
-            )
-            ref[1 - q, at, :] = x
-
-    whole = pl.ds(PAD, extent)
-    wrap(s0, whole, 2)
-    wrap(h0, whole, 1)
-    wrap(slide, whole, 1)
+    zero = jnp.minimum(lax.axis_index("modes"), 0)
+
+    def block(p, carry):
+        for src, at in zip((own_f, near_f, far_f), spots(rows, reach)):
+            slide[p + 2, at, :] = src[p].astype(jnp.float32)
+        return carry
+
+    lax.fori_loop(0, blocks, block, 0, unroll=4)
+    wrap_slots(slide, pl.ds(PAD, extent), blocks, 1)
 
     for step in range(STEPS):
-        h, s, hn, sn = (h0, s0, h1, s1) if step % 2 == 0 else (h1, s1, h0, s0)
+        h, s = (h_in, s_in) if step == 0 else ((h0, s0), (h1, s1))[step % 2]
+        hn, sn = ((h1, s1), (h0, s0))[step % 2]
         final = step == STEPS - 1
         edge = 2 * step + 2
 
         def window(first):
-            low = first // 8 * 8
-            at = pl.ds(PAD + low, extent - 2 * low)
-            up = pl.ds(PAD + low - 1 + zero, extent - 2 * low)
-            down = pl.ds(PAD + low + 1 + zero, extent - 2 * low)
-            return at, up, down
-
-        at, up, down = window(edge - 1)
+            count = -(-(extent - 2 * first) // 8) * 8
+            return [pl.ds(PAD + first + off + zero, count) for off in (-1, 0, 1)]
+
+        up, at, down = window(edge - 1)
 
         def diffuse(i, carry, h=h, s=s, at=at, up=up, down=down):
             for q in range(span):
@@ -229,13 +258,13 @@
                 gy = s[j + 1, at, :] - s[j - 1, at, :]
                 thick = h[j, at, :]
                 squared = thick * thick
-                grad = (gx * gx + gy * gy) * (0.25 * flow_rate)
-                diff[j, at, :] = jnp.minimum(squared * (squared * thick * grad + slide[j, at, :]), diff_cap)
+                value = squared * (squared * thick * (gx * gx + gy * gy) + slide[j, at, :])
+                diff[j, at, :] = jnp.minimum(value, cap_unit)
             return carry
 
         span = (blocks + 2) // 2
         lax.fori_loop(0, 2, diffuse, 0)
-        at, up, down = window(edge)
+        up, at, down = window(edge)
 
         def flow(i, carry, h=h, s=s, hn=hn, sn=sn, at=at, up=up, down=down, final=final):
             first = 2 + i * count
@@ -248,7 +277,7 @@
                 total = right - left
                 total += (diff[j, down, :] + d_mid) * (s[j, down, :] - s_mid)
                 total -= (diff[j, up, :] + d_mid) * (s_mid - s[j, up, :])
-                value = jnp.maximum(h[j, at, :] + (0.5 * time_step) * total + bal[j, at, :], 0.0)
+                value = jnp.maximum(h[j, at, :] + total + bal[j, at, :], 0.0)
                 hn[j, at, :] = value
                 if not final:
                     sn[j, at, :] = value + bed[j, at, :]
@@ -258,37 +287,31 @@
         count = min(GROUP, blocks)
         lax.fori_loop(0, blocks // count, flow, 0)
         if not final:
-            wrap(sn, at, 2)
-            wrap(hn, at, 1)
+            wrap_slots(sn, at, blocks, 2)
+            for slot in (1, blocks + 2):
+                hn[slot, at, :] = sn[slot, at, :] - bed[slot, at, :]
 
     h = h1 if STEPS % 2 else h0
 
     def tile(r, carry):
         at = pl.ds(pl.multiple_of(r * 8, 8), 8)
         from_at = pl.ds(pl.multiple_of(PAD + reach + r * 8, 8), 8)
-        for k, part in enumerate(fold([h[p + 2, from_at, :] for p in range(blocks)])):
+        for k, part in enumerate(fold([h[p + 2, from_at, :] * (1.0 / unit) for p in range(blocks)])):
             out[at, k * LANES : (k + 1) * LANES] = part
         return carry
 
     lax.fori_loop(0, rows // 8, tile, 0)
 
 
-def march(peers, own_s, near_s, far_s, own_f, near_f, far_f):
+def march(own_f, near_f, far_f, *state):
     blocks, rows, _ = own_f.shape
-    vmem = pl.BlockSpec(memory_space=pltpu.VMEM)
-    scratch = pltpu.VMEM((blocks + 4, rows + 4 * STEPS + 2 * PAD, LANES), jnp.float32)
-
-    def kernel(*refs):
-        ice(peers, *refs)
-
-    return pl.pallas_call(
-        kernel,
-        in_specs=[vmem] * 6,
-        out_specs=vmem,
+    scratch = pltpu.VMEM(state[0].shape, jnp.float32)
+    return pl.pallas_call(
+        ice,
         out_shape=jax.ShapeDtypeStruct((rows, blocks * LANES), jnp.float32),
-        scratch_shapes=[scratch] * 8,
+        scratch_shapes=[scratch] * 6,
         compiler_params=pltpu.CompilerParams(vmem_limit_bytes=32 << 20),
-    )(own_s, near_s, far_s, own_f, near_f, far_f)
+    )(own_f, near_f, far_f, *state)
 
 
 def per_device(mode_fields, coeff, eigen, map_friction, bed, smb, thickness):
@@ -305,8 +328,11 @@
         pairs = [(i, i + 1) for i in range(1, peers - 1, 2)]
         return lax.ppermute(value, "modes", pairs + [(j, i) for i, j in pairs])
 
-    given = shares(coeff[None], eigen[None], mode_fields, rows, False, jnp.bfloat16)
-    kept = shares(coeff[None], eigen[None], mode_fields, rows, True, jnp.float32)
+    coeff, eigen, mode_fields = (
+        pltpu.with_memory_space_constraint(x, pltpu.HBM) for x in (coeff[None], eigen[None], mode_fields)
+    )
+    given = shares(coeff, eigen, mode_fields, rows, False, jnp.bfloat16)
+    kept = shares(coeff, eigen, mode_fields, rows, True, jnp.float32)
     total = kept + swap(given, 1).astype(jnp.float32)
     strips = total.shape[0]
     inner = min(strips, 4)
@@ -317,15 +343,17 @@
     thickness, total = lax.optimization_barrier((thickness, total))
     statics = folded(thickness, bed, smb)
     sent = statics.astype(jnp.float16)
-    near_s, far_s = swap(sent, 1).astype(jnp.float32), across(sent).astype(jnp.float32)
-
+    far_s, near_s = across(sent).astype(jnp.float32), swap(sent, 1).astype(jnp.float32)
+
+    taken, sent = lax.optimization_barrier((taken, sent))
     while taken.shape[0] > 1:
         half = taken.shape[0] // 2
         taken = taken[:half] + swap(taken[half:].astype(jnp.float16), 2 * inner * half).astype(jnp.float32)
     log_friction = map_friction + taken[0]
     sliding, sent = slides(log_friction)
     far_f, near_f = across(sent), swap(sent, 1)
-    height = march(peers, statics, near_s, far_s, sliding, near_f, far_f)
+    state = settled(peers, statics, near_s, far_s)
+    height = march(sliding, near_f, far_f, *state)
     return (log_friction, height)
 
 

time: 36.4 us -> 33.6 us (0.923)
  local copies, waits for them, and re-layouts: 1.4 us -> 0.1 us
  waiting for transfers between devices: 8.23 us -> 7.15 us
    unnamed x14 -> x10, local copies, waits for them, and re-layouts: 1.33 us -> 0.03 us
    ppermute x7, waiting for transfers between devices: 6.43 us -> 5.7 us  [swap(): return lax.ppermute(value, 'modes', [(i, i ^ mask) for i in range(peers)])]
    pallas_call x3 -> x4, Pallas kernels: 9.99 us -> 9.66 us  [the longest x2 4.84 us: shares(): pl.pallas_call(kernel, in_specs=[pl.BlockSpec(memory_space=pltpu.HBM)] *...]
  transfers between devices with their start and end apart: 9 -> 9, of which waited for: 4 -> 4; matrix products, arithmetic and copies ran while one was open for 0% -> 0% of each run, Pallas kernels for 10% -> 11%
where the time goes in v2:
time: 33.6 us; the launch traced here: 33.3 us
  starting transfers between devices  14.2 us (42%)
  Pallas kernels  10.7 us (32%)
  waiting for transfers between devices  7.15 us (21%)
  between operations  0.83 us (2%)
  other arithmetic  0.34 us (1%)
    ppermute x2, starting transfers between devices, across(): return lax.ppermute(value, 'modes', pairs + [(j, i) for i, j in pairs])  7.4 us
    ppermute x7, starting transfers between devices, swap(): return lax.ppermute(value, 'modes', [(i, i ^ mask) for i in range(peers)])  6.79 us
    ppermute x7, waiting for transfers between devices, swap(): return lax.ppermute(value, 'modes', [(i, i ^ mask) for i in range(peers)])  5.7 us
    pallas_call x2, Pallas kernels, shares(): pl.pallas_call(kernel, in_specs=[pl.BlockSpec(memory_space=pltpu.HBM)] *...  4.84 us
    pallas_call x1, Pallas kernels, march(): pl.pallas_call(ice, out_shape=jax.ShapeDtypeStruct((rows, blocks * LANES)...  4.47 us
    ppermute x2, waiting for transfers between devices, across(): return lax.ppermute(value, 'modes', pairs + [(j, i) for i, j in pairs])  1.45 us
  transfers between devices with their start and end apart: 9, of which 4 were waited for; matrix products, arithmetic and copies ran while one was open for 0% of the time, Pallas kernels for 11%

profile of v2, /device:TPU:1, one launch (start us, length us, event | category | flops | bytes accessed | tf_op | source)
XLA Modules:
  0.0 33.3 jit_solution(15989916358785339766)
XLA Ops:
  0.6 2.4 %shard_map.87 = bf16[8,16,2048]{2,1,0:T(8,128)(2,1)S(1)} custom-call(f32[1,128]{1,0:T(1,128)} %bitcast.4, f32[1,128]{1,0:T(1,128)} %bitcast.6, bf16[8,256,2048]{2,1,0:T(8,128)(2,1)} %refs_2_.4), custom_call_target="tpu_custom_call" | custom-call | flops 4194304 | bytes 4194304 | tf_op jit(solution)/shard_map/pallas_call | solution.py:140
  3.0 0.0 copy-start.1
  3.0 0.0 copy-start.2
  3.1 0.0 copy-start.3
  3.1 0.0 copy-start.4
  3.1 0.1 collective-permute-start
  3.2 2.5 %shard_map.86 = f32[8,16,2048]{2,1,0:T(8,128)S(1)} custom-call(f32[1,128]{1,0:T(1,128)} %bitcast.5, f32[1,128]{1,0:T(1,128)} %bitcast.7, bf16[8,256,2048]{2,1,0:T(8,128)(2,1)} %refs_2_.4), custom_call_target="tpu_custom_call" | custom-call | flops 4194304 | bytes 4194304 | tf_op jit(solution)/shard_map/pallas_call | solution.py:140
  5.7 0.0 collective-permute-done
  5.7 0.2 fusion
  5.8 0.1 fusion.1
  5.9 3.7 %collective-permute-start.1 = (f16[2,16,2048]{2,1,0:T(8,128)(2,1)S(1)}, f16[2,16,2048]{2,1,0:T(8,128)(2,1)S(1)}, u32[]{:S(2)}, u32[]{:S(2)}) collective-permute-start(f16[2,16,2048]{2,1,0:T(8,128)(2,1)S(1)} %get-tuple-element.20), channel_id=1, source_target_pairs={{0,6},{1,7},{2,4},{3,5},{4,2},{5,3},{6,0},{7,1},{8,14},{9,15},{10,... | collective-permute-start | bytes 393224 | tf_op jit(solution)/shard_map/ppermute | solution.py:325
  9.6 0.2 collective-permute-start.3
  9.8 0.1 collective-permute-start.2
  10.0 0.0 copy-done.1
  10.0 0.0 copy-done.2
  10.0 0.0 copy-done.3
  10.0 0.7 %shard_map.88.refs_0_ = f32[3,16,16,128]{3,2,1,0:T(8,128)S(1)} custom-call(f32[16,2048]{1,0:T(8,128)S(1)} %copy-done.1, f32[16,2048]{1,0:T(8,128)S(1)} %copy-done.2, f32[16,2048]{1,0:T(8,128)S(1)} %copy-done.3), custom_call_target="tpu_custom_call" | custom-call | flops 4194304 | bytes 4194304 | tf_op jit(solution)/shard_map/pallas_call | solution.py:61
  10.7 2.6 %collective-permute-done.1 = f16[2,16,2048]{2,1,0:T(8,128)(2,1)S(1)} collective-permute-done((f16[2,16,2048]{2,1,0:T(8,128)(2,1)S(1)}, f16[2,16,2048]{2,1,0:T(8,128)(2,1)S(1)}, u32[]{:S(2)}, u32[]{:S(2)}) %collective-permute-start.1) | collective-permute-done | bytes 131104 | tf_op jit(solution)/shard_map/ppermute | solution.py:325
  13.3 3.0 %collective-permute-done.3 = f16[2,16,2048]{2,1,0:T(8,128)(2,1)S(1)} collective-permute-done((f16[2,16,2048]{2,1,0:T(8,128)(2,1)S(1)}, f16[2,16,2048]{2,1,0:T(8,128)(2,1)S(1)}, u32[]{:S(2)}, u32[]{:S(2)}) %collective-permute-start.3) | collective-permute-done | bytes 131104 | tf_op jit(solution)/shard_map/ppermute | solution.py:325
  16.4 0.0 collective-permute-done.2
  16.4 0.1 convert_add_fusion.1
  16.5 2.5 %collective-permute-start.4 = (f16[1,16,2048]{2,1,0:T(8,128)(2,1)S(1)}, f16[1,16,2048]{2,1,0:T(8,128)(2,1)S(1)}, u32[]{:S(2)}, u32[]{:S(2)}) collective-permute-start(f16[1,16,2048]{2,1,0:T(8,128)(2,1)S(1)} %slice_convert_fusion), channel_id=1, source_target_pairs={{0,8},{1,9},{2,10},{3,11},{4,12},{5,13},{6,14},{7,15},{8,0},{9,1},... | collective-permute-start | bytes 196616 | tf_op jit(solution)/shard_map/ppermute | solution.py:325
  18.9 3.8 %collective-permute-start.8 = (f16[3,16,16,128]{3,2,1,0:T(8,128)(2,1)S(1)}, f16[3,16,16,128]{3,2,1,0:T(8,128)(2,1)S(1)}, u32[]{:S(2)}, u32[]{:S(2)}) collective-permute-start(f16[3,16,16,128]{3,2,1,0:T(8,128)(2,1)S(1)} %convert_element_type.32), channel_id=1, source_target_pairs={{1,2},{3,4},{5,6},{7,8},{9,10},{11,12},{13,14},{2,1},{4,3},{6,5},{... | collective-permute-start | bytes 589832 | tf_op jit(solution)/shard_map/ppermute | solution.py:329
  22.7 0.1 collective-permute-start.7
  22.8 0.0 collective-permute-done.4
  22.8 0.0 copy-done.4
  22.9 0.0 copy-start
  22.9 0.3 %shard_map.89 = (f32[16,16,128]{2,1,0:T(8,128)S(1)}, bf16[16,16,128]{2,1,0:T(8,128)(2,1)S(1)}) custom-call(f32[16,2048]{1,0:T(8,128)S(1)} %bitcast_add_fusion.friction), custom_call_target="tpu_custom_call" | custom-call | tf_op jit(solution)/shard_map/pallas_call | solution.py:80
  23.2 3.6 %collective-permute-start.6 = (bf16[16,16,128]{2,1,0:T(8,128)(2,1)S(1)}, bf16[16,16,128]{2,1,0:T(8,128)(2,1)S(1)}, u32[]{:S(2)}, u32[]{:S(2)}) collective-permute-start(bf16[16,16,128]{2,1,0:T(8,128)(2,1)S(1)} %get-tuple-element.13), channel_id=1, source_target_pairs={{1,2},{3,4},{5,6},{7,8},{9,10},{11,12},{13,14},{2,1},{4,3},{6,5},{... | collective-permute-start | bytes 196616 | tf_op jit(solution)/shard_map/ppermute | solution.py:329
  26.8 0.1 collective-permute-start.5
  26.9 0.5 %collective-permute-done.8 = f16[3,16,16,128]{3,2,1,0:T(8,128)(2,1)S(1)} collective-permute-done((f16[3,16,16,128]{3,2,1,0:T(8,128)(2,1)S(1)}, f16[3,16,16,128]{3,2,1,0:T(8,128)(2,1)S(1)}, u32[]{:S(2)}, u32[]{:S(2)}) %collective-permute-start.8) | collective-permute-done | bytes 196640 | tf_op jit(solution)/shard_map/ppermute | solution.py:329
  27.5 0.0 collective-permute-done.7
  27.5 0.3 %shard_map.90 = (f32[20,64,128]{2,1,0:T(8,128)S(1)}, f32[20,64,128]{2,1,0:T(8,128)S(1)}, f32[20,64,128]{2,1,0:T(8,128)S(1)}, f32[20,64,128]{2,1,0:T(8,128)S(1)}) custom-call(f32[3,16,16,128]{3,2,1,0:T(8,128)S(1)} %shard_map.88.refs_0_, f32[3,16,16,128]{3,2,1,0:T(8,128)S(1)} %convert_element_type.34.refs_1_, f32[3,16,16,128]{3,2,1,0:T(8,128)S(1)} %convert_element_type.35.refs_2_), custom_call_target="tpu_custom_call" | custom-call | flops 1 | bytes 1 | tf_op jit(solution)/shard_map/pallas_call | solution.py:220
  27.9 0.9 %collective-permute-done.6.far_f = bf16[16,16,128]{2,1,0:T(8,128)(2,1)S(1)} collective-permute-done((bf16[16,16,128]{2,1,0:T(8,128)(2,1)S(1)}, bf16[16,16,128]{2,1,0:T(8,128)(2,1)S(1)}, u32[]{:S(2)}, u32[]{:S(2)}) %collective-permute-start.6) | collective-permute-done | bytes 65568 | tf_op jit(solution)/shard_map/ppermute | solution.py:329
  28.8 0.0 collective-permute-done.5.near_f
  28.8 4.5 %shard_map.91 = f32[16,2048]{1,0:T(8,128)} custom-call(f32[16,16,128]{2,1,0:T(8,128)S(1)} %get-tuple-element.12.own_f, bf16[16,16,128]{2,1,0:T(8,128)(2,1)S(1)} %collective-permute-done.5.near_f, bf16[16,16,128]{2,1,0:T(8,128)(2,1)S(1)} %collective-permute-done.6.far_f, f32[20,64,128]{2,1,0:T(8,128)S(1)} %get-tuple-element.14.h_in, ...), custom_call_target="tpu_custom_call" | custom-call | tf_op jit(solution)/shard_map/pallas_call | solution.py:309
  33.3 0.0 copy-done
  (5 shorter events, 0.1 us)
Async XLA Ops:
  3.0 6.9 %copy-start.1 = (f32[16,2048]{1,0:T(8,128)S(1)}, f32[16,2048]{1,0:T(8,128)}, u32[]{:S(2)}) copy-start(f32[16,2048]{1,0:T(8,128)} %refs_0_) | copy-start | bytes 393220
  3.0 6.9 %copy-start.2 = (f32[16,2048]{1,0:T(8,128)S(1)}, f32[16,2048]{1,0:T(8,128)}, u32[]{:S(2)}) copy-start(f32[16,2048]{1,0:T(8,128)} %refs_1_.1) | copy-start | bytes 393220
  3.1 6.9 %copy-start.3 = (f32[16,2048]{1,0:T(8,128)S(1)}, f32[16,2048]{1,0:T(8,128)}, u32[]{:S(2)}) copy-start(f32[16,2048]{1,0:T(8,128)} %refs_2_.5) | copy-start | bytes 393220
  3.1 19.8 %copy-start.4 = (f32[16,2048]{1,0:T(8,128)S(1)}, f32[16,2048]{1,0:T(8,128)}, u32[]{:S(2)}) copy-start(f32[16,2048]{1,0:T(8,128)} %param.10) | copy-start | bytes 393220
  3.1 2.6 %collective-permute-start = (bf16[8,16,2048]{2,1,0:T(8,128)(2,1)S(1)}, bf16[8,16,2048]{2,1,0:T(8,128)(2,1)S(1)}, u32[]{:S(2)}, u32[]{:S(2)}) collective-permute-start(bf16[8,16,2048]{2,1,0:T(8,128)(2,1)S(1)} %shard_map.87), channel_id=1, source_target_pairs={{0,1},{1,0},{2,3},{3,2},{4,5},{5,4},{6,7},{7,6},{8,9},{9,8},{10,11... | collective-permute-start | bytes 1572872 | tf_op jit(solution)/shard_map/ppermute | solution.py:325
  5.9 7.4 %collective-permute-start.1 = (f16[2,16,2048]{2,1,0:T(8,128)(2,1)S(1)}, f16[2,16,2048]{2,1,0:T(8,128)(2,1)S(1)}, u32[]{:S(2)}, u32[]{:S(2)}) collective-permute-start(f16[2,16,2048]{2,1,0:T(8,128)(2,1)S(1)} %get-tuple-element.20), channel_id=1, source_target_pairs={{0,6},{1,7},{2,4},{3,5},{4,2},{5,3},{6,0},{7,1},{8,14},{9,15},{10,... | collective-permute-start | bytes 393224 | tf_op jit(solution)/shard_map/ppermute | solution.py:325
  9.6 6.8 %collective-permute-start.3 = (f16[2,16,2048]{2,1,0:T(8,128)(2,1)S(1)}, f16[2,16,2048]{2,1,0:T(8,128)(2,1)S(1)}, u32[]{:S(2)}, u32[]{:S(2)}) collective-permute-start(f16[2,16,2048]{2,1,0:T(8,128)(2,1)S(1)} %get-tuple-element.21), channel_id=1, source_target_pairs={{0,2},{1,3},{2,0},{3,1},{4,6},{5,7},{6,4},{7,5},{8,10},{9,11},{10,... | collective-permute-start | bytes 393224 | tf_op jit(solution)/shard_map/ppermute | solution.py:325
  9.8 6.6 %collective-permute-start.2 = (f16[2,16,2048]{2,1,0:T(8,128)(2,1)S(1)}, f16[2,16,2048]{2,1,0:T(8,128)(2,1)S(1)}, u32[]{:S(2)}, u32[]{:S(2)}) collective-permute-start(f16[2,16,2048]{2,1,0:T(8,128)(2,1)S(1)} %get-tuple-element.22), channel_id=1, source_target_pairs={{0,4},{1,5},{2,6},{3,7},{4,0},{5,1},{6,2},{7,3},{8,12},{9,13},{10,... | collective-permute-start | bytes 393224 | tf_op jit(solution)/shard_map/ppermute | solution.py:325
  16.5 6.4 %collective-permute-start.4 = (f16[1,16,2048]{2,1,0:T(8,128)(2,1)S(1)}, f16[1,16,2048]{2,1,0:T(8,128)(2,1)S(1)}, u32[]{:S(2)}, u32[]{:S(2)}) collective-permute-start(f16[1,16,2048]{2,1,0:T(8,128)(2,1)S(1)} %slice_convert_fusion), channel_id=1, source_target_pairs={{0,8},{1,9},{2,10},{3,11},{4,12},{5,13},{6,14},{7,15},{8,0},{9,1},... | collective-permute-start | bytes 196616 | tf_op jit(solution)/shard_map/ppermute | solution.py:325
  18.9 8.5 %collective-permute-start.8 = (f16[3,16,16,128]{3,2,1,0:T(8,128)(2,1)S(1)}, f16[3,16,16,128]{3,2,1,0:T(8,128)(2,1)S(1)}, u32[]{:S(2)}, u32[]{:S(2)}) collective-permute-start(f16[3,16,16,128]{3,2,1,0:T(8,128)(2,1)S(1)} %convert_element_type.32), channel_id=1, source_target_pairs={{1,2},{3,4},{5,6},{7,8},{9,10},{11,12},{13,14},{2,1},{4,3},{6,5},{... | collective-permute-start | bytes 589832 | tf_op jit(solution)/shard_map/ppermute | solution.py:329
  22.7 4.7 %collective-permute-start.7 = (f16[3,16,16,128]{3,2,1,0:T(8,128)(2,1)S(1)}, f16[3,16,16,128]{3,2,1,0:T(8,128)(2,1)S(1)}, u32[]{:S(2)}, u32[]{:S(2)}) collective-permute-start(f16[3,16,16,128]{3,2,1,0:T(8,128)(2,1)S(1)} %convert_element_type.32), channel_id=1, source_target_pairs={{0,1},{1,0},{2,3},{3,2},{4,5},{5,4},{6,7},{7,6},{8,9},{9,8},{10,11... | collective-permute-start | bytes 589832 | tf_op jit(solution)/shard_map/ppermute | solution.py:325
  22.9 10.4 %copy-start = (f32[16,2048]{1,0:T(8,128)}, f32[16,2048]{1,0:T(8,128)S(1)}, u32[]{:S(2)}) copy-start(f32[16,2048]{1,0:T(8,128)S(1)} %bitcast_add_fusion.friction) | copy-start | bytes 393220
  23.2 5.6 %collective-permute-start.6 = (bf16[16,16,128]{2,1,0:T(8,128)(2,1)S(1)}, bf16[16,16,128]{2,1,0:T(8,128)(2,1)S(1)}, u32[]{:S(2)}, u32[]{:S(2)}) collective-permute-start(bf16[16,16,128]{2,1,0:T(8,128)(2,1)S(1)} %get-tuple-element.13), channel_id=1, source_target_pairs={{1,2},{3,4},{5,6},{7,8},{9,10},{11,12},{13,14},{2,1},{4,3},{6,5},{... | collective-permute-start | bytes 196616 | tf_op jit(solution)/shard_map/ppermute | solution.py:329
  26.8 2.0 %collective-permute-start.5 = (bf16[16,16,128]{2,1,0:T(8,128)(2,1)S(1)}, bf16[16,16,128]{2,1,0:T(8,128)(2,1)S(1)}, u32[]{:S(2)}, u32[]{:S(2)}) collective-permute-start(bf16[16,16,128]{2,1,0:T(8,128)(2,1)S(1)} %get-tuple-element.13), channel_id=1, source_target_pairs={{0,1},{1,0},{2,3},{3,2},{4,5},{5,4},{6,7},{7,6},{8,9},{9,8},{10,11... | collective-permute-start | bytes 196616 | tf_op jit(solution)/shard_map/ppermute | solution.py:325

commit v3 on v2

--- a/solution.py
+++ b/solution.py
@@ -84,13 +84,22 @@
     )(friction)
 
 
+def direct(strips):
+    return min(strips, 4)
+
+
+def pair_at(i, strips):
+    together = strips // direct(strips)
+    return (i % together) * direct(strips) + i // together
+
+
 def weigh(own, coeff_ref, eigen_ref, fields, out, held, given, sems):
     strips, modes, rows, columns = held.shape
     me = lax.axis_index("modes")
     parity = me % 2 if own else 1 - me % 2
 
     def copy(p):
-        row = (((me // 2) ^ p) * 2 + parity) * rows
+        row = (((me // 2) ^ pair_at(p, strips)) * 2 + parity) * rows
         return pltpu.make_async_copy(
             fields.at[:, pl.ds(pl.multiple_of(row, rows), rows), :], held.at[p], sems.at[p]
         )
@@ -186,7 +195,7 @@
     return pl.ds(PAD + reach, rows), pl.ds(near, reach), pl.ds(far, reach)
 
 
-def settle(peers, own_s, near_s, far_s, h0, s0, bed, bal):
+def settle(peers, own_s, near_s, far_s, h0, s0, bed, bal, square, steep):
     _, blocks, rows, _ = own_s.shape
     reach = 2 * STEPS
     me = lax.axis_index("modes")
@@ -208,6 +217,21 @@
     wrap_slots(s0, whole, blocks, 2)
     wrap_slots(bed, whole, blocks, 1)
     wrap_slots(h0, whole, blocks, 1)
+    zero = jnp.minimum(me, 0)
+    up, down = (pl.ds(PAD + off + zero, rows + 2 * reach) for off in (-1, 1))
+
+    def flux(i, carry):
+        for q in range((blocks + 2) // 2):
+            j = 1 + i * ((blocks + 2) // 2) + q
+            gx = s0[j, down, :] - s0[j, up, :]
+            gy = s0[j + 1, whole, :] - s0[j - 1, whole, :]
+            thick = h0[j, whole, :]
+            squared = thick * thick
+            square[j, whole, :] = squared
+            steep[j, whole, :] = squared * (squared * thick * (gx * gx + gy * gy))
+        return carry
+
+    lax.fori_loop(0, 2, flux, 0)
 
 
 def settled(peers, own_s, near_s, far_s):
@@ -219,13 +243,13 @@
 
     return pl.pallas_call(
         kernel,
-        out_shape=[jax.ShapeDtypeStruct(shape, jnp.float32)] * 4,
+        out_shape=[jax.ShapeDtypeStruct(shape, jnp.float32)] * 6,
         compiler_params=pltpu.CompilerParams(vmem_limit_bytes=8 << 20),
         cost_estimate=pl.CostEstimate(flops=1, bytes_accessed=1, transcendentals=0),
     )(own_s, near_s, far_s)
 
 
-def ice(own_f, near_f, far_f, h_in, s_in, bed, bal, out, h0, s0, h1, s1, slide, diff):
+def ice(own_f, near_f, far_f, h_in, s_in, bed, bal, square, steep, out, h0, s0, h1, s1, slide, diff):
     blocks, rows, _ = own_f.shape
     reach = 2 * STEPS
     extent = rows + 2 * reach
@@ -251,19 +275,19 @@
 
         up, at, down = window(edge - 1)
 
-        def diffuse(i, carry, h=h, s=s, at=at, up=up, down=down):
-            for q in range(span):
-                j = 1 + i * span + q
+        def diffuse(h=h, s=s, at=at, up=up, down=down, step=step):
+            for j in range(1, blocks + 3):
+                if step == 0:
+                    diff[j, at, :] = jnp.minimum(steep[j, at, :] + square[j, at, :] * slide[j, at, :], cap_unit)
+                    continue
                 gx = s[j, down, :] - s[j, up, :]
                 gy = s[j + 1, at, :] - s[j - 1, at, :]
                 thick = h[j, at, :]
                 squared = thick * thick
                 value = squared * (squared * thick * (gx * gx + gy * gy) + slide[j, at, :])
                 diff[j, at, :] = jnp.minimum(value, cap_unit)
-            return carry
-
-        span = (blocks + 2) // 2
-        lax.fori_loop(0, 2, diffuse, 0)
+
+        diffuse()
         up, at, down = window(edge)
 
         def flow(i, carry, h=h, s=s, hn=hn, sn=sn, at=at, up=up, down=down, final=final):
@@ -300,7 +324,7 @@
             out[at, k * LANES : (k + 1) * LANES] = part
         return carry
 
-    lax.fori_loop(0, rows // 8, tile, 0)
+    lax.fori_loop(0, rows // 8, tile, 0, unroll=2)
 
 
 def march(own_f, near_f, far_f, *state):
@@ -333,14 +357,19 @@
     )
     given = shares(coeff, eigen, mode_fields, rows, False, jnp.bfloat16)
     kept = shares(coeff, eigen, mode_fields, rows, True, jnp.float32)
-    total = kept + swap(given, 1).astype(jnp.float32)
-    strips = total.shape[0]
-    inner = min(strips, 4)
-    taken = total[::inner]
-    for part in [swap(total[k::inner].astype(jnp.float16), 2 * k) for k in reversed(range(1, inner))]:
+    arrived = swap(given, 1)
+    strips = kept.shape[0]
+    inner = direct(strips)
+
+    def summed(k):
+        at = slice(k * (strips // inner), (k + 1) * (strips // inner))
+        return kept[at] + arrived[at].astype(jnp.float32)
+
+    taken = summed(0)
+    for part in [swap(summed(k).astype(jnp.float16), 2 * k) for k in reversed(range(1, inner))]:
         taken = taken + part.astype(jnp.float32)
 
-    thickness, total = lax.optimization_barrier((thickness, total))
+    thickness, arrived = lax.optimization_barrier((thickness, arrived))
     statics = folded(thickness, bed, smb)
     sent = statics.astype(jnp.float16)
     far_s, near_s = across(sent).astype(jnp.float32), swap(sent, 1).astype(jnp.float32)

time: 33.6 us -> 32.8 us (0.976)
  Pallas kernels: 10.7 us -> 10.1 us
    pallas_call x1, Pallas kernels: 4.47 us -> 3.64 us  [march(): pl.pallas_call(ice, out_shape=jax.ShapeDtypeStruct((rows, blocks * LANES)...]
  transfers between devices with their start and end apart: 9 -> 9, of which waited for: 4 -> 4; matrix products, arithmetic and copies ran while one was open for 0% -> 0% of each run, Pallas kernels for 11% -> 12%
where the time goes in v3:
time: 32.8 us; the launch traced here: 32.5 us
  starting transfers between devices  14.2 us (43%)
  Pallas kernels  10.1 us (31%)
  waiting for transfers between devices  6.99 us (21%)
  between operations  0.82 us (2%)
    ppermute x2, starting transfers between devices, across(): return lax.ppermute(value, 'modes', pairs + [(j, i) for i, j in pairs])  7.39 us
    ppermute x7, starting transfers between devices, swap(): return lax.ppermute(value, 'modes', [(i, i ^ mask) for i in range(peers)])  6.86 us
    ppermute x7, waiting for transfers between devices, swap(): return lax.ppermute(value, 'modes', [(i, i ^ mask) for i in range(peers)])  5.71 us
    pallas_call x2, Pallas kernels, shares(): pl.pallas_call(kernel, in_specs=[pl.BlockSpec(memory_space=pltpu.HBM)] *...  4.92 us
    pallas_call x1, Pallas kernels, march(): pl.pallas_call(ice, out_shape=jax.ShapeDtypeStruct((rows, blocks * LANES)...  3.64 us
    ppermute x2, waiting for transfers between devices, across(): return lax.ppermute(value, 'modes', pairs + [(j, i) for i, j in pairs])  1.28 us
    pallas_call x1, Pallas kernels, folded(): pl.pallas_call(fold_all, out_shape=jax.ShapeDtypeStruct(shape, jnp.float3...  0.67 us
  transfers between devices with their start and end apart: 9, of which 4 were waited for; matrix products, arithmetic and copies ran while one was open for 0% of the time, Pallas kernels for 12%

profile of v3, /device:TPU:1, one launch (start us, length us, event | category | flops | bytes accessed | tf_op | source)
XLA Modules:
  0.0 32.5 jit_solution(16589625922016496700)
XLA Ops:
  0.6 0.0 copy-start.1
  0.6 0.0 copy-start.2
  0.7 0.0 copy-start.3
  0.7 2.5 %shard_map.87 = bf16[8,16,2048]{2,1,0:T(8,128)(2,1)S(1)} custom-call(f32[1,128]{1,0:T(1,128)} %bitcast.4, f32[1,128]{1,0:T(1,128)} %bitcast.6, bf16[8,256,2048]{2,1,0:T(8,128)(2,1)} %refs_2_.4), custom_call_target="tpu_custom_call" | custom-call | flops 4194304 | bytes 4194304 | tf_op jit(solution)/shard_map/pallas_call | solution.py:149
  3.2 0.0 copy-start.4
  3.2 0.1 collective-permute-start
  3.3 2.4 %shard_map.86 = f32[8,16,2048]{2,1,0:T(8,128)S(1)} custom-call(f32[1,128]{1,0:T(1,128)} %bitcast.5, f32[1,128]{1,0:T(1,128)} %bitcast.7, bf16[8,256,2048]{2,1,0:T(8,128)(2,1)} %refs_2_.4), custom_call_target="tpu_custom_call" | custom-call | flops 4194304 | bytes 4194304 | tf_op jit(solution)/shard_map/pallas_call | solution.py:149
  5.7 0.0 collective-permute-done
  5.7 0.1 fusion.2
  5.8 3.7 %collective-permute-start.1 = (f16[2,16,2048]{2,1,0:T(8,128)(2,1)S(1)}, f16[2,16,2048]{2,1,0:T(8,128)(2,1)S(1)}, u32[]{:S(2)}, u32[]{:S(2)}) collective-permute-start(f16[2,16,2048]{2,1,0:T(8,128)(2,1)S(1)} %get-tuple-element.22), channel_id=1, source_target_pairs={{0,6},{1,7},{2,4},{3,5},{4,2},{5,3},{6,0},{7,1},{8,14},{9,15},{10,... | collective-permute-start | bytes 393224 | tf_op jit(solution)/shard_map/ppermute | solution.py:349
  9.6 0.2 collective-permute-start.3
  9.8 0.1 collective-permute-start.2
  10.0 0.0 copy-done.1
  10.0 0.0 copy-done.2
  10.0 0.0 copy-done.3
  10.0 0.7 %shard_map.88.refs_0_ = f32[3,16,16,128]{3,2,1,0:T(8,128)S(1)} custom-call(f32[16,2048]{1,0:T(8,128)S(1)} %copy-done.1, f32[16,2048]{1,0:T(8,128)S(1)} %copy-done.2, f32[16,2048]{1,0:T(8,128)S(1)} %copy-done.3), custom_call_target="tpu_custom_call" | custom-call | flops 4194304 | bytes 4194304 | tf_op jit(solution)/shard_map/pallas_call | solution.py:61
  10.7 2.7 %collective-permute-done.1 = f16[2,16,2048]{2,1,0:T(8,128)(2,1)S(1)} collective-permute-done((f16[2,16,2048]{2,1,0:T(8,128)(2,1)S(1)}, f16[2,16,2048]{2,1,0:T(8,128)(2,1)S(1)}, u32[]{:S(2)}, u32[]{:S(2)}) %collective-permute-start.1) | collective-permute-done | bytes 131104 | tf_op jit(solution)/shard_map/ppermute | solution.py:349
  13.4 3.0 %collective-permute-done.3 = f16[2,16,2048]{2,1,0:T(8,128)(2,1)S(1)} collective-permute-done((f16[2,16,2048]{2,1,0:T(8,128)(2,1)S(1)}, f16[2,16,2048]{2,1,0:T(8,128)(2,1)S(1)}, u32[]{:S(2)}, u32[]{:S(2)}) %collective-permute-start.3) | collective-permute-done | bytes 131104 | tf_op jit(solution)/shard_map/ppermute | solution.py:349
  16.4 0.0 collective-permute-done.2
  16.4 0.1 fusion.5
  16.5 2.5 %collective-permute-start.4 = (f16[1,16,2048]{2,1,0:T(8,128)(2,1)S(1)}, f16[1,16,2048]{2,1,0:T(8,128)(2,1)S(1)}, u32[]{:S(2)}, u32[]{:S(2)}) collective-permute-start(f16[1,16,2048]{2,1,0:T(8,128)(2,1)S(1)} %slice_convert_fusion), channel_id=1, source_target_pairs={{0,8},{1,9},{2,10},{3,11},{4,12},{5,13},{6,14},{7,15},{8,0},{9,1},... | collective-permute-start | bytes 196616 | tf_op jit(solution)/shard_map/ppermute | solution.py:349
  19.0 3.8 %collective-permute-start.8 = (f16[3,16,16,128]{3,2,1,0:T(8,128)(2,1)S(1)}, f16[3,16,16,128]{3,2,1,0:T(8,128)(2,1)S(1)}, u32[]{:S(2)}, u32[]{:S(2)}) collective-permute-start(f16[3,16,16,128]{3,2,1,0:T(8,128)(2,1)S(1)} %convert_element_type.53), channel_id=1, source_target_pairs={{1,2},{3,4},{5,6},{7,8},{9,10},{11,12},{13,14},{2,1},{4,3},{6,5},{... | collective-permute-start | bytes 589832 | tf_op jit(solution)/shard_map/ppermute | solution.py:353
  22.8 0.1 collective-permute-start.7
  22.8 0.0 collective-permute-done.4
  22.8 0.0 copy-done.4
  22.9 0.0 copy-start
  22.9 0.3 %shard_map.89 = (f32[16,16,128]{2,1,0:T(8,128)S(1)}, bf16[16,16,128]{2,1,0:T(8,128)(2,1)S(1)}) custom-call(f32[16,2048]{1,0:T(8,128)S(1)} %bitcast_add_fusion.friction), custom_call_target="tpu_custom_call" | custom-call | tf_op jit(solution)/shard_map/pallas_call | solution.py:80
  23.2 3.6 %collective-permute-start.6 = (bf16[16,16,128]{2,1,0:T(8,128)(2,1)S(1)}, bf16[16,16,128]{2,1,0:T(8,128)(2,1)S(1)}, u32[]{:S(2)}, u32[]{:S(2)}) collective-permute-start(bf16[16,16,128]{2,1,0:T(8,128)(2,1)S(1)} %get-tuple-element.15), channel_id=1, source_target_pairs={{1,2},{3,4},{5,6},{7,8},{9,10},{11,12},{13,14},{2,1},{4,3},{6,5},{... | collective-permute-start | bytes 196616 | tf_op jit(solution)/shard_map/ppermute | solution.py:353
  26.9 0.1 collective-permute-start.5
  26.9 0.5 %collective-permute-done.8 = f16[3,16,16,128]{3,2,1,0:T(8,128)(2,1)S(1)} collective-permute-done((f16[3,16,16,128]{3,2,1,0:T(8,128)(2,1)S(1)}, f16[3,16,16,128]{3,2,1,0:T(8,128)(2,1)S(1)}, u32[]{:S(2)}, u32[]{:S(2)}) %collective-permute-start.8) | collective-permute-done | bytes 196640 | tf_op jit(solution)/shard_map/ppermute | solution.py:353
  27.5 0.0 collective-permute-done.7
  27.5 0.5 %shard_map.90 = (f32[20,64,128]{2,1,0:T(8,128)S(1)}, f32[20,64,128]{2,1,0:T(8,128)S(1)}, f32[20,64,128]{2,1,0:T(8,128)S(1)}, f32[20,64,128]{2,1,0:T(8,128)S(1)},...) custom-call(f32[3,16,16,128]{3,2,1,0:T(8,128)S(1)} %shard_map.88.refs_0_, ...), custom_call_target="tpu_custom_call" | custom-call | flops 1 | bytes 1 | tf_op jit(solution)/shard_map/pallas_call | solution.py:244
  28.1 0.8 %collective-permute-done.6.far_f = bf16[16,16,128]{2,1,0:T(8,128)(2,1)S(1)} collective-permute-done((bf16[16,16,128]{2,1,0:T(8,128)(2,1)S(1)}, bf16[16,16,128]{2,1,0:T(8,128)(2,1)S(1)}, u32[]{:S(2)}, u32[]{:S(2)}) %collective-permute-start.6) | collective-permute-done | bytes 65568 | tf_op jit(solution)/shard_map/ppermute | solution.py:353
  28.8 0.0 collective-permute-done.5.near_f
  28.8 3.6 %shard_map.91 = f32[16,2048]{1,0:T(8,128)} custom-call(f32[16,16,128]{2,1,0:T(8,128)S(1)} %get-tuple-element.14.own_f, bf16[16,16,128]{2,1,0:T(8,128)(2,1)S(1)} %collective-permute-done.5.near_f, bf16[16,16,128]{2,1,0:T(8,128)(2,1)S(1)} %collective-permute-done.6.far_f, f32[20,64,128]{2,1,0:T(8,128)S(1)} %get-tuple-element.16.h_in, ...), custom_call_target="tpu_custom_call" | custom-call | tf_op jit(solution)/shard_map/pallas_call | solution.py:333
  32.5 0.0 copy-done
  (5 shorter events, 0.1 us)
Async XLA Ops:
  0.6 9.3 %copy-start.1 = (f32[16,2048]{1,0:T(8,128)S(1)}, f32[16,2048]{1,0:T(8,128)}, u32[]{:S(2)}) copy-start(f32[16,2048]{1,0:T(8,128)} %refs_0_) | copy-start | bytes 393220
  0.6 9.3 %copy-start.2 = (f32[16,2048]{1,0:T(8,128)S(1)}, f32[16,2048]{1,0:T(8,128)}, u32[]{:S(2)}) copy-start(f32[16,2048]{1,0:T(8,128)} %refs_1_.1) | copy-start | bytes 393220
  0.7 9.3 %copy-start.3 = (f32[16,2048]{1,0:T(8,128)S(1)}, f32[16,2048]{1,0:T(8,128)}, u32[]{:S(2)}) copy-start(f32[16,2048]{1,0:T(8,128)} %refs_2_.5) | copy-start | bytes 393220
  3.2 19.6 %copy-start.4 = (f32[16,2048]{1,0:T(8,128)S(1)}, f32[16,2048]{1,0:T(8,128)}, u32[]{:S(2)}) copy-start(f32[16,2048]{1,0:T(8,128)} %param.10) | copy-start | bytes 393220
  3.2 2.5 %collective-permute-start = (bf16[8,16,2048]{2,1,0:T(8,128)(2,1)S(1)}, bf16[8,16,2048]{2,1,0:T(8,128)(2,1)S(1)}, u32[]{:S(2)}, u32[]{:S(2)}) collective-permute-start(bf16[8,16,2048]{2,1,0:T(8,128)(2,1)S(1)} %shard_map.87), channel_id=1, source_target_pairs={{0,1},{1,0},{2,3},{3,2},{4,5},{5,4},{6,7},{7,6},{8,9},{9,8},{10,11... | collective-permute-start | bytes 1572872 | tf_op jit(solution)/shard_map/ppermute | solution.py:349
  5.8 7.6 %collective-permute-start.1 = (f16[2,16,2048]{2,1,0:T(8,128)(2,1)S(1)}, f16[2,16,2048]{2,1,0:T(8,128)(2,1)S(1)}, u32[]{:S(2)}, u32[]{:S(2)}) collective-permute-start(f16[2,16,2048]{2,1,0:T(8,128)(2,1)S(1)} %get-tuple-element.22), channel_id=1, source_target_pairs={{0,6},{1,7},{2,4},{3,5},{4,2},{5,3},{6,0},{7,1},{8,14},{9,15},{10,... | collective-permute-start | bytes 393224 | tf_op jit(solution)/shard_map/ppermute | solution.py:349
  9.6 6.8 %collective-permute-start.3 = (f16[2,16,2048]{2,1,0:T(8,128)(2,1)S(1)}, f16[2,16,2048]{2,1,0:T(8,128)(2,1)S(1)}, u32[]{:S(2)}, u32[]{:S(2)}) collective-permute-start(f16[2,16,2048]{2,1,0:T(8,128)(2,1)S(1)} %get-tuple-element.23), channel_id=1, source_target_pairs={{0,2},{1,3},{2,0},{3,1},{4,6},{5,7},{6,4},{7,5},{8,10},{9,11},{10,... | collective-permute-start | bytes 393224 | tf_op jit(solution)/shard_map/ppermute | solution.py:349
  9.8 6.6 %collective-permute-start.2 = (f16[2,16,2048]{2,1,0:T(8,128)(2,1)S(1)}, f16[2,16,2048]{2,1,0:T(8,128)(2,1)S(1)}, u32[]{:S(2)}, u32[]{:S(2)}) collective-permute-start(f16[2,16,2048]{2,1,0:T(8,128)(2,1)S(1)} %get-tuple-element.24), channel_id=1, source_target_pairs={{0,4},{1,5},{2,6},{3,7},{4,0},{5,1},{6,2},{7,3},{8,12},{9,13},{10,... | collective-permute-start | bytes 393224 | tf_op jit(solution)/shard_map/ppermute | solution.py:349
  16.5 6.3 %collective-permute-start.4 = (f16[1,16,2048]{2,1,0:T(8,128)(2,1)S(1)}, f16[1,16,2048]{2,1,0:T(8,128)(2,1)S(1)}, u32[]{:S(2)}, u32[]{:S(2)}) collective-permute-start(f16[1,16,2048]{2,1,0:T(8,128)(2,1)S(1)} %slice_convert_fusion), channel_id=1, source_target_pairs={{0,8},{1,9},{2,10},{3,11},{4,12},{5,13},{6,14},{7,15},{8,0},{9,1},... | collective-permute-start | bytes 196616 | tf_op jit(solution)/shard_map/ppermute | solution.py:349
  19.0 8.5 %collective-permute-start.8 = (f16[3,16,16,128]{3,2,1,0:T(8,128)(2,1)S(1)}, f16[3,16,16,128]{3,2,1,0:T(8,128)(2,1)S(1)}, u32[]{:S(2)}, u32[]{:S(2)}) collective-permute-start(f16[3,16,16,128]{3,2,1,0:T(8,128)(2,1)S(1)} %convert_element_type.53), channel_id=1, source_target_pairs={{1,2},{3,4},{5,6},{7,8},{9,10},{11,12},{13,14},{2,1},{4,3},{6,5},{... | collective-permute-start | bytes 589832 | tf_op jit(solution)/shard_map/ppermute | solution.py:353
  22.8 4.7 %collective-permute-start.7 = (f16[3,16,16,128]{3,2,1,0:T(8,128)(2,1)S(1)}, f16[3,16,16,128]{3,2,1,0:T(8,128)(2,1)S(1)}, u32[]{:S(2)}, u32[]{:S(2)}) collective-permute-start(f16[3,16,16,128]{3,2,1,0:T(8,128)(2,1)S(1)} %convert_element_type.53), channel_id=1, source_target_pairs={{0,1},{1,0},{2,3},{3,2},{4,5},{5,4},{6,7},{7,6},{8,9},{9,8},{10,11... | collective-permute-start | bytes 589832 | tf_op jit(solution)/shard_map/ppermute | solution.py:349
  22.9 9.6 %copy-start = (f32[16,2048]{1,0:T(8,128)}, f32[16,2048]{1,0:T(8,128)S(1)}, u32[]{:S(2)}) copy-start(f32[16,2048]{1,0:T(8,128)S(1)} %bitcast_add_fusion.friction) | copy-start | bytes 393220
  23.2 5.6 %collective-permute-start.6 = (bf16[16,16,128]{2,1,0:T(8,128)(2,1)S(1)}, bf16[16,16,128]{2,1,0:T(8,128)(2,1)S(1)}, u32[]{:S(2)}, u32[]{:S(2)}) collective-permute-start(bf16[16,16,128]{2,1,0:T(8,128)(2,1)S(1)} %get-tuple-element.15), channel_id=1, source_target_pairs={{1,2},{3,4},{5,6},{7,8},{9,10},{11,12},{13,14},{2,1},{4,3},{6,5},{... | collective-permute-start | bytes 196616 | tf_op jit(solution)/shard_map/ppermute | solution.py:353
  26.9 2.0 %collective-permute-start.5 = (bf16[16,16,128]{2,1,0:T(8,128)(2,1)S(1)}, bf16[16,16,128]{2,1,0:T(8,128)(2,1)S(1)}, u32[]{:S(2)}, u32[]{:S(2)}) collective-permute-start(bf16[16,16,128]{2,1,0:T(8,128)(2,1)S(1)} %get-tuple-element.15), channel_id=1, source_target_pairs={{0,1},{1,0},{2,3},{3,2},{4,5},{5,4},{6,7},{7,6},{8,9},{9,8},{10,11... | collective-permute-start | bytes 196616 | tf_op jit(solution)/shard_map/ppermute | solution.py:349

commit v4 on v3

--- a/solution.py
+++ b/solution.py
@@ -88,9 +88,18 @@
     return min(strips, 4)
 
 
-def pair_at(i, strips):
+def partner(slot, odd):
+    other = slot if slot in (0, 3) else 3 - slot
+    return other if odd else slot
+
+
+def pair_at(i, strips, parity):
     together = strips // direct(strips)
-    return (i % together) * direct(strips) + i // together
+    slot = i // together
+    if direct(strips) == 4:
+        middle = jnp.logical_and(slot > 0, slot < 3)
+        slot = jnp.where(jnp.logical_and(middle, parity == 1), 3 - slot, slot)
+    return (i % together) * direct(strips) + slot
 
 
 def weigh(own, coeff_ref, eigen_ref, fields, out, held, given, sems):
@@ -99,7 +108,7 @@
     parity = me % 2 if own else 1 - me % 2
 
     def copy(p):
-        row = (((me // 2) ^ pair_at(p, strips)) * 2 + parity) * rows
+        row = (((me // 2) ^ pair_at(p, strips, parity)) * 2 + parity) * rows
         return pltpu.make_async_copy(
             fields.at[:, pl.ds(pl.multiple_of(row, rows), rows), :], held.at[p], sems.at[p]
         )
@@ -365,19 +374,29 @@
         at = slice(k * (strips // inner), (k + 1) * (strips // inner))
         return kept[at] + arrived[at].astype(jnp.float32)
 
-    taken = summed(0)
-    for part in [swap(summed(k).astype(jnp.float16), 2 * k) for k in reversed(range(1, inner))]:
-        taken = taken + part.astype(jnp.float32)
+    def exchanged(many):
+        found = summed(0)[many]
+        for k in (1, 2, 3) if inner == 4 else range(1, inner):
+            pairs = [(i, i ^ (2 * (partner(k, i % 2) if inner == 4 else k))) for i in range(peers)]
+            part = lax.ppermute(summed(k)[many].astype(jnp.float16), "modes", pairs)
+            found = found + part.astype(jnp.float32)
+        return found
+
+    together = strips // inner
+    half = together // 2
+    onward = exchanged(slice(half, together)) if half else None
+    taken = exchanged(slice(0, max(half, 1)))
 
     thickness, arrived = lax.optimization_barrier((thickness, arrived))
     statics = folded(thickness, bed, smb)
     sent = statics.astype(jnp.float16)
     far_s, near_s = across(sent).astype(jnp.float32), swap(sent, 1).astype(jnp.float32)
 
-    taken, sent = lax.optimization_barrier((taken, sent))
-    while taken.shape[0] > 1:
-        half = taken.shape[0] // 2
-        taken = taken[:half] + swap(taken[half:].astype(jnp.float16), 2 * inner * half).astype(jnp.float32)
+    onward, sent = lax.optimization_barrier((onward, sent))
+    while half:
+        taken = taken + swap(onward.astype(jnp.float16), 2 * inner * half).astype(jnp.float32)
+        half //= 2
+        taken, onward = taken[: max(half, 1)], taken[half:]
     log_friction = map_friction + taken[0]
     sliding, sent = slides(log_friction)
     far_f, near_f = across(sent), swap(sent, 1)

time: 32.8 us -> 31.3 us (0.954)
  waiting for transfers between devices: 6.99 us -> 2.5 us
  starting transfers between devices: 14.2 us -> 17.3 us
    ppermute x0 -> x6, starting transfers between devices: none -> 6.83 us  [exchanged(): part = lax.ppermute(summed(k)[many].astype(jnp.float16), 'modes', pairs)]
    ppermute x7 -> x4, waiting for transfers between devices: 5.71 us -> 0.01 us  [swap(): return lax.ppermute(value, 'modes', [(i, i ^ mask) for i in range(peers)])]
    ppermute x7 -> x4, starting transfers between devices: 6.86 us -> 2.64 us  [swap(): return lax.ppermute(value, 'modes', [(i, i ^ mask) for i in range(peers)])]
    ppermute x0 -> x6, waiting for transfers between devices: none -> 0.93 us  [exchanged(): part = lax.ppermute(summed(k)[many].astype(jnp.float16), 'modes', pairs)]
    ppermute x2, starting transfers between devices: 7.39 us -> 7.81 us  [across(): return lax.ppermute(value, 'modes', pairs + [(j, i) for i, j in pairs])]
  transfers between devices with their start and end apart: 9 -> 12, of which waited for: 4 -> 3; matrix products, arithmetic and copies ran while one was open for 0% -> 1% of each run, Pallas kernels for 12% -> 13%
where the time goes in v4:
time: 31.3 us; the launch traced here: 31.1 us
  starting transfers between devices  17.3 us (55%)
  Pallas kernels  10 us (32%)
  waiting for transfers between devices  2.5 us (8%)
  between operations  0.86 us (3%)
    ppermute x2, starting transfers between devices, across(): return lax.ppermute(value, 'modes', pairs + [(j, i) for i, j in pairs])  7.81 us
    ppermute x6, starting transfers between devices, exchanged(): part = lax.ppermute(summed(k)[many].astype(jnp.float16), 'modes', pairs)  6.83 us
    pallas_call x2, Pallas kernels, shares(): pl.pallas_call(kernel, in_specs=[pl.BlockSpec(memory_space=pltpu.HBM)] *...  4.86 us
    pallas_call x1, Pallas kernels, march(): pl.pallas_call(ice, out_shape=jax.ShapeDtypeStruct((rows, blocks * LANES)...  3.64 us
    ppermute x4, starting transfers between devices, swap(): return lax.ppermute(value, 'modes', [(i, i ^ mask) for i in range(peers)])  2.64 us
    ppermute x2, waiting for transfers between devices, across(): return lax.ppermute(value, 'modes', pairs + [(j, i) for i, j in pairs])  1.56 us
    ppermute x6, waiting for transfers between devices, exchanged(): part = lax.ppermute(summed(k)[many].astype(jnp.float16), 'modes', pairs)  0.93 us
    pallas_call x1, Pallas kernels, folded(): pl.pallas_call(fold_all, out_shape=jax.ShapeDtypeStruct(shape, jnp.float3...  0.67 us
  transfers between devices with their start and end apart: 12, of which 3 were waited for; matrix products, arithmetic and copies ran while one was open for 1% of the time, Pallas kernels for 13%

profile of v4, /device:TPU:1, one launch (start us, length us, event | category | flops | bytes accessed | tf_op | source)
XLA Modules:
  0.0 31.1 jit_solution(11708297618896069307)
XLA Ops:
  0.6 2.4 %shard_map.87 = bf16[8,16,2048]{2,1,0:T(8,128)(2,1)S(1)} custom-call(f32[1,128]{1,0:T(1,128)} %bitcast.6, f32[1,128]{1,0:T(1,128)} %bitcast.8, bf16[8,256,2048]{2,1,0:T(8,128)(2,1)} %refs_2_.4), custom_call_target="tpu_custom_call" | custom-call | flops 4194304 | bytes 4194304 | tf_op jit(solution)/shard_map/pallas_call | solution.py:158
  3.0 0.0 copy-start.1
  3.1 0.0 copy-start.2
  3.1 0.0 copy-start.3
  3.1 0.0 copy-start.4
  3.1 0.1 collective-permute-start
  3.2 2.5 %shard_map.86 = f32[8,16,2048]{2,1,0:T(8,128)S(1)} custom-call(f32[1,128]{1,0:T(1,128)} %bitcast.7, f32[1,128]{1,0:T(1,128)} %bitcast.9, bf16[8,256,2048]{2,1,0:T(8,128)(2,1)} %refs_2_.4), custom_call_target="tpu_custom_call" | custom-call | flops 4194304 | bytes 4194304 | tf_op jit(solution)/shard_map/pallas_call | solution.py:158
  5.7 0.0 collective-permute-done
  5.7 0.1 fusion.2
  5.8 2.7 %collective-permute-start.4 = (f16[1,16,2048]{2,1,0:T(8,128)(2,1)S(1)}, f16[1,16,2048]{2,1,0:T(8,128)(2,1)S(1)}, u32[]{:S(2)}, u32[]{:S(2)}) collective-permute-start(f16[1,16,2048]{2,1,0:T(8,128)(2,1)S(1)} %get-tuple-element.27), channel_id=1, source_target_pairs={{0,2},{1,5},{2,0},{3,7},{4,6},{5,1},{6,4},{7,3},{8,10},{9,13},{10,... | collective-permute-start | bytes 196616 | tf_op jit(solution)/shard_map/ppermute | solution.py:381
  8.6 1.2 %collective-permute-start.6 = (f16[1,16,2048]{2,1,0:T(8,128)(2,1)S(1)}, f16[1,16,2048]{2,1,0:T(8,128)(2,1)S(1)}, u32[]{:S(2)}, u32[]{:S(2)}) collective-permute-start(f16[1,16,2048]{2,1,0:T(8,128)(2,1)S(1)} %get-tuple-element.31), channel_id=1, source_target_pairs={{0,6},{1,7},{2,4},{3,5},{4,2},{5,3},{6,0},{7,1},{8,14},{9,15},{10,... | collective-permute-start | bytes 196616 | tf_op jit(solution)/shard_map/ppermute | solution.py:381
  9.8 0.2 collective-permute-start.5
  10.0 0.0 copy-done.1
  10.0 0.0 copy-done.2
  10.0 0.0 copy-done.3
  10.0 0.7 %shard_map.88.refs_0_ = f32[3,16,16,128]{3,2,1,0:T(8,128)S(1)} custom-call(f32[16,2048]{1,0:T(8,128)S(1)} %copy-done.1, f32[16,2048]{1,0:T(8,128)S(1)} %copy-done.2, f32[16,2048]{1,0:T(8,128)S(1)} %copy-done.3), custom_call_target="tpu_custom_call" | custom-call | flops 4194304 | bytes 4194304 | tf_op jit(solution)/shard_map/pallas_call | solution.py:61
  10.7 1.5 %collective-permute-start.1 = (f16[1,16,2048]{2,1,0:T(8,128)(2,1)S(1)}, f16[1,16,2048]{2,1,0:T(8,128)(2,1)S(1)}, u32[]{:S(2)}, u32[]{:S(2)}) collective-permute-start(f16[1,16,2048]{2,1,0:T(8,128)(2,1)S(1)} %get-tuple-element.26), channel_id=1, source_target_pairs={{0,2},{1,5},{2,0},{3,7},{4,6},{5,1},{6,4},{7,3},{8,10},{9,13},{10,... | collective-permute-start | bytes 196616 | tf_op jit(solution)/shard_map/ppermute | solution.py:381
  12.2 1.1 %collective-permute-start.3 = (f16[1,16,2048]{2,1,0:T(8,128)(2,1)S(1)}, f16[1,16,2048]{2,1,0:T(8,128)(2,1)S(1)}, u32[]{:S(2)}, u32[]{:S(2)}) collective-permute-start(f16[1,16,2048]{2,1,0:T(8,128)(2,1)S(1)} %get-tuple-element.30), channel_id=1, source_target_pairs={{0,6},{1,7},{2,4},{3,5},{4,2},{5,3},{6,0},{7,1},{8,14},{9,15},{10,... | collective-permute-start | bytes 196616 | tf_op jit(solution)/shard_map/ppermute | solution.py:381
  13.3 0.0 collective-permute-done.4
  13.3 0.1 collective-permute-start.2
  13.5 0.0 collective-permute-done.6
  13.5 0.9 %collective-permute-done.5 = f16[1,16,2048]{2,1,0:T(8,128)(2,1)S(1)} collective-permute-done((f16[1,16,2048]{2,1,0:T(8,128)(2,1)S(1)}, f16[1,16,2048]{2,1,0:T(8,128)(2,1)S(1)}, u32[]{:S(2)}, u32[]{:S(2)}) %collective-permute-start.5) | collective-permute-done | bytes 65568 | tf_op jit(solution)/shard_map/ppermute | solution.py:381
  14.4 2.4 %collective-permute-start.7 = (f16[1,16,2048]{2,1,0:T(8,128)(2,1)S(1)}, f16[1,16,2048]{2,1,0:T(8,128)(2,1)S(1)}, u32[]{:S(2)}, u32[]{:S(2)}) collective-permute-start(f16[1,16,2048]{2,1,0:T(8,128)(2,1)S(1)} %convert_element_type.66), channel_id=1, source_target_pairs={{0,8},{1,9},{2,10},{3,11},{4,12},{5,13},{6,14},{7,15},{8,0},{9,1},... | collective-permute-start | bytes 196616 | tf_op jit(solution)/shard_map/ppermute | solution.py:358
  16.8 4.5 %collective-permute-start.11 = (f16[3,16,16,128]{3,2,1,0:T(8,128)(2,1)S(1)}, f16[3,16,16,128]{3,2,1,0:T(8,128)(2,1)S(1)}, u32[]{:S(2)}, u32[]{:S(2)}) collective-permute-start(f16[3,16,16,128]{3,2,1,0:T(8,128)(2,1)S(1)} %convert_element_type.65), channel_id=1, source_target_pairs={{1,2},{3,4},{5,6},{7,8},{9,10},{11,12},{13,14},{2,1},{4,3},{6,5},{... | collective-permute-start | bytes 589832 | tf_op jit(solution)/shard_map/ppermute | solution.py:362
  21.3 0.0 collective-permute-done.1
  21.3 0.1 collective-permute-start.10
  21.4 0.0 collective-permute-done.3
  21.4 0.0 collective-permute-done.2
  21.4 0.0 collective-permute-done.7
  21.4 0.0 copy-done.4
  21.4 0.1 fusion.9.friction
  21.5 0.0 copy-start
  21.5 0.3 %shard_map.89 = (f32[16,16,128]{2,1,0:T(8,128)S(1)}, bf16[16,16,128]{2,1,0:T(8,128)(2,1)S(1)}) custom-call(f32[16,2048]{1,0:T(8,128)S(1)} %fusion.9.friction), custom_call_target="tpu_custom_call" | custom-call | tf_op jit(solution)/shard_map/pallas_call | solution.py:80
  21.8 3.3 %collective-permute-start.9 = (bf16[16,16,128]{2,1,0:T(8,128)(2,1)S(1)}, bf16[16,16,128]{2,1,0:T(8,128)(2,1)S(1)}, u32[]{:S(2)}, u32[]{:S(2)}) collective-permute-start(bf16[16,16,128]{2,1,0:T(8,128)(2,1)S(1)} %get-tuple-element.15), channel_id=1, source_target_pairs={{1,2},{3,4},{5,6},{7,8},{9,10},{11,12},{13,14},{2,1},{4,3},{6,5},{... | collective-permute-start | bytes 196616 | tf_op jit(solution)/shard_map/ppermute | solution.py:362
  25.2 0.1 collective-permute-start.8
  25.3 0.6 %collective-permute-done.11 = f16[3,16,16,128]{3,2,1,0:T(8,128)(2,1)S(1)} collective-permute-done((f16[3,16,16,128]{3,2,1,0:T(8,128)(2,1)S(1)}, f16[3,16,16,128]{3,2,1,0:T(8,128)(2,1)S(1)}, u32[]{:S(2)}, u32[]{:S(2)}) %collective-permute-start.11) | collective-permute-done | bytes 196640 | tf_op jit(solution)/shard_map/ppermute | solution.py:362
  25.9 0.0 collective-permute-done.10
  26.0 0.5 %shard_map.90 = (f32[20,64,128]{2,1,0:T(8,128)S(1)}, f32[20,64,128]{2,1,0:T(8,128)S(1)}, f32[20,64,128]{2,1,0:T(8,128)S(1)}, f32[20,64,128]{2,1,0:T(8,128)S(1)},...) custom-call(f32[3,16,16,128]{3,2,1,0:T(8,128)S(1)} %shard_map.88.refs_0_, ...), custom_call_target="tpu_custom_call" | custom-call | flops 1 | bytes 1 | tf_op jit(solution)/shard_map/pallas_call | solution.py:253
  26.5 0.9 %collective-permute-done.9.far_f = bf16[16,16,128]{2,1,0:T(8,128)(2,1)S(1)} collective-permute-done((bf16[16,16,128]{2,1,0:T(8,128)(2,1)S(1)}, bf16[16,16,128]{2,1,0:T(8,128)(2,1)S(1)}, u32[]{:S(2)}, u32[]{:S(2)}) %collective-permute-start.9) | collective-permute-done | bytes 65568 | tf_op jit(solution)/shard_map/ppermute | solution.py:362
  27.4 0.0 collective-permute-done.8.near_f
  27.4 3.6 %shard_map.91 = f32[16,2048]{1,0:T(8,128)} custom-call(f32[16,16,128]{2,1,0:T(8,128)S(1)} %get-tuple-element.14.own_f, bf16[16,16,128]{2,1,0:T(8,128)(2,1)S(1)} %collective-permute-done.8.near_f, bf16[16,16,128]{2,1,0:T(8,128)(2,1)S(1)} %collective-permute-done.9.far_f, f32[20,64,128]{2,1,0:T(8,128)S(1)} %get-tuple-element.16.h_in, ...), custom_call_target="tpu_custom_call" | custom-call | tf_op jit(solution)/shard_map/pallas_call | solution.py:342
  31.1 0.0 copy-done
  (8 shorter events, 0.2 us)
Async XLA Ops:
  3.0 7.0 %copy-start.1 = (f32[16,2048]{1,0:T(8,128)S(1)}, f32[16,2048]{1,0:T(8,128)}, u32[]{:S(2)}) copy-start(f32[16,2048]{1,0:T(8,128)} %refs_0_) | copy-start | bytes 393220
  3.1 7.0 %copy-start.2 = (f32[16,2048]{1,0:T(8,128)S(1)}, f32[16,2048]{1,0:T(8,128)}, u32[]{:S(2)}) copy-start(f32[16,2048]{1,0:T(8,128)} %refs_1_.1) | copy-start | bytes 393220
  3.1 7.0 %copy-start.3 = (f32[16,2048]{1,0:T(8,128)S(1)}, f32[16,2048]{1,0:T(8,128)}, u32[]{:S(2)}) copy-start(f32[16,2048]{1,0:T(8,128)} %refs_2_.5) | copy-start | bytes 393220
  3.1 18.3 %copy-start.4 = (f32[16,2048]{1,0:T(8,128)S(1)}, f32[16,2048]{1,0:T(8,128)}, u32[]{:S(2)}) copy-start(f32[16,2048]{1,0:T(8,128)} %param.10) | copy-start | bytes 393220
  3.1 2.6 %collective-permute-start = (bf16[8,16,2048]{2,1,0:T(8,128)(2,1)S(1)}, bf16[8,16,2048]{2,1,0:T(8,128)(2,1)S(1)}, u32[]{:S(2)}, u32[]{:S(2)}) collective-permute-start(bf16[8,16,2048]{2,1,0:T(8,128)(2,1)S(1)} %shard_map.87), channel_id=1, source_target_pairs={{0,1},{1,0},{2,3},{3,2},{4,5},{5,4},{6,7},{7,6},{8,9},{9,8},{10,11... | collective-permute-start | bytes 1572872 | tf_op jit(solution)/shard_map/ppermute | solution.py:358
  5.8 7.5 %collective-permute-start.4 = (f16[1,16,2048]{2,1,0:T(8,128)(2,1)S(1)}, f16[1,16,2048]{2,1,0:T(8,128)(2,1)S(1)}, u32[]{:S(2)}, u32[]{:S(2)}) collective-permute-start(f16[1,16,2048]{2,1,0:T(8,128)(2,1)S(1)} %get-tuple-element.27), channel_id=1, source_target_pairs={{0,2},{1,5},{2,0},{3,7},{4,6},{5,1},{6,4},{7,3},{8,10},{9,13},{10,... | collective-permute-start | bytes 196616 | tf_op jit(solution)/shard_map/ppermute | solution.py:381
  8.6 4.9 %collective-permute-start.6 = (f16[1,16,2048]{2,1,0:T(8,128)(2,1)S(1)}, f16[1,16,2048]{2,1,0:T(8,128)(2,1)S(1)}, u32[]{:S(2)}, u32[]{:S(2)}) collective-permute-start(f16[1,16,2048]{2,1,0:T(8,128)(2,1)S(1)} %get-tuple-element.31), channel_id=1, source_target_pairs={{0,6},{1,7},{2,4},{3,5},{4,2},{5,3},{6,0},{7,1},{8,14},{9,15},{10,... | collective-permute-start | bytes 196616 | tf_op jit(solution)/shard_map/ppermute | solution.py:381
  9.8 4.6 %collective-permute-start.5 = (f16[1,16,2048]{2,1,0:T(8,128)(2,1)S(1)}, f16[1,16,2048]{2,1,0:T(8,128)(2,1)S(1)}, u32[]{:S(2)}, u32[]{:S(2)}) collective-permute-start(f16[1,16,2048]{2,1,0:T(8,128)(2,1)S(1)} %get-tuple-element.29), channel_id=1, source_target_pairs={{0,4},{1,3},{2,6},{3,1},{4,0},{5,7},{6,2},{7,5},{8,12},{9,11},{10,... | collective-permute-start | bytes 196616 | tf_op jit(solution)/shard_map/ppermute | solution.py:381
  10.7 10.6 %collective-permute-start.1 = (f16[1,16,2048]{2,1,0:T(8,128)(2,1)S(1)}, f16[1,16,2048]{2,1,0:T(8,128)(2,1)S(1)}, u32[]{:S(2)}, u32[]{:S(2)}) collective-permute-start(f16[1,16,2048]{2,1,0:T(8,128)(2,1)S(1)} %get-tuple-element.26), channel_id=1, source_target_pairs={{0,2},{1,5},{2,0},{3,7},{4,6},{5,1},{6,4},{7,3},{8,10},{9,13},{10,... | collective-permute-start | bytes 196616 | tf_op jit(solution)/shard_map/ppermute | solution.py:381
  12.2 9.2 %collective-permute-start.3 = (f16[1,16,2048]{2,1,0:T(8,128)(2,1)S(1)}, f16[1,16,2048]{2,1,0:T(8,128)(2,1)S(1)}, u32[]{:S(2)}, u32[]{:S(2)}) collective-permute-start(f16[1,16,2048]{2,1,0:T(8,128)(2,1)S(1)} %get-tuple-element.30), channel_id=1, source_target_pairs={{0,6},{1,7},{2,4},{3,5},{4,2},{5,3},{6,0},{7,1},{8,14},{9,15},{10,... | collective-permute-start | bytes 196616 | tf_op jit(solution)/shard_map/ppermute | solution.py:381
  13.3 8.1 %collective-permute-start.2 = (f16[1,16,2048]{2,1,0:T(8,128)(2,1)S(1)}, f16[1,16,2048]{2,1,0:T(8,128)(2,1)S(1)}, u32[]{:S(2)}, u32[]{:S(2)}) collective-permute-start(f16[1,16,2048]{2,1,0:T(8,128)(2,1)S(1)} %get-tuple-element.28), channel_id=1, source_target_pairs={{0,4},{1,3},{2,6},{3,1},{4,0},{5,7},{6,2},{7,5},{8,12},{9,11},{10,... | collective-permute-start | bytes 196616 | tf_op jit(solution)/shard_map/ppermute | solution.py:381
  14.4 7.0 %collective-permute-start.7 = (f16[1,16,2048]{2,1,0:T(8,128)(2,1)S(1)}, f16[1,16,2048]{2,1,0:T(8,128)(2,1)S(1)}, u32[]{:S(2)}, u32[]{:S(2)}) collective-permute-start(f16[1,16,2048]{2,1,0:T(8,128)(2,1)S(1)} %convert_element_type.66), channel_id=1, source_target_pairs={{0,8},{1,9},{2,10},{3,11},{4,12},{5,13},{6,14},{7,15},{8,0},{9,1},... | collective-permute-start | bytes 196616 | tf_op jit(solution)/shard_map/ppermute | solution.py:358
  16.8 9.1 %collective-permute-start.11 = (f16[3,16,16,128]{3,2,1,0:T(8,128)(2,1)S(1)}, f16[3,16,16,128]{3,2,1,0:T(8,128)(2,1)S(1)}, u32[]{:S(2)}, u32[]{:S(2)}) collective-permute-start(f16[3,16,16,128]{3,2,1,0:T(8,128)(2,1)S(1)} %convert_element_type.65), channel_id=1, source_target_pairs={{1,2},{3,4},{5,6},{7,8},{9,10},{11,12},{13,14},{2,1},{4,3},{6,5},{... | collective-permute-start | bytes 589832 | tf_op jit(solution)/shard_map/ppermute | solution.py:362
  21.3 4.6 %collective-permute-start.10 = (f16[3,16,16,128]{3,2,1,0:T(8,128)(2,1)S(1)}, f16[3,16,16,128]{3,2,1,0:T(8,128)(2,1)S(1)}, u32[]{:S(2)}, u32[]{:S(2)}) collective-permute-start(f16[3,16,16,128]{3,2,1,0:T(8,128)(2,1)S(1)} %convert_element_type.65), channel_id=1, source_target_pairs={{0,1},{1,0},{2,3},{3,2},{4,5},{5,4},{6,7},{7,6},{8,9},{9,8},{10,11... | collective-permute-start | bytes 589832 | tf_op jit(solution)/shard_map/ppermute | solution.py:358
  21.5 9.6 %copy-start = (f32[16,2048]{1,0:T(8,128)}, f32[16,2048]{1,0:T(8,128)S(1)}, u32[]{:S(2)}) copy-start(f32[16,2048]{1,0:T(8,128)S(1)} %fusion.9.friction) | copy-start | bytes 393220
  21.8 5.6 %collective-permute-start.9 = (bf16[16,16,128]{2,1,0:T(8,128)(2,1)S(1)}, bf16[16,16,128]{2,1,0:T(8,128)(2,1)S(1)}, u32[]{:S(2)}, u32[]{:S(2)}) collective-permute-start(bf16[16,16,128]{2,1,0:T(8,128)(2,1)S(1)} %get-tuple-element.15), channel_id=1, source_target_pairs={{1,2},{3,4},{5,6},{7,8},{9,10},{11,12},{13,14},{2,1},{4,3},{6,5},{... | collective-permute-start | bytes 196616 | tf_op jit(solution)/shard_map/ppermute | solution.py:362
  25.2 2.3 %collective-permute-start.8 = (bf16[16,16,128]{2,1,0:T(8,128)(2,1)S(1)}, bf16[16,16,128]{2,1,0:T(8,128)(2,1)S(1)}, u32[]{:S(2)}, u32[]{:S(2)}) collective-permute-start(bf16[16,16,128]{2,1,0:T(8,128)(2,1)S(1)} %get-tuple-element.15), channel_id=1, source_target_pairs={{0,1},{1,0},{2,3},{3,2},{4,5},{5,4},{6,7},{7,6},{8,9},{9,8},{10,11... | collective-permute-start | bytes 196616 | tf_op jit(solution)/shard_map/ppermute | solution.py:358

commit v5 on v4

--- a/solution.py
+++ b/solution.py
@@ -55,17 +55,6 @@
     lax.fori_loop(0, rows // 8, tile, 0)
 
 
-def folded(*arrays):
-    rows, columns = arrays[0].shape
-    shape = (len(arrays), columns // LANES, rows, LANES)
-    return pl.pallas_call(
-        fold_all,
-        out_shape=jax.ShapeDtypeStruct(shape, jnp.float32),
-        compiler_params=pltpu.CompilerParams(vmem_limit_bytes=8 << 20),
-        cost_estimate=pl.CostEstimate(flops=4 << 20, bytes_accessed=4 << 20, transcendentals=0),
-    )(*arrays)
-
-
 def slide_fold(friction, wide, narrow):
     blocks, rows = wide.shape[0], wide.shape[1]
     parts = fold([slide_unit * jnp.exp(-part) for part in cut(friction, slice(0, rows), blocks)])
@@ -102,7 +91,8 @@
     return (i % together) * direct(strips) + slot
 
 
-def weigh(own, coeff_ref, eigen_ref, fields, out, held, given, sems):
+def weigh(own, coeff_ref, eigen_ref, fields, *refs):
+    out, held, given, sems = refs[-5:-4] + refs[-3:] if own else refs
     strips, modes, rows, columns = held.shape
     me = lax.axis_index("modes")
     parity = me % 2 if own else 1 - me % 2
@@ -125,6 +115,8 @@
         return carry
 
     lax.fori_loop(0, strips, begin, 0)
+    if own:
+        fold_all(*refs[:-5], refs[-4])
     for one in small:
         one.wait()
     weights = given[0] / jnp.sqrt(1.0 + given[1])
@@ -148,18 +140,23 @@
     lax.fori_loop(0, strips, strip, 0)
 
 
-def shares(coeff, eigen, mode_fields, rows, own, dtype):
+def shares(coeff, eigen, mode_fields, rows, own, dtype, *statics):
     modes, total_rows, columns = mode_fields.shape
     strips = total_rows // rows // 2
 
     def kernel(*refs):
         weigh(own, *refs)
 
+    vmem = pl.BlockSpec(memory_space=pltpu.VMEM)
+    shapes = [jax.ShapeDtypeStruct((strips, rows, columns), dtype)]
+    if own:
+        folded = (len(statics), columns // LANES, rows, LANES)
+        shapes.append(jax.ShapeDtypeStruct(folded, jnp.float32))
     return pl.pallas_call(
         kernel,
-        in_specs=[pl.BlockSpec(memory_space=pltpu.HBM)] * 3,
-        out_specs=pl.BlockSpec(memory_space=pltpu.VMEM),
-        out_shape=jax.ShapeDtypeStruct((strips, rows, columns), dtype),
+        in_specs=[pl.BlockSpec(memory_space=pltpu.HBM)] * 3 + [vmem] * len(statics),
+        out_specs=[vmem] * len(shapes),
+        out_shape=shapes,
         scratch_shapes=[
             pltpu.VMEM((strips, modes, rows, columns), jnp.bfloat16),
             pltpu.VMEM((2,) + coeff.shape, jnp.float32),
@@ -171,7 +168,7 @@
             bytes_accessed=modes * total_rows * columns,
             transcendentals=0,
         ),
-    )(coeff, eigen, mode_fields)
+    )(coeff, eigen, mode_fields, *statics)
 
 
 PAD = 8
@@ -364,8 +361,8 @@
     coeff, eigen, mode_fields = (
         pltpu.with_memory_space_constraint(x, pltpu.HBM) for x in (coeff[None], eigen[None], mode_fields)
     )
-    given = shares(coeff, eigen, mode_fields, rows, False, jnp.bfloat16)
-    kept = shares(coeff, eigen, mode_fields, rows, True, jnp.float32)
+    (given,) = shares(coeff, eigen, mode_fields, rows, False, jnp.bfloat16)
+    kept, statics = shares(coeff, eigen, mode_fields, rows, True, jnp.float32, thickness, bed, smb)
     arrived = swap(given, 1)
     strips = kept.shape[0]
     inner = direct(strips)
@@ -387,8 +384,6 @@
     onward = exchanged(slice(half, together)) if half else None
     taken = exchanged(slice(0, max(half, 1)))
 
-    thickness, arrived = lax.optimization_barrier((thickness, arrived))
-    statics = folded(thickness, bed, smb)
     sent = statics.astype(jnp.float16)
     far_s, near_s = across(sent).astype(jnp.float32), swap(sent, 1).astype(jnp.float32)
 

time: 31.3 us -> 31.1 us (level)
  waiting for transfers between devices: 2.5 us -> 4.41 us
  starting transfers between devices: 17.3 us -> 15.9 us
  Pallas kernels: 10 us -> 9.43 us
    ppermute x6, waiting for transfers between devices: 0.93 us -> 2.11 us  [exchanged(): part = lax.ppermute(summed(k)[many].astype(jnp.float16), 'modes', pairs)]
    ppermute x2, starting transfers between devices: 7.81 us -> 6.79 us  [across(): return lax.ppermute(value, 'modes', pairs + [(j, i) for i, j in pairs])]
    pallas_call x1 -> x0, Pallas kernels: 0.67 us -> none  [folded(): pl.pallas_call(fold_all, out_shape=jax.ShapeDtypeStruct(shape, jnp.float3...]
    ppermute x2, waiting for transfers between devices: 1.56 us -> 2.1 us  [across(): return lax.ppermute(value, 'modes', pairs + [(j, i) for i, j in pairs])]
    ppermute x4, starting transfers between devices: 2.64 us -> 2.2 us  [swap(): return lax.ppermute(value, 'modes', [(i, i ^ mask) for i in range(peers)])]
  transfers between devices with their start and end apart: 12 -> 12, of which waited for: 3 -> 4; matrix products, arithmetic and copies ran while one was open for 1% -> 1% of each run, Pallas kernels for 13% -> 11%
where the time goes in v5:
time: 31.1 us; the launch traced here: 31 us
  starting transfers between devices  15.9 us (51%)
  Pallas kernels  9.43 us (30%)
  waiting for transfers between devices  4.41 us (14%)
  between operations  0.84 us (3%)
    ppermute x6, starting transfers between devices, exchanged(): part = lax.ppermute(summed(k)[many].astype(jnp.float16), 'modes', pairs)  6.91 us
    ppermute x2, starting transfers between devices, across(): return lax.ppermute(value, 'modes', pairs + [(j, i) for i, j in pairs])  6.79 us
    pallas_call x2, Pallas kernels, shares(): pl.pallas_call(kernel, in_specs=[pl.BlockSpec(memory_space=pltpu.HBM)] *...  4.93 us
    pallas_call x1, Pallas kernels, march(): pl.pallas_call(ice, out_shape=jax.ShapeDtypeStruct((rows, blocks * LANES)...  3.64 us
    ppermute x4, starting transfers between devices, swap(): return lax.ppermute(value, 'modes', [(i, i ^ mask) for i in range(peers)])  2.2 us
    ppermute x6, waiting for transfers between devices, exchanged(): part = lax.ppermute(summed(k)[many].astype(jnp.float16), 'modes', pairs)  2.11 us
    ppermute x2, waiting for transfers between devices, across(): return lax.ppermute(value, 'modes', pairs + [(j, i) for i, j in pairs])  2.1 us
  transfers between devices with their start and end apart: 12, of which 4 were waited for; matrix products, arithmetic and copies ran while one was open for 1% of the time, Pallas kernels for 11%

profile of v5, /device:TPU:1, one launch (start us, length us, event | category | flops | bytes accessed | tf_op | source)
XLA Modules:
  0.0 31.0 jit_solution(7978892914726053405)
XLA Ops:
  0.6 0.0 copy-start.1
  0.6 0.0 copy-start.3
  0.7 0.0 copy-start.2
  0.7 2.5 %shard_map.87 = bf16[8,16,2048]{2,1,0:T(8,128)(2,1)S(1)} custom-call(f32[1,128]{1,0:T(1,128)} %bitcast.6, f32[1,128]{1,0:T(1,128)} %bitcast.8, bf16[8,256,2048]{2,1,0:T(8,128)(2,1)} %refs_2_.3), custom_call_target="tpu_custom_call" | custom-call | flops 4194304 | bytes 4194304 | tf_op jit(solution)/shard_map/pallas_call | solution.py:155
  3.2 0.0 copy-start.4
  3.2 0.1 collective-permute-start
  3.3 0.0 copy-done.1
  3.3 0.0 copy-done.3
  3.3 0.0 copy-done.2
  3.3 2.4 %shard_map.86 = (f32[8,16,2048]{2,1,0:T(8,128)S(1)}, f32[3,16,16,128]{3,2,1,0:T(8,128)S(1)}) custom-call(f32[1,128]{1,0:T(1,128)} %bitcast.7, f32[1,128]{1,0:T(1,128)} %bitcast.9, bf16[8,256,2048]{2,1,0:T(8,128)(2,1)} %refs_2_.3, f32[16,2048]{1,0:T(8,128)S(1)} %copy-done.1, f32[16,2048]{1,0:T(8,128)S(1)} %copy-done.2, f32[16,2048]{1,0:T(8,128)S(1)} %copy-done.3), custom_call_target="tpu_custom_call" | custom-call | flops 4194304 | bytes 4194304 | tf_op jit(solution)/shard_map/pallas_call | solution.py:155
  5.8 0.0 collective-permute-done
  5.8 0.1 add_convert_fusion.2
  5.9 2.8 %collective-permute-start.4 = (f16[1,16,2048]{2,1,0:T(8,128)(2,1)S(1)}, f16[1,16,2048]{2,1,0:T(8,128)(2,1)S(1)}, u32[]{:S(2)}, u32[]{:S(2)}) collective-permute-start(f16[1,16,2048]{2,1,0:T(8,128)(2,1)S(1)} %get-tuple-element.29), channel_id=1, source_target_pairs={{0,2},{1,5},{2,0},{3,7},{4,6},{5,1},{6,4},{7,3},{8,10},{9,13},{10,... | collective-permute-start | bytes 196616 | tf_op jit(solution)/shard_map/ppermute | solution.py:378
  8.8 1.2 %collective-permute-start.6 = (f16[1,16,2048]{2,1,0:T(8,128)(2,1)S(1)}, f16[1,16,2048]{2,1,0:T(8,128)(2,1)S(1)}, u32[]{:S(2)}, u32[]{:S(2)}) collective-permute-start(f16[1,16,2048]{2,1,0:T(8,128)(2,1)S(1)} %get-tuple-element.33), channel_id=1, source_target_pairs={{0,6},{1,7},{2,4},{3,5},{4,2},{5,3},{6,0},{7,1},{8,14},{9,15},{10,... | collective-permute-start | bytes 196616 | tf_op jit(solution)/shard_map/ppermute | solution.py:378
  10.0 0.2 collective-permute-start.5
  10.2 1.5 %collective-permute-start.1 = (f16[1,16,2048]{2,1,0:T(8,128)(2,1)S(1)}, f16[1,16,2048]{2,1,0:T(8,128)(2,1)S(1)}, u32[]{:S(2)}, u32[]{:S(2)}) collective-permute-start(f16[1,16,2048]{2,1,0:T(8,128)(2,1)S(1)} %get-tuple-element.28), channel_id=1, source_target_pairs={{0,2},{1,5},{2,0},{3,7},{4,6},{5,1},{6,4},{7,3},{8,10},{9,13},{10,... | collective-permute-start | bytes 196616 | tf_op jit(solution)/shard_map/ppermute | solution.py:378
  11.7 1.1 %collective-permute-start.3 = (f16[1,16,2048]{2,1,0:T(8,128)(2,1)S(1)}, f16[1,16,2048]{2,1,0:T(8,128)(2,1)S(1)}, u32[]{:S(2)}, u32[]{:S(2)}) collective-permute-start(f16[1,16,2048]{2,1,0:T(8,128)(2,1)S(1)} %get-tuple-element.32), channel_id=1, source_target_pairs={{0,6},{1,7},{2,4},{3,5},{4,2},{5,3},{6,0},{7,1},{8,14},{9,15},{10,... | collective-permute-start | bytes 196616 | tf_op jit(solution)/shard_map/ppermute | solution.py:378
  12.8 0.0 collective-permute-done.4
  12.8 0.1 collective-permute-start.2
  12.9 0.0 collective-permute-done.6
  12.9 2.1 %collective-permute-done.5 = f16[1,16,2048]{2,1,0:T(8,128)(2,1)S(1)} collective-permute-done((f16[1,16,2048]{2,1,0:T(8,128)(2,1)S(1)}, f16[1,16,2048]{2,1,0:T(8,128)(2,1)S(1)}, u32[]{:S(2)}, u32[]{:S(2)}) %collective-permute-start.5) | collective-permute-done | bytes 65568 | tf_op jit(solution)/shard_map/ppermute | solution.py:378
  15.1 1.9 %collective-permute-start.7 = (f16[1,16,2048]{2,1,0:T(8,128)(2,1)S(1)}, f16[1,16,2048]{2,1,0:T(8,128)(2,1)S(1)}, u32[]{:S(2)}, u32[]{:S(2)}) collective-permute-start(f16[1,16,2048]{2,1,0:T(8,128)(2,1)S(1)} %convert_element_type.66), channel_id=1, source_target_pairs={{0,8},{1,9},{2,10},{3,11},{4,12},{5,13},{6,14},{7,15},{8,0},{9,1},... | collective-permute-start | bytes 196616 | tf_op jit(solution)/shard_map/ppermute | solution.py:355
  17.0 4.0 %collective-permute-start.11 = (f16[3,16,16,128]{3,2,1,0:T(8,128)(2,1)S(1)}, f16[3,16,16,128]{3,2,1,0:T(8,128)(2,1)S(1)}, u32[]{:S(2)}, u32[]{:S(2)}) collective-permute-start(f16[3,16,16,128]{3,2,1,0:T(8,128)(2,1)S(1)} %convert_element_type.65), channel_id=1, source_target_pairs={{1,2},{3,4},{5,6},{7,8},{9,10},{11,12},{13,14},{2,1},{4,3},{6,5},{... | collective-permute-start | bytes 589832 | tf_op jit(solution)/shard_map/ppermute | solution.py:359
  21.0 0.0 collective-permute-done.1
  21.0 0.1 collective-permute-start.10
  21.1 0.0 collective-permute-done.3
  21.1 0.0 collective-permute-done.2
  21.1 0.2 collective-permute-done.7
  21.3 0.0 copy-done.4
  21.4 0.0 copy-start
  21.4 0.3 %shard_map.88 = (f32[16,16,128]{2,1,0:T(8,128)S(1)}, bf16[16,16,128]{2,1,0:T(8,128)(2,1)S(1)}) custom-call(f32[16,2048]{1,0:T(8,128)S(1)} %fusion.6.friction), custom_call_target="tpu_custom_call" | custom-call | tf_op jit(solution)/shard_map/pallas_call | solution.py:69
  21.7 2.8 %collective-permute-start.9 = (bf16[16,16,128]{2,1,0:T(8,128)(2,1)S(1)}, bf16[16,16,128]{2,1,0:T(8,128)(2,1)S(1)}, u32[]{:S(2)}, u32[]{:S(2)}) collective-permute-start(bf16[16,16,128]{2,1,0:T(8,128)(2,1)S(1)} %get-tuple-element.17), channel_id=1, source_target_pairs={{1,2},{3,4},{5,6},{7,8},{9,10},{11,12},{13,14},{2,1},{4,3},{6,5},{... | collective-permute-start | bytes 196616 | tf_op jit(solution)/shard_map/ppermute | solution.py:359
  24.5 0.1 collective-permute-start.8
  24.6 0.7 %collective-permute-done.11 = f16[3,16,16,128]{3,2,1,0:T(8,128)(2,1)S(1)} collective-permute-done((f16[3,16,16,128]{3,2,1,0:T(8,128)(2,1)S(1)}, f16[3,16,16,128]{3,2,1,0:T(8,128)(2,1)S(1)}, u32[]{:S(2)}, u32[]{:S(2)}) %collective-permute-start.11) | collective-permute-done | bytes 196640 | tf_op jit(solution)/shard_map/ppermute | solution.py:359
  25.3 0.0 collective-permute-done.10
  25.4 0.5 %shard_map.89 = (f32[20,64,128]{2,1,0:T(8,128)S(1)}, f32[20,64,128]{2,1,0:T(8,128)S(1)}, f32[20,64,128]{2,1,0:T(8,128)S(1)}, f32[20,64,128]{2,1,0:T(8,128)S(1)},...) custom-call(f32[3,16,16,128]{3,2,1,0:T(8,128)S(1)} %get-tuple-element.14.refs_0_, ...), custom_call_target="tpu_custom_call" | custom-call | flops 1 | bytes 1 | tf_op jit(solution)/shard_map/pallas_call | solution.py:250
  25.9 1.4 %collective-permute-done.9.far_f = bf16[16,16,128]{2,1,0:T(8,128)(2,1)S(1)} collective-permute-done((bf16[16,16,128]{2,1,0:T(8,128)(2,1)S(1)}, bf16[16,16,128]{2,1,0:T(8,128)(2,1)S(1)}, u32[]{:S(2)}, u32[]{:S(2)}) %collective-permute-start.9) | collective-permute-done | bytes 65568 | tf_op jit(solution)/shard_map/ppermute | solution.py:359
  27.3 0.0 collective-permute-done.8.near_f
  27.3 3.6 %shard_map.90 = f32[16,2048]{1,0:T(8,128)} custom-call(f32[16,16,128]{2,1,0:T(8,128)S(1)} %get-tuple-element.16.own_f, bf16[16,16,128]{2,1,0:T(8,128)(2,1)S(1)} %collective-permute-done.8.near_f, bf16[16,16,128]{2,1,0:T(8,128)(2,1)S(1)} %collective-permute-done.9.far_f, f32[20,64,128]{2,1,0:T(8,128)S(1)} %get-tuple-element.18.h_in, ...), custom_call_target="tpu_custom_call" | custom-call | tf_op jit(solution)/shard_map/pallas_call | solution.py:339
  31.0 0.0 copy-done
  (9 shorter events, 0.2 us)
Async XLA Ops:
  0.6 2.7 %copy-start.1 = (f32[16,2048]{1,0:T(8,128)S(1)}, f32[16,2048]{1,0:T(8,128)}, u32[]{:S(2)}) copy-start(f32[16,2048]{1,0:T(8,128)} %refs_3_.1) | copy-start | bytes 393220
  0.6 2.7 %copy-start.3 = (f32[16,2048]{1,0:T(8,128)S(1)}, f32[16,2048]{1,0:T(8,128)}, u32[]{:S(2)}) copy-start(f32[16,2048]{1,0:T(8,128)} %refs_5_.1) | copy-start | bytes 393220
  0.7 2.7 %copy-start.2 = (f32[16,2048]{1,0:T(8,128)S(1)}, f32[16,2048]{1,0:T(8,128)}, u32[]{:S(2)}) copy-start(f32[16,2048]{1,0:T(8,128)} %refs_4_.1) | copy-start | bytes 393220
  3.2 18.1 %copy-start.4 = (f32[16,2048]{1,0:T(8,128)S(1)}, f32[16,2048]{1,0:T(8,128)}, u32[]{:S(2)}) copy-start(f32[16,2048]{1,0:T(8,128)} %param.10) | copy-start | bytes 393220
  3.2 2.5 %collective-permute-start = (bf16[8,16,2048]{2,1,0:T(8,128)(2,1)S(1)}, bf16[8,16,2048]{2,1,0:T(8,128)(2,1)S(1)}, u32[]{:S(2)}, u32[]{:S(2)}) collective-permute-start(bf16[8,16,2048]{2,1,0:T(8,128)(2,1)S(1)} %shard_map.87), channel_id=1, source_target_pairs={{0,1},{1,0},{2,3},{3,2},{4,5},{5,4},{6,7},{7,6},{8,9},{9,8},{10,11... | collective-permute-start | bytes 1572872 | tf_op jit(solution)/shard_map/ppermute | solution.py:355
  5.9 6.9 %collective-permute-start.4 = (f16[1,16,2048]{2,1,0:T(8,128)(2,1)S(1)}, f16[1,16,2048]{2,1,0:T(8,128)(2,1)S(1)}, u32[]{:S(2)}, u32[]{:S(2)}) collective-permute-start(f16[1,16,2048]{2,1,0:T(8,128)(2,1)S(1)} %get-tuple-element.29), channel_id=1, source_target_pairs={{0,2},{1,5},{2,0},{3,7},{4,6},{5,1},{6,4},{7,3},{8,10},{9,13},{10,... | collective-permute-start | bytes 196616 | tf_op jit(solution)/shard_map/ppermute | solution.py:378
  8.8 4.2 %collective-permute-start.6 = (f16[1,16,2048]{2,1,0:T(8,128)(2,1)S(1)}, f16[1,16,2048]{2,1,0:T(8,128)(2,1)S(1)}, u32[]{:S(2)}, u32[]{:S(2)}) collective-permute-start(f16[1,16,2048]{2,1,0:T(8,128)(2,1)S(1)} %get-tuple-element.33), channel_id=1, source_target_pairs={{0,6},{1,7},{2,4},{3,5},{4,2},{5,3},{6,0},{7,1},{8,14},{9,15},{10,... | collective-permute-start | bytes 196616 | tf_op jit(solution)/shard_map/ppermute | solution.py:378
  10.0 5.1 %collective-permute-start.5 = (f16[1,16,2048]{2,1,0:T(8,128)(2,1)S(1)}, f16[1,16,2048]{2,1,0:T(8,128)(2,1)S(1)}, u32[]{:S(2)}, u32[]{:S(2)}) collective-permute-start(f16[1,16,2048]{2,1,0:T(8,128)(2,1)S(1)} %get-tuple-element.31), channel_id=1, source_target_pairs={{0,4},{1,3},{2,6},{3,1},{4,0},{5,7},{6,2},{7,5},{8,12},{9,11},{10,... | collective-permute-start | bytes 196616 | tf_op jit(solution)/shard_map/ppermute | solution.py:378
  10.2 10.8 %collective-permute-start.1 = (f16[1,16,2048]{2,1,0:T(8,128)(2,1)S(1)}, f16[1,16,2048]{2,1,0:T(8,128)(2,1)S(1)}, u32[]{:S(2)}, u32[]{:S(2)}) collective-permute-start(f16[1,16,2048]{2,1,0:T(8,128)(2,1)S(1)} %get-tuple-element.28), channel_id=1, source_target_pairs={{0,2},{1,5},{2,0},{3,7},{4,6},{5,1},{6,4},{7,3},{8,10},{9,13},{10,... | collective-permute-start | bytes 196616 | tf_op jit(solution)/shard_map/ppermute | solution.py:378
  11.7 9.5 %collective-permute-start.3 = (f16[1,16,2048]{2,1,0:T(8,128)(2,1)S(1)}, f16[1,16,2048]{2,1,0:T(8,128)(2,1)S(1)}, u32[]{:S(2)}, u32[]{:S(2)}) collective-permute-start(f16[1,16,2048]{2,1,0:T(8,128)(2,1)S(1)} %get-tuple-element.32), channel_id=1, source_target_pairs={{0,6},{1,7},{2,4},{3,5},{4,2},{5,3},{6,0},{7,1},{8,14},{9,15},{10,... | collective-permute-start | bytes 196616 | tf_op jit(solution)/shard_map/ppermute | solution.py:378
  12.8 8.3 %collective-permute-start.2 = (f16[1,16,2048]{2,1,0:T(8,128)(2,1)S(1)}, f16[1,16,2048]{2,1,0:T(8,128)(2,1)S(1)}, u32[]{:S(2)}, u32[]{:S(2)}) collective-permute-start(f16[1,16,2048]{2,1,0:T(8,128)(2,1)S(1)} %get-tuple-element.30), channel_id=1, source_target_pairs={{0,4},{1,3},{2,6},{3,1},{4,0},{5,7},{6,2},{7,5},{8,12},{9,11},{10,... | collective-permute-start | bytes 196616 | tf_op jit(solution)/shard_map/ppermute | solution.py:378
  15.1 6.3 %collective-permute-start.7 = (f16[1,16,2048]{2,1,0:T(8,128)(2,1)S(1)}, f16[1,16,2048]{2,1,0:T(8,128)(2,1)S(1)}, u32[]{:S(2)}, u32[]{:S(2)}) collective-permute-start(f16[1,16,2048]{2,1,0:T(8,128)(2,1)S(1)} %convert_element_type.66), channel_id=1, source_target_pairs={{0,8},{1,9},{2,10},{3,11},{4,12},{5,13},{6,14},{7,15},{8,0},{9,1},... | collective-permute-start | bytes 196616 | tf_op jit(solution)/shard_map/ppermute | solution.py:355
  17.0 8.3 %collective-permute-start.11 = (f16[3,16,16,128]{3,2,1,0:T(8,128)(2,1)S(1)}, f16[3,16,16,128]{3,2,1,0:T(8,128)(2,1)S(1)}, u32[]{:S(2)}, u32[]{:S(2)}) collective-permute-start(f16[3,16,16,128]{3,2,1,0:T(8,128)(2,1)S(1)} %convert_element_type.65), channel_id=1, source_target_pairs={{1,2},{3,4},{5,6},{7,8},{9,10},{11,12},{13,14},{2,1},{4,3},{6,5},{... | collective-permute-start | bytes 589832 | tf_op jit(solution)/shard_map/ppermute | solution.py:359
  21.0 4.3 %collective-permute-start.10 = (f16[3,16,16,128]{3,2,1,0:T(8,128)(2,1)S(1)}, f16[3,16,16,128]{3,2,1,0:T(8,128)(2,1)S(1)}, u32[]{:S(2)}, u32[]{:S(2)}) collective-permute-start(f16[3,16,16,128]{3,2,1,0:T(8,128)(2,1)S(1)} %convert_element_type.65), channel_id=1, source_target_pairs={{0,1},{1,0},{2,3},{3,2},{4,5},{5,4},{6,7},{7,6},{8,9},{9,8},{10,11... | collective-permute-start | bytes 589832 | tf_op jit(solution)/shard_map/ppermute | solution.py:355
  21.4 9.6 %copy-start = (f32[16,2048]{1,0:T(8,128)}, f32[16,2048]{1,0:T(8,128)S(1)}, u32[]{:S(2)}) copy-start(f32[16,2048]{1,0:T(8,128)S(1)} %fusion.6.friction) | copy-start | bytes 393220
  21.7 5.6 %collective-permute-start.9 = (bf16[16,16,128]{2,1,0:T(8,128)(2,1)S(1)}, bf16[16,16,128]{2,1,0:T(8,128)(2,1)S(1)}, u32[]{:S(2)}, u32[]{:S(2)}) collective-permute-start(bf16[16,16,128]{2,1,0:T(8,128)(2,1)S(1)} %get-tuple-element.17), channel_id=1, source_target_pairs={{1,2},{3,4},{5,6},{7,8},{9,10},{11,12},{13,14},{2,1},{4,3},{6,5},{... | collective-permute-start | bytes 196616 | tf_op jit(solution)/shard_map/ppermute | solution.py:359
  24.5 2.8 %collective-permute-start.8 = (bf16[16,16,128]{2,1,0:T(8,128)(2,1)S(1)}, bf16[16,16,128]{2,1,0:T(8,128)(2,1)S(1)}, u32[]{:S(2)}, u32[]{:S(2)}) collective-permute-start(bf16[16,16,128]{2,1,0:T(8,128)(2,1)S(1)} %get-tuple-element.17), channel_id=1, source_target_pairs={{0,1},{1,0},{2,3},{3,2},{4,5},{5,4},{6,7},{7,6},{8,9},{9,8},{10,11... | collective-permute-start | bytes 196616 | tf_op jit(solution)/shard_map/ppermute | solution.py:355

commit v6 on v5

--- a/solution.py
+++ b/solution.py
@@ -92,16 +92,20 @@
 
 
 def weigh(own, coeff_ref, eigen_ref, fields, *refs):
-    out, held, given, sems = refs[-5:-4] + refs[-3:] if own else refs
+    if own:
+        early, *others, out, folded, held, given, sems = refs
+    else:
+        out, early, held, given, sems = refs
     strips, modes, rows, columns = held.shape
     me = lax.axis_index("modes")
     parity = me % 2 if own else 1 - me % 2
 
+    def rows_of(p, parity):
+        row = (((me // 2) ^ pair_at(p, strips, parity)) * 2 + parity) * rows
+        return fields.at[:, pl.ds(pl.multiple_of(row, rows), rows), :]
+
     def copy(p):
-        row = (((me // 2) ^ pair_at(p, strips, parity)) * 2 + parity) * rows
-        return pltpu.make_async_copy(
-            fields.at[:, pl.ds(pl.multiple_of(row, rows), rows), :], held.at[p], sems.at[p]
-        )
+        return pltpu.make_async_copy(rows_of(p, parity), held.at[p], sems.at[p])
 
     small = [
         pltpu.make_async_copy(ref, given.at[i], sems.at[strips + i])
@@ -114,9 +118,12 @@
         copy(p).start()
         return carry
 
-    lax.fori_loop(0, strips, begin, 0)
+    lax.fori_loop(1 if own else 0, strips, begin, 0)
     if own:
-        fold_all(*refs[:-5], refs[-4])
+        fold_all(*others, folded)
+    else:
+        ahead = pltpu.make_async_copy(rows_of(0, me % 2), early, sems.at[strips + 2])
+        ahead.start()
     for one in small:
         one.wait()
     weights = given[0] / jnp.sqrt(1.0 + given[1])
@@ -127,17 +134,24 @@
         for k in range(modes)
     ]
 
+    def sums(p, source):
+        for b in range(columns // LANES):
+            span = slice(b * LANES, (b + 1) * LANES)
+            total = scale[0] * source[0, :, span].astype(jnp.float32)
+            for k in range(1, modes):
+                total = total + scale[k] * source[k, :, span].astype(jnp.float32)
+            out[p, :, span] = total.astype(out.dtype)
+
     def strip(p, carry):
         copy(p).wait()
-        for b in range(columns // LANES):
-            span = slice(b * LANES, (b + 1) * LANES)
-            total = scale[0] * held[p, 0, :, span].astype(jnp.float32)
-            for k in range(1, modes):
-                total = total + scale[k] * held[p, k, :, span].astype(jnp.float32)
-            out[p, :, span] = total.astype(out.dtype)
-        return carry
-
-    lax.fori_loop(0, strips, strip, 0)
+        sums(p, held.at[p])
+        return carry
+
+    if own:
+        sums(0, early)
+    lax.fori_loop(1 if own else 0, strips, strip, 0)
+    if not own:
+        ahead.wait()
 
 
 def shares(coeff, eigen, mode_fields, rows, own, dtype, *statics):
@@ -150,8 +164,10 @@
     vmem = pl.BlockSpec(memory_space=pltpu.VMEM)
     shapes = [jax.ShapeDtypeStruct((strips, rows, columns), dtype)]
     if own:
-        folded = (len(statics), columns // LANES, rows, LANES)
+        folded = (len(statics) - 1, columns // LANES, rows, LANES)
         shapes.append(jax.ShapeDtypeStruct(folded, jnp.float32))
+    else:
+        shapes.append(jax.ShapeDtypeStruct((modes, rows, columns), jnp.bfloat16))
     return pl.pallas_call(
         kernel,
         in_specs=[pl.BlockSpec(memory_space=pltpu.HBM)] * 3 + [vmem] * len(statics),
@@ -160,7 +176,7 @@
         scratch_shapes=[
             pltpu.VMEM((strips, modes, rows, columns), jnp.bfloat16),
             pltpu.VMEM((2,) + coeff.shape, jnp.float32),
-            pltpu.SemaphoreType.DMA((strips + 2,)),
+            pltpu.SemaphoreType.DMA((strips + 3,)),
         ],
         compiler_params=pltpu.CompilerParams(vmem_limit_bytes=LIMIT << 20),
         cost_estimate=pl.CostEstimate(
@@ -361,8 +377,8 @@
     coeff, eigen, mode_fields = (
         pltpu.with_memory_space_constraint(x, pltpu.HBM) for x in (coeff[None], eigen[None], mode_fields)
     )
-    (given,) = shares(coeff, eigen, mode_fields, rows, False, jnp.bfloat16)
-    kept, statics = shares(coeff, eigen, mode_fields, rows, True, jnp.float32, thickness, bed, smb)
+    given, early = shares(coeff, eigen, mode_fields, rows, False, jnp.bfloat16)
+    kept, statics = shares(coeff, eigen, mode_fields, rows, True, jnp.float32, early, thickness, bed, smb)
     arrived = swap(given, 1)
     strips = kept.shape[0]
     inner = direct(strips)

time: 31.1 us -> 31.1 us (level)
  transfers between devices with their start and end apart: 12 -> 12, of which waited for: 4 -> 4; matrix products, arithmetic and copies ran while one was open for 1% -> 1% of each run, Pallas kernels for 11% -> 10%
where the time goes in v6:
time: 31.1 us; the launch traced here: 30.9 us
  starting transfers between devices  15.9 us (51%)
  Pallas kernels  9.33 us (30%)
  waiting for transfers between devices  4.41 us (14%)
  between operations  0.84 us (3%)
    ppermute x6, starting transfers between devices, exchanged(): part = lax.ppermute(summed(k)[many].astype(jnp.float16), 'modes', pairs)  6.91 us
    ppermute x2, starting transfers between devices, across(): return lax.ppermute(value, 'modes', pairs + [(j, i) for i, j in pairs])  6.8 us
    pallas_call x2, Pallas kernels, shares(): pl.pallas_call(kernel, in_specs=[pl.BlockSpec(memory_space=pltpu.HBM)] *...  4.83 us
    pallas_call x1, Pallas kernels, march(): pl.pallas_call(ice, out_shape=jax.ShapeDtypeStruct((rows, blocks * LANES)...  3.64 us
    ppermute x4, starting transfers between devices, swap(): return lax.ppermute(value, 'modes', [(i, i ^ mask) for i in range(peers)])  2.2 us
    ppermute x6, waiting for transfers between devices, exchanged(): part = lax.ppermute(summed(k)[many].astype(jnp.float16), 'modes', pairs)  2.11 us
    ppermute x2, waiting for transfers between devices, across(): return lax.ppermute(value, 'modes', pairs + [(j, i) for i, j in pairs])  2.1 us
  transfers between devices with their start and end apart: 12, of which 4 were waited for; matrix products, arithmetic and copies ran while one was open for 1% of the time, Pallas kernels for 10%

profile of v6, /device:TPU:1, one launch (start us, length us, event | category | flops | bytes accessed | tf_op | source)
XLA Modules:
  0.0 30.9 jit_solution(1686685897248776663)
XLA Ops:
  0.6 0.0 copy-start.1
  0.6 0.0 copy-start.3
  0.7 0.0 copy-start.2
  0.7 2.6 %shard_map.86 = (bf16[8,16,2048]{2,1,0:T(8,128)(2,1)S(1)}, bf16[8,16,2048]{2,1,0:T(8,128)(2,1)S(1)}) custom-call(f32[1,128]{1,0:T(1,128)} %bitcast.6, f32[1,128]{1,0:T(1,128)} %bitcast.8, bf16[8,256,2048]{2,1,0:T(8,128)(2,1)} %refs_2_.3), custom_call_target="tpu_custom_call" | custom-call | flops 4194304 | bytes 4194304 | tf_op jit(solution)/shard_map/pallas_call | solution.py:171
  3.3 0.0 copy-start.4
  3.3 0.1 collective-permute-start
  3.4 0.0 copy-done.1
  3.4 0.0 copy-done.3
  3.4 0.0 copy-done.2
  3.4 2.2 %shard_map.87 = (f32[8,16,2048]{2,1,0:T(8,128)S(1)}, f32[3,16,16,128]{3,2,1,0:T(8,128)S(1)}) custom-call(f32[1,128]{1,0:T(1,128)} %bitcast.7, f32[1,128]{1,0:T(1,128)} %bitcast.9, bf16[8,256,2048]{2,1,0:T(8,128)(2,1)} %refs_2_.3, bf16[8,16,2048]{2,1,0:T(8,128)(2,1)S(1)} %get-tuple-element.15.refs_3_, f32[16,2048]{1,0:T(8,128)S(1)} %copy-done.1, ...), custom_call_target="tpu_custom_call" | custom-call | flops 4194304 | bytes 4194304 | tf_op jit(solution)/shard_map/pallas_call | solution.py:171
  5.7 0.0 collective-permute-done
  5.7 0.1 add_convert_fusion.2
  5.8 2.8 %collective-permute-start.4 = (f16[1,16,2048]{2,1,0:T(8,128)(2,1)S(1)}, f16[1,16,2048]{2,1,0:T(8,128)(2,1)S(1)}, u32[]{:S(2)}, u32[]{:S(2)}) collective-permute-start(f16[1,16,2048]{2,1,0:T(8,128)(2,1)S(1)} %get-tuple-element.33), channel_id=1, source_target_pairs={{0,2},{1,5},{2,0},{3,7},{4,6},{5,1},{6,4},{7,3},{8,10},{9,13},{10,... | collective-permute-start | bytes 196616 | tf_op jit(solution)/shard_map/ppermute | solution.py:394
  8.7 1.2 %collective-permute-start.6 = (f16[1,16,2048]{2,1,0:T(8,128)(2,1)S(1)}, f16[1,16,2048]{2,1,0:T(8,128)(2,1)S(1)}, u32[]{:S(2)}, u32[]{:S(2)}) collective-permute-start(f16[1,16,2048]{2,1,0:T(8,128)(2,1)S(1)} %get-tuple-element.37), channel_id=1, source_target_pairs={{0,6},{1,7},{2,4},{3,5},{4,2},{5,3},{6,0},{7,1},{8,14},{9,15},{10,... | collective-permute-start | bytes 196616 | tf_op jit(solution)/shard_map/ppermute | solution.py:394
  9.9 0.2 collective-permute-start.5
  10.1 1.5 %collective-permute-start.1 = (f16[1,16,2048]{2,1,0:T(8,128)(2,1)S(1)}, f16[1,16,2048]{2,1,0:T(8,128)(2,1)S(1)}, u32[]{:S(2)}, u32[]{:S(2)}) collective-permute-start(f16[1,16,2048]{2,1,0:T(8,128)(2,1)S(1)} %get-tuple-element.32), channel_id=1, source_target_pairs={{0,2},{1,5},{2,0},{3,7},{4,6},{5,1},{6,4},{7,3},{8,10},{9,13},{10,... | collective-permute-start | bytes 196616 | tf_op jit(solution)/shard_map/ppermute | solution.py:394
  11.6 1.1 %collective-permute-start.3 = (f16[1,16,2048]{2,1,0:T(8,128)(2,1)S(1)}, f16[1,16,2048]{2,1,0:T(8,128)(2,1)S(1)}, u32[]{:S(2)}, u32[]{:S(2)}) collective-permute-start(f16[1,16,2048]{2,1,0:T(8,128)(2,1)S(1)} %get-tuple-element.36), channel_id=1, source_target_pairs={{0,6},{1,7},{2,4},{3,5},{4,2},{5,3},{6,0},{7,1},{8,14},{9,15},{10,... | collective-permute-start | bytes 196616 | tf_op jit(solution)/shard_map/ppermute | solution.py:394
  12.7 0.0 collective-permute-done.4
  12.7 0.1 collective-permute-start.2
  12.8 0.0 collective-permute-done.6
  12.8 2.1 %collective-permute-done.5 = f16[1,16,2048]{2,1,0:T(8,128)(2,1)S(1)} collective-permute-done((f16[1,16,2048]{2,1,0:T(8,128)(2,1)S(1)}, f16[1,16,2048]{2,1,0:T(8,128)(2,1)S(1)}, u32[]{:S(2)}, u32[]{:S(2)}) %collective-permute-start.5) | collective-permute-done | bytes 65568 | tf_op jit(solution)/shard_map/ppermute | solution.py:394
  15.0 1.9 %collective-permute-start.7 = (f16[1,16,2048]{2,1,0:T(8,128)(2,1)S(1)}, f16[1,16,2048]{2,1,0:T(8,128)(2,1)S(1)}, u32[]{:S(2)}, u32[]{:S(2)}) collective-permute-start(f16[1,16,2048]{2,1,0:T(8,128)(2,1)S(1)} %convert_element_type.66), channel_id=1, source_target_pairs={{0,8},{1,9},{2,10},{3,11},{4,12},{5,13},{6,14},{7,15},{8,0},{9,1},... | collective-permute-start | bytes 196616 | tf_op jit(solution)/shard_map/ppermute | solution.py:371
  16.9 4.0 %collective-permute-start.11 = (f16[3,16,16,128]{3,2,1,0:T(8,128)(2,1)S(1)}, f16[3,16,16,128]{3,2,1,0:T(8,128)(2,1)S(1)}, u32[]{:S(2)}, u32[]{:S(2)}) collective-permute-start(f16[3,16,16,128]{3,2,1,0:T(8,128)(2,1)S(1)} %convert_element_type.65), channel_id=1, source_target_pairs={{1,2},{3,4},{5,6},{7,8},{9,10},{11,12},{13,14},{2,1},{4,3},{6,5},{... | collective-permute-start | bytes 589832 | tf_op jit(solution)/shard_map/ppermute | solution.py:375
  20.9 0.0 collective-permute-done.1
  20.9 0.1 collective-permute-start.10
  21.0 0.0 collective-permute-done.3
  21.0 0.0 collective-permute-done.2
  21.0 0.2 collective-permute-done.7
  21.2 0.0 copy-done.4
  21.3 0.0 copy-start
  21.3 0.3 %shard_map.88 = (f32[16,16,128]{2,1,0:T(8,128)S(1)}, bf16[16,16,128]{2,1,0:T(8,128)(2,1)S(1)}) custom-call(f32[16,2048]{1,0:T(8,128)S(1)} %fusion.6.friction), custom_call_target="tpu_custom_call" | custom-call | tf_op jit(solution)/shard_map/pallas_call | solution.py:69
  21.6 2.8 %collective-permute-start.9 = (bf16[16,16,128]{2,1,0:T(8,128)(2,1)S(1)}, bf16[16,16,128]{2,1,0:T(8,128)(2,1)S(1)}, u32[]{:S(2)}, u32[]{:S(2)}) collective-permute-start(bf16[16,16,128]{2,1,0:T(8,128)(2,1)S(1)} %get-tuple-element.21), channel_id=1, source_target_pairs={{1,2},{3,4},{5,6},{7,8},{9,10},{11,12},{13,14},{2,1},{4,3},{6,5},{... | collective-permute-start | bytes 196616 | tf_op jit(solution)/shard_map/ppermute | solution.py:375
  24.4 0.1 collective-permute-start.8
  24.5 0.7 %collective-permute-done.11 = f16[3,16,16,128]{3,2,1,0:T(8,128)(2,1)S(1)} collective-permute-done((f16[3,16,16,128]{3,2,1,0:T(8,128)(2,1)S(1)}, f16[3,16,16,128]{3,2,1,0:T(8,128)(2,1)S(1)}, u32[]{:S(2)}, u32[]{:S(2)}) %collective-permute-start.11) | collective-permute-done | bytes 196640 | tf_op jit(solution)/shard_map/ppermute | solution.py:375
  25.2 0.0 collective-permute-done.10
  25.3 0.5 %shard_map.89 = (f32[20,64,128]{2,1,0:T(8,128)S(1)}, f32[20,64,128]{2,1,0:T(8,128)S(1)}, f32[20,64,128]{2,1,0:T(8,128)S(1)}, f32[20,64,128]{2,1,0:T(8,128)S(1)},...) custom-call(f32[3,16,16,128]{3,2,1,0:T(8,128)S(1)} %get-tuple-element.18.refs_0_, ...), custom_call_target="tpu_custom_call" | custom-call | flops 1 | bytes 1 | tf_op jit(solution)/shard_map/pallas_call | solution.py:266
  25.8 1.4 %collective-permute-done.9.far_f = bf16[16,16,128]{2,1,0:T(8,128)(2,1)S(1)} collective-permute-done((bf16[16,16,128]{2,1,0:T(8,128)(2,1)S(1)}, bf16[16,16,128]{2,1,0:T(8,128)(2,1)S(1)}, u32[]{:S(2)}, u32[]{:S(2)}) %collective-permute-start.9) | collective-permute-done | bytes 65568 | tf_op jit(solution)/shard_map/ppermute | solution.py:375
  27.2 0.0 collective-permute-done.8.near_f
  27.2 3.6 %shard_map.90 = f32[16,2048]{1,0:T(8,128)} custom-call(f32[16,16,128]{2,1,0:T(8,128)S(1)} %get-tuple-element.20.own_f, bf16[16,16,128]{2,1,0:T(8,128)(2,1)S(1)} %collective-permute-done.8.near_f, bf16[16,16,128]{2,1,0:T(8,128)(2,1)S(1)} %collective-permute-done.9.far_f, f32[20,64,128]{2,1,0:T(8,128)S(1)} %get-tuple-element.22.h_in, ...), custom_call_target="tpu_custom_call" | custom-call | tf_op jit(solution)/shard_map/pallas_call | solution.py:355
  30.9 0.0 copy-done
  (9 shorter events, 0.2 us)
Async XLA Ops:
  0.6 2.8 %copy-start.1 = (f32[16,2048]{1,0:T(8,128)S(1)}, f32[16,2048]{1,0:T(8,128)}, u32[]{:S(2)}) copy-start(f32[16,2048]{1,0:T(8,128)} %refs_4_.1) | copy-start | bytes 393220
  0.6 2.8 %copy-start.3 = (f32[16,2048]{1,0:T(8,128)S(1)}, f32[16,2048]{1,0:T(8,128)}, u32[]{:S(2)}) copy-start(f32[16,2048]{1,0:T(8,128)} %refs_6_.1) | copy-start | bytes 393220
  0.7 2.7 %copy-start.2 = (f32[16,2048]{1,0:T(8,128)S(1)}, f32[16,2048]{1,0:T(8,128)}, u32[]{:S(2)}) copy-start(f32[16,2048]{1,0:T(8,128)} %refs_5_.1) | copy-start | bytes 393220
  3.3 18.0 %copy-start.4 = (f32[16,2048]{1,0:T(8,128)S(1)}, f32[16,2048]{1,0:T(8,128)}, u32[]{:S(2)}) copy-start(f32[16,2048]{1,0:T(8,128)} %param.10) | copy-start | bytes 393220
  3.3 2.4 %collective-permute-start = (bf16[8,16,2048]{2,1,0:T(8,128)(2,1)S(1)}, bf16[8,16,2048]{2,1,0:T(8,128)(2,1)S(1)}, u32[]{:S(2)}, u32[]{:S(2)}) collective-permute-start(bf16[8,16,2048]{2,1,0:T(8,128)(2,1)S(1)} %get-tuple-element.17), channel_id=1, source_target_pairs={{0,1},{1,0},{2,3},{3,2},{4,5},{5,4},{6,7},{7,6},{8,9},{9,8},{10,11... | collective-permute-start | bytes 1572872 | tf_op jit(solution)/shard_map/ppermute | solution.py:371
  5.8 6.9 %collective-permute-start.4 = (f16[1,16,2048]{2,1,0:T(8,128)(2,1)S(1)}, f16[1,16,2048]{2,1,0:T(8,128)(2,1)S(1)}, u32[]{:S(2)}, u32[]{:S(2)}) collective-permute-start(f16[1,16,2048]{2,1,0:T(8,128)(2,1)S(1)} %get-tuple-element.33), channel_id=1, source_target_pairs={{0,2},{1,5},{2,0},{3,7},{4,6},{5,1},{6,4},{7,3},{8,10},{9,13},{10,... | collective-permute-start | bytes 196616 | tf_op jit(solution)/shard_map/ppermute | solution.py:394
  8.7 4.2 %collective-permute-start.6 = (f16[1,16,2048]{2,1,0:T(8,128)(2,1)S(1)}, f16[1,16,2048]{2,1,0:T(8,128)(2,1)S(1)}, u32[]{:S(2)}, u32[]{:S(2)}) collective-permute-start(f16[1,16,2048]{2,1,0:T(8,128)(2,1)S(1)} %get-tuple-element.37), channel_id=1, source_target_pairs={{0,6},{1,7},{2,4},{3,5},{4,2},{5,3},{6,0},{7,1},{8,14},{9,15},{10,... | collective-permute-start | bytes 196616 | tf_op jit(solution)/shard_map/ppermute | solution.py:394
  9.9 5.1 %collective-permute-start.5 = (f16[1,16,2048]{2,1,0:T(8,128)(2,1)S(1)}, f16[1,16,2048]{2,1,0:T(8,128)(2,1)S(1)}, u32[]{:S(2)}, u32[]{:S(2)}) collective-permute-start(f16[1,16,2048]{2,1,0:T(8,128)(2,1)S(1)} %get-tuple-element.35), channel_id=1, source_target_pairs={{0,4},{1,3},{2,6},{3,1},{4,0},{5,7},{6,2},{7,5},{8,12},{9,11},{10,... | collective-permute-start | bytes 196616 | tf_op jit(solution)/shard_map/ppermute | solution.py:394
  10.1 10.8 %collective-permute-start.1 = (f16[1,16,2048]{2,1,0:T(8,128)(2,1)S(1)}, f16[1,16,2048]{2,1,0:T(8,128)(2,1)S(1)}, u32[]{:S(2)}, u32[]{:S(2)}) collective-permute-start(f16[1,16,2048]{2,1,0:T(8,128)(2,1)S(1)} %get-tuple-element.32), channel_id=1, source_target_pairs={{0,2},{1,5},{2,0},{3,7},{4,6},{5,1},{6,4},{7,3},{8,10},{9,13},{10,... | collective-permute-start | bytes 196616 | tf_op jit(solution)/shard_map/ppermute | solution.py:394
  11.6 9.5 %collective-permute-start.3 = (f16[1,16,2048]{2,1,0:T(8,128)(2,1)S(1)}, f16[1,16,2048]{2,1,0:T(8,128)(2,1)S(1)}, u32[]{:S(2)}, u32[]{:S(2)}) collective-permute-start(f16[1,16,2048]{2,1,0:T(8,128)(2,1)S(1)} %get-tuple-element.36), channel_id=1, source_target_pairs={{0,6},{1,7},{2,4},{3,5},{4,2},{5,3},{6,0},{7,1},{8,14},{9,15},{10,... | collective-permute-start | bytes 196616 | tf_op jit(solution)/shard_map/ppermute | solution.py:394
  12.7 8.3 %collective-permute-start.2 = (f16[1,16,2048]{2,1,0:T(8,128)(2,1)S(1)}, f16[1,16,2048]{2,1,0:T(8,128)(2,1)S(1)}, u32[]{:S(2)}, u32[]{:S(2)}) collective-permute-start(f16[1,16,2048]{2,1,0:T(8,128)(2,1)S(1)} %get-tuple-element.34), channel_id=1, source_target_pairs={{0,4},{1,3},{2,6},{3,1},{4,0},{5,7},{6,2},{7,5},{8,12},{9,11},{10,... | collective-permute-start | bytes 196616 | tf_op jit(solution)/shard_map/ppermute | solution.py:394
  15.0 6.3 %collective-permute-start.7 = (f16[1,16,2048]{2,1,0:T(8,128)(2,1)S(1)}, f16[1,16,2048]{2,1,0:T(8,128)(2,1)S(1)}, u32[]{:S(2)}, u32[]{:S(2)}) collective-permute-start(f16[1,16,2048]{2,1,0:T(8,128)(2,1)S(1)} %convert_element_type.66), channel_id=1, source_target_pairs={{0,8},{1,9},{2,10},{3,11},{4,12},{5,13},{6,14},{7,15},{8,0},{9,1},... | collective-permute-start | bytes 196616 | tf_op jit(solution)/shard_map/ppermute | solution.py:371
  16.9 8.3 %collective-permute-start.11 = (f16[3,16,16,128]{3,2,1,0:T(8,128)(2,1)S(1)}, f16[3,16,16,128]{3,2,1,0:T(8,128)(2,1)S(1)}, u32[]{:S(2)}, u32[]{:S(2)}) collective-permute-start(f16[3,16,16,128]{3,2,1,0:T(8,128)(2,1)S(1)} %convert_element_type.65), channel_id=1, source_target_pairs={{1,2},{3,4},{5,6},{7,8},{9,10},{11,12},{13,14},{2,1},{4,3},{6,5},{... | collective-permute-start | bytes 589832 | tf_op jit(solution)/shard_map/ppermute | solution.py:375
  20.9 4.3 %collective-permute-start.10 = (f16[3,16,16,128]{3,2,1,0:T(8,128)(2,1)S(1)}, f16[3,16,16,128]{3,2,1,0:T(8,128)(2,1)S(1)}, u32[]{:S(2)}, u32[]{:S(2)}) collective-permute-start(f16[3,16,16,128]{3,2,1,0:T(8,128)(2,1)S(1)} %convert_element_type.65), channel_id=1, source_target_pairs={{0,1},{1,0},{2,3},{3,2},{4,5},{5,4},{6,7},{7,6},{8,9},{9,8},{10,11... | collective-permute-start | bytes 589832 | tf_op jit(solution)/shard_map/ppermute | solution.py:371
  21.3 9.6 %copy-start = (f32[16,2048]{1,0:T(8,128)}, f32[16,2048]{1,0:T(8,128)S(1)}, u32[]{:S(2)}) copy-start(f32[16,2048]{1,0:T(8,128)S(1)} %fusion.6.friction) | copy-start | bytes 393220
  21.6 5.6 %collective-permute-start.9 = (bf16[16,16,128]{2,1,0:T(8,128)(2,1)S(1)}, bf16[16,16,128]{2,1,0:T(8,128)(2,1)S(1)}, u32[]{:S(2)}, u32[]{:S(2)}) collective-permute-start(bf16[16,16,128]{2,1,0:T(8,128)(2,1)S(1)} %get-tuple-element.21), channel_id=1, source_target_pairs={{1,2},{3,4},{5,6},{7,8},{9,10},{11,12},{13,14},{2,1},{4,3},{6,5},{... | collective-permute-start | bytes 196616 | tf_op jit(solution)/shard_map/ppermute | solution.py:375
  24.4 2.8 %collective-permute-start.8 = (bf16[16,16,128]{2,1,0:T(8,128)(2,1)S(1)}, bf16[16,16,128]{2,1,0:T(8,128)(2,1)S(1)}, u32[]{:S(2)}, u32[]{:S(2)}) collective-permute-start(bf16[16,16,128]{2,1,0:T(8,128)(2,1)S(1)} %get-tuple-element.21), channel_id=1, source_target_pairs={{0,1},{1,0},{2,3},{3,2},{4,5},{5,4},{6,7},{7,6},{8,9},{9,8},{10,11... | collective-permute-start | bytes 196616 | tf_op jit(solution)/shard_map/ppermute | solution.py:371

commit v7 on v6

--- a/solution.py
+++ b/solution.py
@@ -401,7 +401,7 @@
     taken = exchanged(slice(0, max(half, 1)))
 
     sent = statics.astype(jnp.float16)
-    far_s, near_s = across(sent).astype(jnp.float32), swap(sent, 1).astype(jnp.float32)
+    near_s, far_s = swap(sent, 1).astype(jnp.float32), across(sent).astype(jnp.float32)
 
     onward, sent = lax.optimization_barrier((onward, sent))
     while half:

time: 31.1 us -> 31.1 us (level)
  no operation moved by 1% of the time
where the time goes in v7:
time: 31.1 us; the launch traced here: 30.9 us
  starting transfers between devices  15.9 us (51%)
  Pallas kernels  9.33 us (30%)
  waiting for transfers between devices  4.41 us (14%)
  between operations  0.84 us (3%)
    ppermute x6, starting transfers between devices, exchanged(): part = lax.ppermute(summed(k)[many].astype(jnp.float16), 'modes', pairs)  6.91 us
    ppermute x2, starting transfers between devices, across(): return lax.ppermute(value, 'modes', pairs + [(j, i) for i, j in pairs])  6.8 us
    pallas_call x2, Pallas kernels, shares(): pl.pallas_call(kernel, in_specs=[pl.BlockSpec(memory_space=pltpu.HBM)] *...  4.83 us
    pallas_call x1, Pallas kernels, march(): pl.pallas_call(ice, out_shape=jax.ShapeDtypeStruct((rows, blocks * LANES)...  3.64 us
    ppermute x4, starting transfers between devices, swap(): return lax.ppermute(value, 'modes', [(i, i ^ mask) for i in range(peers)])  2.2 us
    ppermute x6, waiting for transfers between devices, exchanged(): part = lax.ppermute(summed(k)[many].astype(jnp.float16), 'modes', pairs)  2.11 us
    ppermute x2, waiting for transfers between devices, across(): return lax.ppermute(value, 'modes', pairs + [(j, i) for i, j in pairs])  2.1 us
  transfers between devices with their start and end apart: 12, of which 4 were waited for; matrix products, arithmetic and copies ran while one was open for 1% of the time, Pallas kernels for 10%

profile of v7, /device:TPU:1, one launch (start us, length us, event | category | flops | bytes accessed | tf_op | source)
XLA Modules:
  0.0 30.9 jit_solution(1686685897248776663)
XLA Ops:
  0.6 0.0 copy-start.1
  0.6 0.0 copy-start.3
  0.7 0.0 copy-start.2
  0.7 2.6 %shard_map.86 = (bf16[8,16,2048]{2,1,0:T(8,128)(2,1)S(1)}, bf16[8,16,2048]{2,1,0:T(8,128)(2,1)S(1)}) custom-call(f32[1,128]{1,0:T(1,128)} %bitcast.6, f32[1,128]{1,0:T(1,128)} %bitcast.8, bf16[8,256,2048]{2,1,0:T(8,128)(2,1)} %refs_2_.3), custom_call_target="tpu_custom_call" | custom-call | flops 4194304 | bytes 4194304 | tf_op jit(solution)/shard_map/pallas_call | solution.py:171
  3.3 0.0 copy-start.4
  3.3 0.1 collective-permute-start
  3.4 0.0 copy-done.1
  3.4 0.0 copy-done.3
  3.4 0.0 copy-done.2
  3.4 2.2 %shard_map.87 = (f32[8,16,2048]{2,1,0:T(8,128)S(1)}, f32[3,16,16,128]{3,2,1,0:T(8,128)S(1)}) custom-call(f32[1,128]{1,0:T(1,128)} %bitcast.7, f32[1,128]{1,0:T(1,128)} %bitcast.9, bf16[8,256,2048]{2,1,0:T(8,128)(2,1)} %refs_2_.3, bf16[8,16,2048]{2,1,0:T(8,128)(2,1)S(1)} %get-tuple-element.15.refs_3_, f32[16,2048]{1,0:T(8,128)S(1)} %copy-done.1, ...), custom_call_target="tpu_custom_call" | custom-call | flops 4194304 | bytes 4194304 | tf_op jit(solution)/shard_map/pallas_call | solution.py:171
  5.7 0.0 collective-permute-done
  5.7 0.1 add_convert_fusion.2
  5.8 2.8 %collective-permute-start.4 = (f16[1,16,2048]{2,1,0:T(8,128)(2,1)S(1)}, f16[1,16,2048]{2,1,0:T(8,128)(2,1)S(1)}, u32[]{:S(2)}, u32[]{:S(2)}) collective-permute-start(f16[1,16,2048]{2,1,0:T(8,128)(2,1)S(1)} %get-tuple-element.33), channel_id=1, source_target_pairs={{0,2},{1,5},{2,0},{3,7},{4,6},{5,1},{6,4},{7,3},{8,10},{9,13},{10,... | collective-permute-start | bytes 196616 | tf_op jit(solution)/shard_map/ppermute | solution.py:394
  8.7 1.2 %collective-permute-start.6 = (f16[1,16,2048]{2,1,0:T(8,128)(2,1)S(1)}, f16[1,16,2048]{2,1,0:T(8,128)(2,1)S(1)}, u32[]{:S(2)}, u32[]{:S(2)}) collective-permute-start(f16[1,16,2048]{2,1,0:T(8,128)(2,1)S(1)} %get-tuple-element.37), channel_id=1, source_target_pairs={{0,6},{1,7},{2,4},{3,5},{4,2},{5,3},{6,0},{7,1},{8,14},{9,15},{10,... | collective-permute-start | bytes 196616 | tf_op jit(solution)/shard_map/ppermute | solution.py:394
  9.9 0.2 collective-permute-start.5
  10.1 1.5 %collective-permute-start.1 = (f16[1,16,2048]{2,1,0:T(8,128)(2,1)S(1)}, f16[1,16,2048]{2,1,0:T(8,128)(2,1)S(1)}, u32[]{:S(2)}, u32[]{:S(2)}) collective-permute-start(f16[1,16,2048]{2,1,0:T(8,128)(2,1)S(1)} %get-tuple-element.32), channel_id=1, source_target_pairs={{0,2},{1,5},{2,0},{3,7},{4,6},{5,1},{6,4},{7,3},{8,10},{9,13},{10,... | collective-permute-start | bytes 196616 | tf_op jit(solution)/shard_map/ppermute | solution.py:394
  11.6 1.1 %collective-permute-start.3 = (f16[1,16,2048]{2,1,0:T(8,128)(2,1)S(1)}, f16[1,16,2048]{2,1,0:T(8,128)(2,1)S(1)}, u32[]{:S(2)}, u32[]{:S(2)}) collective-permute-start(f16[1,16,2048]{2,1,0:T(8,128)(2,1)S(1)} %get-tuple-element.36), channel_id=1, source_target_pairs={{0,6},{1,7},{2,4},{3,5},{4,2},{5,3},{6,0},{7,1},{8,14},{9,15},{10,... | collective-permute-start | bytes 196616 | tf_op jit(solution)/shard_map/ppermute | solution.py:394
  12.7 0.0 collective-permute-done.4
  12.7 0.1 collective-permute-start.2
  12.8 0.0 collective-permute-done.6
  12.8 2.1 %collective-permute-done.5 = f16[1,16,2048]{2,1,0:T(8,128)(2,1)S(1)} collective-permute-done((f16[1,16,2048]{2,1,0:T(8,128)(2,1)S(1)}, f16[1,16,2048]{2,1,0:T(8,128)(2,1)S(1)}, u32[]{:S(2)}, u32[]{:S(2)}) %collective-permute-start.5) | collective-permute-done | bytes 65568 | tf_op jit(solution)/shard_map/ppermute | solution.py:394
  15.0 1.9 %collective-permute-start.7 = (f16[1,16,2048]{2,1,0:T(8,128)(2,1)S(1)}, f16[1,16,2048]{2,1,0:T(8,128)(2,1)S(1)}, u32[]{:S(2)}, u32[]{:S(2)}) collective-permute-start(f16[1,16,2048]{2,1,0:T(8,128)(2,1)S(1)} %convert_element_type.66), channel_id=1, source_target_pairs={{0,8},{1,9},{2,10},{3,11},{4,12},{5,13},{6,14},{7,15},{8,0},{9,1},... | collective-permute-start | bytes 196616 | tf_op jit(solution)/shard_map/ppermute | solution.py:371
  16.9 4.0 %collective-permute-start.11 = (f16[3,16,16,128]{3,2,1,0:T(8,128)(2,1)S(1)}, f16[3,16,16,128]{3,2,1,0:T(8,128)(2,1)S(1)}, u32[]{:S(2)}, u32[]{:S(2)}) collective-permute-start(f16[3,16,16,128]{3,2,1,0:T(8,128)(2,1)S(1)} %convert_element_type.65), channel_id=1, source_target_pairs={{1,2},{3,4},{5,6},{7,8},{9,10},{11,12},{13,14},{2,1},{4,3},{6,5},{... | collective-permute-start | bytes 589832 | tf_op jit(solution)/shard_map/ppermute | solution.py:375
  20.9 0.0 collective-permute-done.1
  20.9 0.1 collective-permute-start.10
  21.0 0.0 collective-permute-done.3
  21.0 0.0 collective-permute-done.2
  21.0 0.2 collective-permute-done.7
  21.2 0.0 copy-done.4
  21.3 0.0 copy-start
  21.3 0.3 %shard_map.88 = (f32[16,16,128]{2,1,0:T(8,128)S(1)}, bf16[16,16,128]{2,1,0:T(8,128)(2,1)S(1)}) custom-call(f32[16,2048]{1,0:T(8,128)S(1)} %fusion.6.friction), custom_call_target="tpu_custom_call" | custom-call | tf_op jit(solution)/shard_map/pallas_call | solution.py:69
  21.6 2.8 %collective-permute-start.9 = (bf16[16,16,128]{2,1,0:T(8,128)(2,1)S(1)}, bf16[16,16,128]{2,1,0:T(8,128)(2,1)S(1)}, u32[]{:S(2)}, u32[]{:S(2)}) collective-permute-start(bf16[16,16,128]{2,1,0:T(8,128)(2,1)S(1)} %get-tuple-element.21), channel_id=1, source_target_pairs={{1,2},{3,4},{5,6},{7,8},{9,10},{11,12},{13,14},{2,1},{4,3},{6,5},{... | collective-permute-start | bytes 196616 | tf_op jit(solution)/shard_map/ppermute | solution.py:375
  24.4 0.1 collective-permute-start.8
  24.5 0.7 %collective-permute-done.11 = f16[3,16,16,128]{3,2,1,0:T(8,128)(2,1)S(1)} collective-permute-done((f16[3,16,16,128]{3,2,1,0:T(8,128)(2,1)S(1)}, f16[3,16,16,128]{3,2,1,0:T(8,128)(2,1)S(1)}, u32[]{:S(2)}, u32[]{:S(2)}) %collective-permute-start.11) | collective-permute-done | bytes 196640 | tf_op jit(solution)/shard_map/ppermute | solution.py:375
  25.2 0.0 collective-permute-done.10
  25.3 0.5 %shard_map.89 = (f32[20,64,128]{2,1,0:T(8,128)S(1)}, f32[20,64,128]{2,1,0:T(8,128)S(1)}, f32[20,64,128]{2,1,0:T(8,128)S(1)}, f32[20,64,128]{2,1,0:T(8,128)S(1)},...) custom-call(f32[3,16,16,128]{3,2,1,0:T(8,128)S(1)} %get-tuple-element.18.refs_0_, ...), custom_call_target="tpu_custom_call" | custom-call | flops 1 | bytes 1 | tf_op jit(solution)/shard_map/pallas_call | solution.py:266
  25.8 1.4 %collective-permute-done.9.far_f = bf16[16,16,128]{2,1,0:T(8,128)(2,1)S(1)} collective-permute-done((bf16[16,16,128]{2,1,0:T(8,128)(2,1)S(1)}, bf16[16,16,128]{2,1,0:T(8,128)(2,1)S(1)}, u32[]{:S(2)}, u32[]{:S(2)}) %collective-permute-start.9) | collective-permute-done | bytes 65568 | tf_op jit(solution)/shard_map/ppermute | solution.py:375
  27.2 0.0 collective-permute-done.8.near_f
  27.2 3.6 %shard_map.90 = f32[16,2048]{1,0:T(8,128)} custom-call(f32[16,16,128]{2,1,0:T(8,128)S(1)} %get-tuple-element.20.own_f, bf16[16,16,128]{2,1,0:T(8,128)(2,1)S(1)} %collective-permute-done.8.near_f, bf16[16,16,128]{2,1,0:T(8,128)(2,1)S(1)} %collective-permute-done.9.far_f, f32[20,64,128]{2,1,0:T(8,128)S(1)} %get-tuple-element.22.h_in, ...), custom_call_target="tpu_custom_call" | custom-call | tf_op jit(solution)/shard_map/pallas_call | solution.py:355
  30.9 0.0 copy-done
  (9 shorter events, 0.2 us)
Async XLA Ops:
  0.6 2.8 %copy-start.1 = (f32[16,2048]{1,0:T(8,128)S(1)}, f32[16,2048]{1,0:T(8,128)}, u32[]{:S(2)}) copy-start(f32[16,2048]{1,0:T(8,128)} %refs_4_.1) | copy-start | bytes 393220
  0.6 2.8 %copy-start.3 = (f32[16,2048]{1,0:T(8,128)S(1)}, f32[16,2048]{1,0:T(8,128)}, u32[]{:S(2)}) copy-start(f32[16,2048]{1,0:T(8,128)} %refs_6_.1) | copy-start | bytes 393220
  0.7 2.7 %copy-start.2 = (f32[16,2048]{1,0:T(8,128)S(1)}, f32[16,2048]{1,0:T(8,128)}, u32[]{:S(2)}) copy-start(f32[16,2048]{1,0:T(8,128)} %refs_5_.1) | copy-start | bytes 393220
  3.3 18.0 %copy-start.4 = (f32[16,2048]{1,0:T(8,128)S(1)}, f32[16,2048]{1,0:T(8,128)}, u32[]{:S(2)}) copy-start(f32[16,2048]{1,0:T(8,128)} %param.10) | copy-start | bytes 393220
  3.3 2.4 %collective-permute-start = (bf16[8,16,2048]{2,1,0:T(8,128)(2,1)S(1)}, bf16[8,16,2048]{2,1,0:T(8,128)(2,1)S(1)}, u32[]{:S(2)}, u32[]{:S(2)}) collective-permute-start(bf16[8,16,2048]{2,1,0:T(8,128)(2,1)S(1)} %get-tuple-element.17), channel_id=1, source_target_pairs={{0,1},{1,0},{2,3},{3,2},{4,5},{5,4},{6,7},{7,6},{8,9},{9,8},{10,11... | collective-permute-start | bytes 1572872 | tf_op jit(solution)/shard_map/ppermute | solution.py:371
  5.8 6.9 %collective-permute-start.4 = (f16[1,16,2048]{2,1,0:T(8,128)(2,1)S(1)}, f16[1,16,2048]{2,1,0:T(8,128)(2,1)S(1)}, u32[]{:S(2)}, u32[]{:S(2)}) collective-permute-start(f16[1,16,2048]{2,1,0:T(8,128)(2,1)S(1)} %get-tuple-element.33), channel_id=1, source_target_pairs={{0,2},{1,5},{2,0},{3,7},{4,6},{5,1},{6,4},{7,3},{8,10},{9,13},{10,... | collective-permute-start | bytes 196616 | tf_op jit(solution)/shard_map/ppermute | solution.py:394
  8.7 4.2 %collective-permute-start.6 = (f16[1,16,2048]{2,1,0:T(8,128)(2,1)S(1)}, f16[1,16,2048]{2,1,0:T(8,128)(2,1)S(1)}, u32[]{:S(2)}, u32[]{:S(2)}) collective-permute-start(f16[1,16,2048]{2,1,0:T(8,128)(2,1)S(1)} %get-tuple-element.37), channel_id=1, source_target_pairs={{0,6},{1,7},{2,4},{3,5},{4,2},{5,3},{6,0},{7,1},{8,14},{9,15},{10,... | collective-permute-start | bytes 196616 | tf_op jit(solution)/shard_map/ppermute | solution.py:394
  9.9 5.1 %collective-permute-start.5 = (f16[1,16,2048]{2,1,0:T(8,128)(2,1)S(1)}, f16[1,16,2048]{2,1,0:T(8,128)(2,1)S(1)}, u32[]{:S(2)}, u32[]{:S(2)}) collective-permute-start(f16[1,16,2048]{2,1,0:T(8,128)(2,1)S(1)} %get-tuple-element.35), channel_id=1, source_target_pairs={{0,4},{1,3},{2,6},{3,1},{4,0},{5,7},{6,2},{7,5},{8,12},{9,11},{10,... | collective-permute-start | bytes 196616 | tf_op jit(solution)/shard_map/ppermute | solution.py:394
  10.1 10.8 %collective-permute-start.1 = (f16[1,16,2048]{2,1,0:T(8,128)(2,1)S(1)}, f16[1,16,2048]{2,1,0:T(8,128)(2,1)S(1)}, u32[]{:S(2)}, u32[]{:S(2)}) collective-permute-start(f16[1,16,2048]{2,1,0:T(8,128)(2,1)S(1)} %get-tuple-element.32), channel_id=1, source_target_pairs={{0,2},{1,5},{2,0},{3,7},{4,6},{5,1},{6,4},{7,3},{8,10},{9,13},{10,... | collective-permute-start | bytes 196616 | tf_op jit(solution)/shard_map/ppermute | solution.py:394
  11.6 9.5 %collective-permute-start.3 = (f16[1,16,2048]{2,1,0:T(8,128)(2,1)S(1)}, f16[1,16,2048]{2,1,0:T(8,128)(2,1)S(1)}, u32[]{:S(2)}, u32[]{:S(2)}) collective-permute-start(f16[1,16,2048]{2,1,0:T(8,128)(2,1)S(1)} %get-tuple-element.36), channel_id=1, source_target_pairs={{0,6},{1,7},{2,4},{3,5},{4,2},{5,3},{6,0},{7,1},{8,14},{9,15},{10,... | collective-permute-start | bytes 196616 | tf_op jit(solution)/shard_map/ppermute | solution.py:394
  12.7 8.3 %collective-permute-start.2 = (f16[1,16,2048]{2,1,0:T(8,128)(2,1)S(1)}, f16[1,16,2048]{2,1,0:T(8,128)(2,1)S(1)}, u32[]{:S(2)}, u32[]{:S(2)}) collective-permute-start(f16[1,16,2048]{2,1,0:T(8,128)(2,1)S(1)} %get-tuple-element.34), channel_id=1, source_target_pairs={{0,4},{1,3},{2,6},{3,1},{4,0},{5,7},{6,2},{7,5},{8,12},{9,11},{10,... | collective-permute-start | bytes 196616 | tf_op jit(solution)/shard_map/ppermute | solution.py:394
  15.0 6.3 %collective-permute-start.7 = (f16[1,16,2048]{2,1,0:T(8,128)(2,1)S(1)}, f16[1,16,2048]{2,1,0:T(8,128)(2,1)S(1)}, u32[]{:S(2)}, u32[]{:S(2)}) collective-permute-start(f16[1,16,2048]{2,1,0:T(8,128)(2,1)S(1)} %convert_element_type.66), channel_id=1, source_target_pairs={{0,8},{1,9},{2,10},{3,11},{4,12},{5,13},{6,14},{7,15},{8,0},{9,1},... | collective-permute-start | bytes 196616 | tf_op jit(solution)/shard_map/ppermute | solution.py:371
  16.9 8.3 %collective-permute-start.11 = (f16[3,16,16,128]{3,2,1,0:T(8,128)(2,1)S(1)}, f16[3,16,16,128]{3,2,1,0:T(8,128)(2,1)S(1)}, u32[]{:S(2)}, u32[]{:S(2)}) collective-permute-start(f16[3,16,16,128]{3,2,1,0:T(8,128)(2,1)S(1)} %convert_element_type.65), channel_id=1, source_target_pairs={{1,2},{3,4},{5,6},{7,8},{9,10},{11,12},{13,14},{2,1},{4,3},{6,5},{... | collective-permute-start | bytes 589832 | tf_op jit(solution)/shard_map/ppermute | solution.py:375
  20.9 4.3 %collective-permute-start.10 = (f16[3,16,16,128]{3,2,1,0:T(8,128)(2,1)S(1)}, f16[3,16,16,128]{3,2,1,0:T(8,128)(2,1)S(1)}, u32[]{:S(2)}, u32[]{:S(2)}) collective-permute-start(f16[3,16,16,128]{3,2,1,0:T(8,128)(2,1)S(1)} %convert_element_type.65), channel_id=1, source_target_pairs={{0,1},{1,0},{2,3},{3,2},{4,5},{5,4},{6,7},{7,6},{8,9},{9,8},{10,11... | collective-permute-start | bytes 589832 | tf_op jit(solution)/shard_map/ppermute | solution.py:371
  21.3 9.6 %copy-start = (f32[16,2048]{1,0:T(8,128)}, f32[16,2048]{1,0:T(8,128)S(1)}, u32[]{:S(2)}) copy-start(f32[16,2048]{1,0:T(8,128)S(1)} %fusion.6.friction) | copy-start | bytes 393220
  21.6 5.6 %collective-permute-start.9 = (bf16[16,16,128]{2,1,0:T(8,128)(2,1)S(1)}, bf16[16,16,128]{2,1,0:T(8,128)(2,1)S(1)}, u32[]{:S(2)}, u32[]{:S(2)}) collective-permute-start(bf16[16,16,128]{2,1,0:T(8,128)(2,1)S(1)} %get-tuple-element.21), channel_id=1, source_target_pairs={{1,2},{3,4},{5,6},{7,8},{9,10},{11,12},{13,14},{2,1},{4,3},{6,5},{... | collective-permute-start | bytes 196616 | tf_op jit(solution)/shard_map/ppermute | solution.py:375
  24.4 2.8 %collective-permute-start.8 = (bf16[16,16,128]{2,1,0:T(8,128)(2,1)S(1)}, bf16[16,16,128]{2,1,0:T(8,128)(2,1)S(1)}, u32[]{:S(2)}, u32[]{:S(2)}) collective-permute-start(bf16[16,16,128]{2,1,0:T(8,128)(2,1)S(1)} %get-tuple-element.21), channel_id=1, source_target_pairs={{0,1},{1,0},{2,3},{3,2},{4,5},{5,4},{6,7},{7,6},{8,9},{9,8},{10,11... | collective-permute-start | bytes 196616 | tf_op jit(solution)/shard_map/ppermute | solution.py:371
